TPU v7x, 512 devices: a whole 4x8x8 slice. The times are simulated.
512 devices in a mesh: stream: 32 (over x, y), azim: 16 (over z, core).
Axes of the slice: x: 4, y: 8, z: 8, core: 2. Of those that a mesh axis runs over, the one named last changes fastest.
Arguments:
- state_in: float32 [21, 1024, 32, 128], P(None, None, 'azim', 'stream'), may hold values from -6 to 6
- new_index: int32 [1024], P('stream'), may hold values from 0 to 1023, as said below
- stencil_index: int32 [1024, 32, 128], P('stream', 'azim'), may hold values from 0 to 126
- stencil_weight: float32 [1024, 32, 128], P('stream', 'azim'), may hold values from 0 to 1
- cell_count: int32 [1024, 32], P('stream', 'azim'), may hold values from 64 to 128
- normal_speed: float32 [1024, 32, 128], P('stream', 'azim'), may hold values from 0.2 to 0.9
- azim_diffusion: float32 [1024, 32, 128], P('stream', 'azim'), may hold values from 0.05 to 0.4
- mixing: float32 [21, 21], replicated, may hold values from -1.25 to 1.25
Outputs:
- state_out: float32 [21, 1024, 32, 128], P(None, 'stream', 'azim')
Inputs may be any that keep to these rules, and one draw needn't show every extreme that they name: A permutation of the stations. The new owner of station s is new_index[s] // 32; one device's stations go to one owner at most 2 at a time, exactly 2 for some owners, and how many depends only on the difference of the two stream indices modulo 32.
All inputs are finite; a program needn't handle non-finite values.
Results may differ from a plain program's by a relative error of at most 0.000071.
Values sent between devices are 32-bit elements; how exact they have to be, the bound alone decides.
No kernel may reach another device: no remote copies, remote signals or barrier semaphores. Data moves between devices by JAX's collectives and lax.ppermute only.
A program may use at most 64 MiB of HBM per device.

v0:
```python
import jax
import jax.numpy as jnp
from jax import lax
from jax.sharding import PartitionSpec as P


def extended(cells, sides, width):
    for axis, dim in sides:
        count = lax.axis_size(axis)
        head = lax.slice_in_dim(cells, 0, width, axis=dim)
        tail = lax.slice_in_dim(cells, cells.shape[dim] - width, cells.shape[dim], axis=dim)
        cells = jnp.concatenate(
            [
                lax.ppermute(tail, axis, [(i, (i + 1) % count) for i in range(count)]),
                cells,
                lax.ppermute(head, axis, [((i + 1) % count, i) for i in range(count)]),
            ],
            axis=dim,
        )
    return cells


def recluster(flow_state, stencil_index, stencil_weight, cell_count):
    cell_total = flow_state.shape[3]
    places = jnp.arange(cell_total, dtype=jnp.int32)[None, None, None, :]
    lower = stencil_index[..., None]
    weight = stencil_weight[..., None]
    table = jnp.where(places == lower, 1.0 - weight, jnp.float32(0.0)) + jnp.where(
        places == lower + 1, weight, jnp.float32(0.0)
    )
    fitted = jnp.einsum("sajk,vsak->vsaj", table, flow_state, precision=lax.Precision.HIGHEST)
    active = active_mask(cell_count, cell_total)
    return jnp.where(active[None] > 0.0, fitted, jnp.float32(0.0))


def active_mask(cell_count, cell_total):
    return (jnp.arange(cell_total, dtype=jnp.int32)[None, None, :] < cell_count[:, :, None]).astype(
        jnp.float32
    )


def flux_rate(widened, line_speed, diffuse, mixing):
    center = widened[:, :, 1:-1]
    below_cell = jnp.concatenate([jnp.zeros_like(center[..., :1]), center[..., :-1]], axis=3)
    lateral = widened[:, :, 2:] + widened[:, :, :-2] - 2.0 * center
    mixed_term = jnp.einsum("uv,vsan->usan", mixing, center, precision=lax.Precision.HIGHEST)
    return diffuse * lateral - line_speed * (center - below_cell) - 0.25 * mixed_term


def routing(new_rows, peer_total):
    row_total = new_rows.shape[0]
    slot_room = 2 * row_total // peer_total
    target = new_rows // row_total
    new_place = new_rows % row_total
    owners = (target[:, None] == jnp.arange(peer_total, dtype=jnp.int32)[None, :]).astype(jnp.int32)
    before = jnp.cumsum(owners, axis=0) - owners
    order_in = jnp.sum(before * owners, axis=1)
    position = target * slot_room + order_in
    packing = jnp.arange(peer_total * slot_room, dtype=jnp.int32)[:, None] == position[None, :]
    slot_list = jnp.max(jnp.where(packing, new_place[None, :], -1), axis=1)
    return (packing.astype(jnp.float32), slot_list)


def unpacking(got_slots, row_total):
    return (jnp.arange(row_total, dtype=jnp.int32)[:, None] == got_slots[None, :]).astype(
        jnp.float32
    )


def shards(
    state_in,
    new_index,
    stencil_index,
    stencil_weight,
    cell_count,
    normal_speed,
    azim_diffusion,
    mixing,
):
    peer_total = lax.axis_size("stream")
    row_total = new_index.shape[0]
    highest = lax.Precision.HIGHEST
    line_state = lax.all_to_all(state_in, "stream", split_axis=1, concat_axis=3, tiled=True)
    cell_total = line_state.shape[3]
    packing, slot_list = routing(new_index, peer_total)
    fitted = recluster(line_state, stencil_index, stencil_weight, cell_count)
    sent_rows = jnp.einsum("pr,vran->pvan", packing, fitted, precision=highest)
    sent_count = jnp.dot(packing, cell_count.astype(jnp.float32), precision=highest)
    got_rows, got_count, got_slots = (
        lax.all_to_all(sent_rows, "stream", split_axis=0, concat_axis=0, tiled=True),
        lax.all_to_all(sent_count, "stream", split_axis=0, concat_axis=0, tiled=True),
        lax.all_to_all(slot_list, "stream", split_axis=0, concat_axis=0, tiled=True),
    )
    placing = unpacking(got_slots, row_total)
    current = jnp.einsum("qp,pvan->vqan", placing, got_rows, precision=highest)
    count_here = jnp.dot(placing, got_count, precision=highest).astype(jnp.int32)
    active = active_mask(count_here, cell_total)

    def widen(field):
        return extended(field, (("azim", 2),), 1)

    section_one = current + active * flux_rate(widen(current), normal_speed, azim_diffusion, mixing)
    return 0.5 * (
        current
        + section_one
        + active * flux_rate(widen(section_one), normal_speed, azim_diffusion, mixing)
    )


def solution(mesh):
    in_specs = (
        P(None, None, "azim", "stream"),
        P("stream"),
        P("stream", "azim", None),
        P("stream", "azim", None),
        P("stream", "azim"),
        P("stream", "azim", None),
        P("stream", "azim", None),
        P(),
    )
    out_specs = P(None, "stream", "azim", None)
    return jax.shard_map(shards, mesh=mesh, in_specs=in_specs, out_specs=out_specs, check_vma=False)
```

profile of v0, /device:TPU:201, one launch (start us, length us, event | category | flops | bytes accessed | tf_op | source)
XLA Modules:
  0.0 161.0 jit_solution(5628012945643935855)
XLA Ops:
  0.0 4.6 %copy.44 = f32[21,1024,2,4]{0,3,2,1:T(4,128)} copy(f32[21,1024,2,4]{1,3,2,0:T(4,128)} %param.8) | data formatting | bytes 1376256 | tf_op args[0]
  4.6 6.7 %reshape.41 = f32[32,1,5376]{2,1,0:T(1,128)} reshape(f32[1024,2,4,21]{3,2,1,0:T(4,128)} %bitcast.43) | data formatting | bytes 1376256
  11.3 9.6 %all-to-all-start = ((f32[32,1,5376]{2,1,0:T(1,128)}), f32[32,1,5376]{2,1,0:T(1,128)S(1)}, u32[]{:S(2)}, u32[]{:S(2)}) async-start(f32[32,1,5376]{2,1,0:T(1,128)} %reshape.41), calls=%async_computation | async-start | bytes 1376256 | tf_op jit(solution)/shard_map/all_to_all | solution.py:83
  25.0 15.0 %all-to-all-done = f32[32,1,5376]{2,1,0:T(1,128)S(1)} async-done(((f32[32,1,5376]{2,1,0:T(1,128)}), f32[32,1,5376]{2,1,0:T(1,128)S(1)}, u32[]{:S(2)}, u32[]{:S(2)}) %all-to-all-start) | async-done | bytes 688160 | tf_op jit(solution)/shard_map/all_to_all | solution.py:83
  40.0 6.4 %all-to-all-start.2 = ((s32[32,2,1]{1,2,0:T(1,128)}), s32[32,2,1]{1,2,0:T(1,128)}, u32[]{:S(2)}, u32[]{:S(2)}) async-start(s32[32,2,1]{1,2,0:T(1,128)} %bitcast.6), calls=%async_computation.2 | async-start | bytes 32768 | tf_op jit(solution)/shard_map/all_to_all | solution.py:92
  47.0 2.3 %reduce.4 = f32[32,5376]{1,0:T(8,128)S(1)} reduce(f32[32,1,5376]{2,1,0:T(1,128)S(1)} %all-to-all-done, f32[]{:T(128)} %broadcast.88), dimensions={1}, to_apply=%all_to_all.30.reduce_sub_computation | reduce | bytes 1376260 | tf_op jit(solution)/shard_map/all_to_all | solution.py:83
  49.3 7.3 %reshape.42 = f32[1024,2,4,21]{3,2,1,0:T(4,128)} reshape(f32[32,5376]{1,0:T(8,128)S(1)} %reduce.4) | data formatting | bytes 1376256
  56.6 5.1 %copy.45 = f32[21,32,32,2,4]{2,4,1,3,0:T(4,128)S(1)} copy(f32[21,32,32,2,4]{0,4,3,2,1:T(4,128)} %bitcast.44) | data formatting | bytes 1376256 | tf_op jit(solution)/shard_map/all_to_all | solution.py:83
  61.6 1.2 copy.46
  62.8 17.3 %fusion.17 = f32[21,32,2,128]{3,0,2,1:T(8,128)S(1)} fusion(f32[21,32,2,128]{3,0,2,1:T(8,128)S(1)} %copy.46, f32[32,2,128]{2,1,0:T(2,128)} %param.11, s32[32,2,128]{2,1,0:T(2,128)} %broadcast_add_fusion, f32[32,2,128]{2,1,0:T(2,128)} %broadcast_subtract_fusion, s32[32,2,128]{2,1,0:T(2,128)} %param.10, pred[32,2,128]{2,1,0:T(4,128)(4,1)} %fusion.41), kind=kOutput, calls=%fused_computation.15 | convolution fusion | flops 269656064 | bytes 1515520 | tf_op jit(solution)/shard_map/sajk,vsak->vsaj/dot_general | solution.py:31
  80.1 9.2 %all-to-all-start.3 = ((f32[32,2,2]{1,2,0:T(2,128)}), f32[32,2,2]{1,2,0:T(2,128)S(1)}, u32[]{:S(2)}, u32[]{:S(2)}) async-start(f32[32,2,2]{1,2,0:T(2,128)} %copy.51), calls=%async_computation.3 | async-start | bytes 65536 | tf_op jit(solution)/shard_map/all_to_all | solution.py:91
  90.3 2.2 %copy.48 = f32[64,21,2,128]{3,2,1,0:T(2,128)} copy(f32[64,21,2,128]{3,0,2,1:T(8,128)S(1)} %fusion.39) | data formatting | bytes 2752512 | tf_op jit(solution)/shard_map/pr,vran->pvan/dot_general | solution.py:87
  92.4 4.9 %all-to-all-done.3 = f32[32,2,2]{1,2,0:T(2,128)S(1)} async-done(((f32[32,2,2]{1,2,0:T(2,128)}), f32[32,2,2]{1,2,0:T(2,128)S(1)}, u32[]{:S(2)}, u32[]{:S(2)}) %all-to-all-start.3) | async-done | bytes 544 | tf_op jit(solution)/shard_map/all_to_all | solution.py:91
  97.3 4.7 %all-to-all-start.1 = ((f32[64,21,2,128]{3,2,1,0:T(2,128)}), f32[64,21,2,128]{3,2,1,0:T(2,128)S(1)}, u32[]{:S(2)}, u32[]{:S(2)}) async-start(f32[64,21,2,128]{3,2,1,0:T(2,128)} %copy.48), calls=%async_computation.1 | async-start | bytes 2752512 | tf_op jit(solution)/shard_map/all_to_all | solution.py:90
  102.6 1.4 reduce.3
  104.3 29.0 %all-to-all-done.1 = f32[64,21,2,128]{3,2,1,0:T(2,128)S(1)} async-done(((f32[64,21,2,128]{3,2,1,0:T(2,128)}), f32[64,21,2,128]{3,2,1,0:T(2,128)S(1)}, u32[]{:S(2)}, u32[]{:S(2)}) %all-to-all-start.1) | async-done | bytes 1376288 | tf_op jit(solution)/shard_map/all_to_all | solution.py:90
  134.0 8.6 %collective-permute-start.1 = (f32[21,32,1,128]{3,1,2,0:T(8,128)S(1)}, f32[21,32,1,128]{3,1,2,0:T(8,128)S(1)}, u32[]{:S(2)}, u32[]{:S(2)}) collective-permute-start(f32[21,32,1,128]{3,1,2,0:T(8,128)S(1)} %get-tuple-element.8), channel_id=1, source_target_pairs={{0,1},{1,2},{2,3},{3,4},{4,5},{5,6},{6,7},{7,8},{8,9},{9,10},{10,1... | collective-permute-start | bytes 1032200 | tf_op jit(solution)/shard_map/ppermute | solution.py:14
  142.8 1.2 fusion.22
  144.0 2.9 %collective-permute-done.1 = f32[21,32,1,128]{3,1,2,0:T(8,128)S(1)} collective-permute-done((f32[21,32,1,128]{3,1,2,0:T(8,128)S(1)}, f32[21,32,1,128]{3,1,2,0:T(8,128)S(1)}, u32[]{:S(2)}, u32[]{:S(2)}) %collective-permute-start.1) | collective-permute-done | bytes 344096 | tf_op jit(solution)/shard_map/ppermute | solution.py:14
  146.9 3.7 %collective-permute-done = f32[21,32,1,128]{3,1,2,0:T(8,128)S(1)} collective-permute-done((f32[21,32,1,128]{3,1,2,0:T(8,128)S(1)}, f32[21,32,1,128]{3,1,2,0:T(8,128)S(1)}, u32[]{:S(2)}, u32[]{:S(2)}) %collective-permute-start) | collective-permute-done | bytes 344096 | tf_op jit(solution)/shard_map/ppermute | solution.py:16
  151.7 1.2 fusion.20
  152.9 2.5 %collective-permute-done.3 = f32[21,32,1,128]{3,1,2,0:T(8,128)S(1)} collective-permute-done((f32[21,32,1,128]{3,1,2,0:T(8,128)S(1)}, f32[21,32,1,128]{3,1,2,0:T(8,128)S(1)}, u32[]{:S(2)}, u32[]{:S(2)}) %collective-permute-start.3) | collective-permute-done | bytes 344096 | tf_op jit(solution)/shard_map/ppermute | solution.py:14
  155.4 3.7 %collective-permute-done.2 = f32[21,32,1,128]{3,1,2,0:T(8,128)S(1)} collective-permute-done((f32[21,32,1,128]{3,1,2,0:T(8,128)S(1)}, f32[21,32,1,128]{3,1,2,0:T(8,128)S(1)}, u32[]{:S(2)}, u32[]{:S(2)}) %collective-permute-start.2) | collective-permute-done | bytes 344096 | tf_op jit(solution)/shard_map/ppermute | solution.py:16
  159.6 1.4 copy.59
  (47 shorter events, 8.8 us)
Async XLA Ops:
  0.0 142.8 %copy-start = (f32[21,21]{1,0:T(8,128)S(1)}, f32[21,21]{1,0:T(8,128)}, u32[]{:S(2)}) copy-start(f32[21,21]{1,0:T(8,128)} %param.15) | copy-start | bytes 5296
  4.6 16.3 %copy-start.5 = (s32[32,2]{0,1:T(2,128)S(1)}, s32[32,2]{0,1:T(2,128)}, u32[]{:S(2)}) copy-start(s32[32,2]{0,1:T(2,128)} %param.12) | copy-start | bytes 772
  4.6 16.4 %copy-start.6 = (s32[32]{0:T(128)S(1)}, s32[32]{0:T(128)}, u32[]{:S(2)}) copy-start(s32[32]{0:T(128)} %param.9) | copy-start | bytes 388
  4.6 19.2 %copy-start.2 = (s32[32,2,128]{2,1,0:T(2,128)S(1)}, s32[32,2,128]{2,1,0:T(2,128)}, u32[]{:S(2)}) copy-start(s32[32,2,128]{2,1,0:T(2,128)} %param.10) | copy-start | bytes 98308
  4.6 19.8 %copy-start.1 = (f32[32,2,128]{2,1,0:T(2,128)S(1)}, f32[32,2,128]{2,1,0:T(2,128)}, u32[]{:S(2)}) copy-start(f32[32,2,128]{2,1,0:T(2,128)} %param.11) | copy-start | bytes 98308
  11.3 28.8 %all-to-all-start = ((f32[32,1,5376]{2,1,0:T(1,128)}), f32[32,1,5376]{2,1,0:T(1,128)S(1)}, u32[]{:S(2)}, u32[]{:S(2)}) async-start(f32[32,1,5376]{2,1,0:T(1,128)} %reshape.41), calls=%async_computation | async-start | bytes 1376256 | tf_op jit(solution)/shard_map/all_to_all | solution.py:83
  40.0 40.1 %all-to-all-start.2 = ((s32[32,2,1]{1,2,0:T(1,128)}), s32[32,2,1]{1,2,0:T(1,128)}, u32[]{:S(2)}, u32[]{:S(2)}) async-start(s32[32,2,1]{1,2,0:T(1,128)} %bitcast.6), calls=%async_computation.2 | async-start | bytes 32768 | tf_op jit(solution)/shard_map/all_to_all | solution.py:92
  80.1 21.9 %copy-start.3 = (f32[32,2,128]{2,1,0:T(2,128)S(1)}, f32[32,2,128]{2,1,0:T(2,128)}, u32[]{:S(2)}) copy-start(f32[32,2,128]{2,1,0:T(2,128)} %param.13) | copy-start | bytes 98308
  80.1 21.9 %copy-start.4 = (f32[32,2,128]{2,1,0:T(2,128)S(1)}, f32[32,2,128]{2,1,0:T(2,128)}, u32[]{:S(2)}) copy-start(f32[32,2,128]{2,1,0:T(2,128)} %param.14) | copy-start | bytes 98308
  80.1 17.2 %all-to-all-start.3 = ((f32[32,2,2]{1,2,0:T(2,128)}), f32[32,2,2]{1,2,0:T(2,128)S(1)}, u32[]{:S(2)}, u32[]{:S(2)}) async-start(f32[32,2,2]{1,2,0:T(2,128)} %copy.51), calls=%async_computation.3 | async-start | bytes 65536 | tf_op jit(solution)/shard_map/all_to_all | solution.py:91
  97.3 36.0 %all-to-all-start.1 = ((f32[64,21,2,128]{3,2,1,0:T(2,128)}), f32[64,21,2,128]{3,2,1,0:T(2,128)S(1)}, u32[]{:S(2)}, u32[]{:S(2)}) async-start(f32[64,21,2,128]{3,2,1,0:T(2,128)} %copy.48), calls=%async_computation.1 | async-start | bytes 2752512 | tf_op jit(solution)/shard_map/all_to_all | solution.py:90
  134.0 12.8 %collective-permute-start.1 = (f32[21,32,1,128]{3,1,2,0:T(8,128)S(1)}, f32[21,32,1,128]{3,1,2,0:T(8,128)S(1)}, u32[]{:S(2)}, u32[]{:S(2)}) collective-permute-start(f32[21,32,1,128]{3,1,2,0:T(8,128)S(1)} %get-tuple-element.8), channel_id=1, source_target_pairs={{0,1},{1,2},{2,3},{3,4},{4,5},{5,6},{6,7},{7,8},{8,9},{9,10},{10,1... | collective-permute-start | bytes 1032200 | tf_op jit(solution)/shard_map/ppermute | solution.py:14
  142.7 7.9 %collective-permute-start = (f32[21,32,1,128]{3,1,2,0:T(8,128)S(1)}, f32[21,32,1,128]{3,1,2,0:T(8,128)S(1)}, u32[]{:S(2)}, u32[]{:S(2)}) collective-permute-start(f32[21,32,1,128]{3,1,2,0:T(8,128)S(1)} %get-tuple-element.7), channel_id=1, source_target_pairs={{1,0},{2,1},{3,2},{4,3},{5,4},{6,5},{7,6},{8,7},{9,8},{10,9},{11,1... | collective-permute-start | bytes 1032200 | tf_op jit(solution)/shard_map/ppermute | solution.py:16
  151.1 4.2 %collective-permute-start.3 = (f32[21,32,1,128]{3,1,2,0:T(8,128)S(1)}, f32[21,32,1,128]{3,1,2,0:T(8,128)S(1)}, u32[]{:S(2)}, u32[]{:S(2)}) collective-permute-start(f32[21,32,1,128]{3,1,2,0:T(8,128)S(1)} %get-tuple-element.6), channel_id=1, source_target_pairs={{0,1},{1,2},{2,3},{3,4},{4,5},{5,6},{6,7},{7,8},{8,9},{9,10},{10,1... | collective-permute-start | bytes 1032200 | tf_op jit(solution)/shard_map/ppermute | solution.py:14
  151.2 7.9 %collective-permute-start.2 = (f32[21,32,1,128]{3,1,2,0:T(8,128)S(1)}, f32[21,32,1,128]{3,1,2,0:T(8,128)S(1)}, u32[]{:S(2)}, u32[]{:S(2)}) collective-permute-start(f32[21,32,1,128]{3,1,2,0:T(8,128)S(1)} %get-tuple-element.5), channel_id=1, source_target_pairs={{1,0},{2,1},{3,2},{4,3},{5,4},{6,5},{7,6},{8,7},{9,8},{10,9},{11,1... | collective-permute-start | bytes 1032200 | tf_op jit(solution)/shard_map/ppermute | solution.py:16
where the time goes:
time: 162 us; the launch traced here: 161 us
  waiting for transfers between devices  61.7 us (38%)
  starting transfers between devices  39 us (24%)
  local copies, waits for them, and re-layouts  31.2 us (19%)
  matrix products  21.5 us (13%)
  other arithmetic  7.24 us (4%)
    all_to_all x1, waiting for transfers between devices, shards(): lax.all_to_all(sent_rows, 'stream', split_axis=0, concat_axis=0, tiled=True)  29 us
    unnamed x20, local copies, waits for them, and re-layouts  18.7 us
    dot_general x1, matrix products, recluster(): jnp.einsum('sajk,vsak->vsaj', table, flow_state, precision=lax.Precision....  17.3 us
    all_to_all x1, waiting for transfers between devices, shards(): lax.all_to_all(state_in, 'stream', split_axis=1, concat_axis=3, tiled=True)  15 us
    all_to_all x1, starting transfers between devices, shards(): lax.all_to_all(state_in, 'stream', split_axis=1, concat_axis=3, tiled=True)  9.6 us
    all_to_all x1, starting transfers between devices, shards(): lax.all_to_all(sent_count, 'stream', split_axis=0, concat_axis=0, tiled=T...  9.24 us
    ppermute x2, starting transfers between devices, extended(): lax.ppermute(tail, axis, [(i, (i + 1) % count) for i in range(count)])  8.66 us
    ppermute x2, waiting for transfers between devices, extended(): lax.ppermute(head, axis, [((i + 1) % count, i) for i in range(count)])  7.4 us
  transfers between devices with their start and end apart: 8, of which 7 were waited for; matrix products, arithmetic and copies ran while one was open for 28% of the time, Pallas kernels for 0%

commit v1 on v0

v1 whole, which is shorter than its diff:
```python
import functools
import jax
import jax.numpy as jnp
from jax import lax
from jax.experimental import pallas as pl
from jax.experimental.pallas import tpu as pltpu
from jax.sharding import PartitionSpec as P

LANES = 128
SLOTS = 2
HIGHEST = lax.Precision.HIGHEST
F32 = jnp.float32
BF16 = jnp.bfloat16
I32 = jnp.int32


def call(body, outs, *args, flops=0):
    touched = sum(a.size * a.dtype.itemsize for a in args) + sum(
        4 * functools.reduce(lambda x, y: x * y, o.shape) for o in outs
    )
    return pl.pallas_call(
        body,
        out_shape=outs,
        in_specs=[pl.BlockSpec(memory_space=pltpu.VMEM)] * len(args),
        out_specs=[pl.BlockSpec(memory_space=pltpu.VMEM)] * len(outs),
        compiler_params=pltpu.CompilerParams(vmem_limit_bytes=24 * 2**20),
        cost_estimate=pl.CostEstimate(flops=flops, bytes_accessed=touched, transcendentals=0),
    )(*args)


def iota(shape, dim):
    return lax.broadcasted_iota(I32, shape, dim)


def split(x):
    high = x.astype(BF16).astype(F32)
    return high, x - high


def rows_of(slot, azim):
    return slot * 2 + azim


STENCIL_ROWS = 10


def stencil_pack(nid_ref, idx_ref, weight_ref, count_ref, out_ref):
    rows = STENCIL_ROWS
    stations = idx_ref.shape[0] // 2
    peers = out_ref.shape[0] // rows
    nid = nid_ref[:, :stations]
    target = nid // stations
    place = nid % stations
    owners = (iota((peers, stations), 0) == target).astype(F32)
    before = (iota((stations, stations), 0) < iota((stations, stations), 1)).astype(F32)
    earlier = jnp.dot(owners, before, preferred_element_type=F32)
    rank = jnp.sum(owners * earlier, axis=0, keepdims=True)
    lane = iota((peers, LANES), 1)
    places = jnp.full((peers, LANES), -1.0, F32)
    cell = iota((stations, LANES), 1)
    for slot in range(SLOTS):
        pick = jnp.where(rank == float(slot), owners, 0.0)
        found = jnp.sum(pick * (place + 1).astype(F32), axis=1, keepdims=True) - 1.0
        places = jnp.where(lane == slot, found, places)
        for azim in range(2):
            idx = idx_ref[pl.ds(azim, stations, stride=2), :]
            live = cell < count_ref[:, azim : azim + 1]
            idx = jnp.where(live, idx, -1).astype(F32)
            weight = weight_ref[pl.ds(azim, stations, stride=2), :]
            at = rows_of(slot, azim)
            out_ref[pl.ds(at, peers, stride=rows), :] = jnp.dot(
                pick, idx, preferred_element_type=F32
            )
            out_ref[pl.ds(4 + at, peers, stride=rows), :] = jnp.dot(
                pick, weight, preferred_element_type=F32, precision=HIGHEST
            )
    out_ref[pl.ds(8, peers, stride=rows), :] = jnp.broadcast_to(
        nid_ref[...].astype(F32), (peers, LANES)
    )
    out_ref[pl.ds(9, peers, stride=rows), :] = places


STATE_ROWS = 44


def state_pack(got_ref, x_ref, out_ref):
    rows, stencil_rows = STATE_ROWS, STENCIL_ROWS
    peers = out_ref.shape[0] // rows
    total = x_ref.shape[1]
    new_rows = got_ref[pl.ds(8, peers, stride=stencil_rows), :].astype(I32)
    quarter = iota((1, LANES), 1) // 32
    tiles = []
    for tile in range(total // LANES):
        row = new_rows[4 * tile : 4 * tile + 1]
        for i in range(1, 4):
            row = jnp.where(quarter == i, new_rows[4 * tile + i : 4 * tile + i + 1], row)
        tiles.append(row)
    nid = jnp.concatenate(tiles, axis=1)
    high, low = split(x_ref[...])
    both = jnp.concatenate([high, low], axis=0).astype(BF16)
    lines = x_ref.shape[0]
    width = 2 * LANES
    for chunk in range(total // width):
        pick = jnp.where(iota((width, total), 0) + chunk * width == nid, 1.0, 0.0).astype(BF16)
        moved = lax.dot_general(
            both, pick, (((1,), (1,)), ((), ())), preferred_element_type=F32
        )
        moved = moved[:lines] + moved[lines:]
        for tile in range(2):
            y = moved[:, tile * LANES : (tile + 1) * LANES]
            first = (chunk * 2 + tile) * 4
            for group in range(5):
                part = [y[(4 * group + i) * 8 : (4 * group + i + 1) * 8] for i in range(4)]
                turned = []
                for d in range(4):
                    diag = part[d]
                    for q in range(1, 4):
                        diag = jnp.where(quarter == q, part[(q + d) % 4], diag)
                    turned.append(diag if d == 0 else pltpu.roll(diag, 32 * d, 1))
                for q in range(4):
                    out = turned[(-q) % 4]
                    for i in range(1, 4):
                        out = jnp.where(quarter == i, turned[(i - q) % 4], out)
                    at = (first + q) * rows + 8 * group
                    out_ref[at : at + 8, :] = out
            rest = y[160:168]
            turned = [rest] + [pltpu.roll(rest, 32 * d, 1) for d in range(1, 4)]
            for q in range(4):
                out = jnp.where(quarter == 0, turned[(-q) % 4][:4], turned[(1 - q) % 4][4:])
                at = (first + q) * rows + 40
                out_ref[at : at + 4, :] = out


def stencil_place(got_ref, speed_ref, diffuse_ref, low_ref, up_ref, wl_ref, wu_ref, lines_ref):
    rows = STENCIL_ROWS
    peers = got_ref.shape[0] // rows
    stations = low_ref.shape[0] // 2
    spots = got_ref[pl.ds(9, peers, stride=rows), :].T
    place = iota((stations, peers), 0).astype(F32)
    picks = [jnp.where(spots[slot : slot + 1, :] == place, 1.0, 0.0) for slot in range(SLOTS)]
    for azim in range(2):
        idx = jnp.zeros((stations, LANES), F32)
        weight = jnp.zeros((stations, LANES), F32)
        for slot in range(SLOTS):
            at = rows_of(slot, azim)
            idx += jnp.dot(
                picks[slot],
                got_ref[pl.ds(at, peers, stride=rows), :],
                preferred_element_type=F32,
            )
            weight += jnp.dot(
                picks[slot],
                got_ref[pl.ds(4 + at, peers, stride=rows), :],
                preferred_element_type=F32,
                precision=HIGHEST,
            )
        live = idx >= 0.0
        low = jnp.where(live, idx, 0.0).astype(I32)
        up = low + 1
        here = pl.ds(azim * stations, stations)
        low_ref[here, :] = (low % 4) * 32 + low // 4
        up_ref[here, :] = (up % 4) * 32 + up // 4
        wl_ref[here, :] = jnp.where(live, 1.0 - weight, 0.0)
        wu_ref[here, :] = jnp.where(live, weight, 0.0)
        lines_ref[pl.ds(azim * stations, stations), :] = speed_ref[
            pl.ds(azim, stations, stride=2), :
        ]
        lines_ref[pl.ds((2 + azim) * stations, stations), :] = diffuse_ref[
            pl.ds(azim, stations, stride=2), :
        ]
        lines_ref[pl.ds((4 + azim) * stations, stations), :] = jnp.where(live, 1.0, 0.0)


def refit(got_ref, low_ref, up_ref, wl_ref, wu_ref, out_ref):
    rows = STATE_ROWS
    stations = low_ref.shape[0] // 2

    def lines(first_row):
        cells = [
            got_ref[pl.ds(block * 8 * rows + first_row + c, 8, stride=rows), :]
            for c in range(4)
            for block in range(4)
        ]
        return jnp.concatenate(cells, axis=0).T

    def fit(x, azim, line):
        here = pl.ds(azim * stations, stations)
        lower = jnp.take_along_axis(x, low_ref[here, :], axis=1)
        upper = jnp.take_along_axis(x, up_ref[here, :], axis=1)
        out_ref[pl.ds(line * stations, stations), :] = (
            wl_ref[here, :] * lower + wu_ref[here, :] * upper
        )

    for group in range(5):
        for half in range(2):
            x = lines(8 * group + 4 * half)
            for i in range(4):
                fit(x[i * stations : (i + 1) * stations], half, 8 * group + 2 * i + half)
    x = lines(40)
    for half in range(2):
        fit(x[half * stations : (half + 1) * stations], half, 40 + half)


def sections(m_ref, left_ref, right_ref, lines_ref, lines_left_ref, lines_right_ref, mix_ref, out_ref):
    nv = m_ref.shape[0]
    stations = m_ref.shape[1] // 2
    cell = iota((nv, 8, LANES), 2)
    mix = mix_ref[...]

    def mixed(fields):
        x = jnp.concatenate([f.reshape(nv * 8, LANES) for f in fields], axis=1)
        high, low = split(x)
        pad = jnp.zeros((8, x.shape[1]), F32)
        stacked = jnp.concatenate([high, low, high, pad], axis=0).astype(BF16)
        y = jnp.dot(mix, stacked, preferred_element_type=F32)[: nv * 8]
        return [
            y[:, i * LANES : (i + 1) * LANES].reshape(nv, 8, LANES) for i in range(len(fields))
        ]

    def rate(below, center, above, term, speed, diffuse):
        lateral = (above + below) - 2.0 * center
        shifted = jnp.where(cell == 0, 0.0, pltpu.roll(center, 1, 2))
        return diffuse * lateral - speed * (center - shifted) - term

    def coefficients(ref, azim, block):
        def one(kind):
            return ref[pl.ds((2 * kind + azim) * stations + 8 * block, 8), :][None]

        return one(0), one(1), one(2)

    for block in range(stations // 8):
        def line(ref, azim):
            return ref[:, pl.ds(azim * stations + 8 * block, 8), :]

        field = [line(r, a) for r in (left_ref, m_ref, right_ref) for a in range(2)]
        co = [
            coefficients(lines_left_ref, 1, block),
            coefficients(lines_ref, 0, block),
            coefficients(lines_ref, 1, block),
            coefficients(lines_right_ref, 0, block),
        ]
        term = mixed(field[1:5])
        first = []
        for i in range(4):
            speed, diffuse, active = co[i]
            r = rate(field[i], field[i + 1], field[i + 2], term[i], speed, diffuse)
            first.append(field[i + 1] + active * r)
        term = mixed(first[1:3])
        for azim in range(2):
            speed, diffuse, active = co[1 + azim]
            r = rate(first[azim], first[azim + 1], first[azim + 2], term[azim], speed, diffuse)
            out = 0.5 * ((field[2 + azim] + first[1 + azim]) + active * r)
            out_ref[:, pl.ds(azim + 16 * block, 8, stride=2), :] = out


def shards(
    state_in,
    new_index,
    stencil_index,
    stencil_weight,
    cell_count,
    normal_speed,
    azim_diffusion,
    mixing,
):
    peers = lax.axis_size("stream")
    count = lax.axis_size("azim")
    nv, total, _, cells = state_in.shape
    stations = new_index.shape[0]
    shape = jax.ShapeDtypeStruct

    def flat(a):
        return a.reshape(2 * stations, LANES)

    def exchange(a):
        return lax.all_to_all(a, "stream", split_axis=0, concat_axis=0, tiled=True)

    def neighbours(a):
        up = [(i, (i + 1) % count) for i in range(count)]
        down = [((i + 1) % count, i) for i in range(count)]
        return lax.ppermute(a, "azim", up), lax.ppermute(a, "azim", down)

    (packed,) = call(
        stencil_pack,
        [shape((peers * STENCIL_ROWS, LANES), F32)],
        jnp.tile(new_index, LANES // stations)[None],
        flat(stencil_index),
        flat(stencil_weight),
        cell_count,
    )
    got = exchange(packed)

    x = state_in.transpose(0, 2, 3, 1).reshape(nv * 2 * cells, total)
    (packed,) = call(state_pack, [shape((peers * STATE_ROWS, LANES), F32)], got, x)
    got_state = exchange(packed)

    plane = shape((2 * stations, LANES), F32)
    index_plane = shape((2 * stations, LANES), I32)
    low, up, wl, wu, lines = call(
        stencil_place,
        [index_plane, index_plane, plane, plane, shape((6 * stations, LANES), F32)],
        got,
        flat(normal_speed),
        flat(azim_diffusion),
    )
    lines_left, lines_right = neighbours(lines)

    (moved,) = call(
        refit, [shape((nv * 2 * stations, LANES), F32)], got_state, low, up, wl, wu
    )
    left, right = neighbours(moved)

    mix = 0.25 * mixing
    high = lax.reduce_precision(mix, 8, 7)
    eye = jnp.eye(8, dtype=F32)

    def spread(a):
        return (a[:, None, :, None] * eye[None, :, None, :]).reshape(nv * 8, nv * 8)

    wide = jnp.concatenate([spread(high), spread(high), spread(mix - high)], axis=1)
    wide = jnp.pad(wide, ((0, 8), (0, 8))).astype(BF16)
    field = (nv, 2 * stations, LANES)
    (out,) = call(
        sections,
        [shape(field, F32)],
        moved.reshape(field),
        left.reshape(field),
        right.reshape(field),
        lines,
        lines_left,
        lines_right,
        wide,
    )
    return out.reshape(nv, stations, 2, LANES)


def solution(mesh):
    in_specs = (
        P(None, None, "azim", "stream"),
        P("stream"),
        P("stream", "azim", None),
        P("stream", "azim", None),
        P("stream", "azim"),
        P("stream", "azim", None),
        P("stream", "azim", None),
        P(),
    )
    out_specs = P(None, "stream", "azim", None)
    return jax.shard_map(shards, mesh=mesh, in_specs=in_specs, out_specs=out_specs, check_vma=False)
```

time: 162 us -> 78.6 us (0.49)
  the two profiles are of different devices: /device:TPU:201 before, /device:TPU:8 now
where the time goes in v1:
time: 78.6 us; the launch traced here: 78.1 us
  waiting for transfers between devices  39.6 us (50%)
  starting transfers between devices  24 us (31%)
  local copies, waits for them, and re-layouts  7.61 us (10%)
  Pallas kernels  5.32 us (7%)
  other arithmetic  1.47 us (2%)
    all_to_all x2, waiting for transfers between devices, exchange(): return lax.all_to_all(a, 'stream', split_axis=0, concat_axis=0, tiled=True)  34 us
    all_to_all x2, starting transfers between devices, exchange(): return lax.all_to_all(a, 'stream', split_axis=0, concat_axis=0, tiled=True)  14.9 us
    ppermute x4, starting transfers between devices, neighbours(): return (lax.ppermute(a, 'azim', up), lax.ppermute(a, 'azim', down))  9.19 us
    ppermute x4, waiting for transfers between devices, neighbours(): return (lax.ppermute(a, 'azim', up), lax.ppermute(a, 'azim', down))  5.57 us
    pallas_call x5, Pallas kernels, call(): pl.pallas_call(body, out_shape=outs, in_specs=[pl.BlockSpec(memory_space=...  5.32 us
    unnamed x13, local copies, waits for them, and re-layouts  2.29 us
    another operation x1, local copies, waits for them, and re-layouts  1.99 us
    all_to_all x4, local copies, waits for them, and re-layouts, exchange(): return lax.all_to_all(a, 'stream', split_axis=0, concat_axis=0, tiled=True)  1.76 us
  transfers between devices with their start and end apart: 6, of which 4 were waited for; matrix products, arithmetic and copies ran while one was open for 5% of the time, Pallas kernels for 0%

profile of v1, /device:TPU:8, one launch (start us, length us, event | category | flops | bytes accessed | tf_op | source)
XLA Modules:
  0.0 78.1 jit_solution(3731679162948996820)
XLA Ops:
  0.0 0.7 tile.2
  0.7 0.8 copy.10.count_ref
  1.5 0.8 copy-done
  2.3 0.8 copy-done.1
  3.0 0.3 shard_map.82
  3.4 0.7 all_to_all.14
  4.1 10.2 %all-to-all-start = ((f32[32,10,128]{2,1,0:T(8,128)}), f32[32,10,128]{2,1,0:T(8,128)S(1)}, u32[]{:S(2)}, u32[]{:S(2)}) async-start(f32[32,10,128]{2,1,0:T(8,128)} %all_to_all.14), calls=%async_computation | async-start | bytes 524288 | tf_op jit(solution)/shard_map/all_to_all | solution.py:276
  14.3 0.2 reshape.54.x_ref
  14.5 12.0 %all-to-all-done = f32[32,10,128]{2,1,0:T(8,128)S(1)} async-done(((f32[32,10,128]{2,1,0:T(8,128)}), f32[32,10,128]{2,1,0:T(8,128)S(1)}, u32[]{:S(2)}, u32[]{:S(2)}) %all-to-all-start) | async-done | bytes 163872 | tf_op jit(solution)/shard_map/all_to_all | solution.py:276
  26.6 1.1 %shard_map.83 = f32[1408,128]{1,0:T(8,128)S(1)} custom-call(f32[320,128]{1,0:T(8,128)S(1)} %all_to_all.16.got_ref, f32[168,1024]{1,0:T(8,128)S(1)} %reshape.54.x_ref), custom_call_target="tpu_custom_call" | custom-call | bytes 1572864 | tf_op jit(solution)/shard_map/pallas_call | solution.py:21
  27.6 1.0 %all_to_all.17 = f32[32,44,128]{2,1,0:T(8,128)} reshape(f32[1408,128]{1,0:T(8,128)S(1)} %shard_map.83) | data formatting | bytes 1441792 | tf_op jit(solution)/shard_map/all_to_all | solution.py:276
  28.6 4.7 %all-to-all-start.1 = ((f32[32,44,128]{2,1,0:T(8,128)}), f32[32,44,128]{2,1,0:T(8,128)S(1)}, u32[]{:S(2)}, u32[]{:S(2)}) async-start(f32[32,44,128]{2,1,0:T(8,128)} %all_to_all.17), calls=%async_computation.1 | async-start | bytes 1572864 | tf_op jit(solution)/shard_map/all_to_all | solution.py:276
  33.3 0.3 shard_map.84
  33.6 22.0 %all-to-all-done.1 = f32[32,44,128]{2,1,0:T(8,128)S(1)} async-done(((f32[32,44,128]{2,1,0:T(8,128)}), f32[32,44,128]{2,1,0:T(8,128)S(1)}, u32[]{:S(2)}, u32[]{:S(2)}) %all-to-all-start.1) | async-done | bytes 720928 | tf_op jit(solution)/shard_map/all_to_all | solution.py:276
  55.6 1.1 %shard_map.85 = f32[1344,128]{1,0:T(8,128)S(1)} custom-call(f32[1408,128]{1,0:T(8,128)S(1)} %all_to_all.19.got_ref, s32[64,128]{1,0:T(8,128)S(1)} %get-tuple-element.10.low_ref, s32[64,128]{1,0:T(8,128)S(1)} %get-tuple-element.11.up_ref, f32[64,128]{1,0:T(8,128)S(1)} %get-tuple-element.12.wl_ref, f32[64,128]{1,0:T(8,128)S(1)} %get-tuple-element.13.wu_ref), custom_call_target="tpu_custom_call" | custom-call | bytes 1540096 | tf_op jit(solution)/shard_map/pallas_call | solution.py:21
  56.7 5.4 %collective-permute-start.1 = (f32[1344,128]{1,0:T(8,128)S(1)}, f32[1344,128]{1,0:T(8,128)S(1)}, u32[]{:S(2)}, u32[]{:S(2)}) collective-permute-start(f32[1344,128]{1,0:T(8,128)S(1)} %shard_map.85), channel_id=1, source_target_pairs={{1,0},{2,1},{3,2},{4,3},{5,4},{6,5},{7,6},{8,7},{9,8},{10,9},{11,1... | collective-permute-start | bytes 2064392 | tf_op jit(solution)/shard_map/ppermute | solution.py:281
  62.2 1.3 %multiply_convert_fusion.1 = (bf16[21,8,21,8]{3,2,1,0:T(8,128)(2,1)}, bf16[21,8,21,8]{3,2,1,0:T(8,128)(2,1)S(1)}) fusion(f32[8,8]{1,0:T(8,128)S(1)} %fusion.9, f32[21,21]{1,0:T(8,128)S(1)} %get-tuple-element.15, f32[21,21]{1,0:T(8,128)S(1)} %get-tuple-element.16), kind=kLoop, calls=%fused_computation.1 | loop fusion | flops 112896 | bytes 116680 | tf_op jit(solution)/shard_map/convert.2
  63.5 2.0 %reshape.61 = bf16[168,168]{1,0:T(8,128)(2,1)S(1)} reshape(bf16[21,8,21,8]{3,2,1,0:T(8,128)(2,1)} %get-tuple-element.17) | data formatting | bytes 112896 | tf_op jit(solution)/shard_map/convert.2
  65.5 0.6 mul.55
  66.1 3.7 %collective-permute-start.3 = (f32[192,128]{1,0:T(8,128)S(1)}, f32[192,128]{1,0:T(8,128)S(1)}, u32[]{:S(2)}, u32[]{:S(2)}) collective-permute-start(f32[192,128]{1,0:T(8,128)S(1)} %get-tuple-element.14.lines_ref), channel_id=1, source_target_pairs={{1,0},{2,1},{3,2},{4,3},{5,4},{6,5},{7,6},{8,7},{9,8},{10,9},{11,1... | collective-permute-start | bytes 294920 | tf_op jit(solution)/shard_map/ppermute | solution.py:281
  69.9 0.1 fusion.8.mix_ref
  70.0 2.1 %collective-permute-done.3.lines_right_ref = f32[192,128]{1,0:T(8,128)S(1)} collective-permute-done((f32[192,128]{1,0:T(8,128)S(1)}, f32[192,128]{1,0:T(8,128)S(1)}, u32[]{:S(2)}, u32[]{:S(2)}) %collective-permute-start.3) | collective-permute-done | bytes 98336 | tf_op jit(solution)/shard_map/ppermute | solution.py:281
  72.1 3.5 %collective-permute-done.2.lines_left_ref = f32[192,128]{1,0:T(8,128)S(1)} collective-permute-done((f32[192,128]{1,0:T(8,128)S(1)}, f32[192,128]{1,0:T(8,128)S(1)}, u32[]{:S(2)}, u32[]{:S(2)}) %collective-permute-start.2) | collective-permute-done | bytes 98336 | tf_op jit(solution)/shard_map/ppermute | solution.py:281
  75.6 2.6 %shard_map.86 = f32[21,64,128]{2,1,0:T(8,128)} custom-call(f32[21,64,128]{2,1,0:T(8,128)S(1)} %bitcast.9, f32[21,64,128]{2,1,0:T(8,128)S(1)} %bitcast.11, f32[21,64,128]{2,1,0:T(8,128)S(1)} %bitcast.10, f32[192,128]{1,0:T(8,128)S(1)} %get-tuple-element.14.lines_ref, f32[192,128]{1,0:T(8,128)S(1)} %collective-permute-done.2.lines_left_ref, ...), custom_call_target="tpu_custom_call" | custom-call | bytes 3227648 | tf_op jit(solution)/shard_map/pallas_call | solution.py:21
  (19 shorter events, 0.2 us)
Async XLA Ops:
  1.5 0.8 copy-start
  2.3 0.8 copy-start.1
  3.0 11.2 %copy-start.4 = (f32[21,1024,2,4]{1,3,2,0:T(4,128)S(1)}, f32[21,1024,2,4]{1,3,2,0:T(4,128)}, u32[]{:S(2)}) copy-start(f32[21,1024,2,4]{1,3,2,0:T(4,128)} %param.8) | copy-start | bytes 2064388
  4.1 22.5 %all-to-all-start = ((f32[32,10,128]{2,1,0:T(8,128)}), f32[32,10,128]{2,1,0:T(8,128)S(1)}, u32[]{:S(2)}, u32[]{:S(2)}) async-start(f32[32,10,128]{2,1,0:T(8,128)} %all_to_all.14), calls=%async_computation | async-start | bytes 524288 | tf_op jit(solution)/shard_map/all_to_all | solution.py:276
  28.6 4.7 %copy-start.2 = (f32[32,2,128]{2,1,0:T(2,128)S(1)}, f32[32,2,128]{2,1,0:T(2,128)}, u32[]{:S(2)}) copy-start(f32[32,2,128]{2,1,0:T(2,128)} %param.13) | copy-start | bytes 98308
  28.6 4.7 %copy-start.3 = (f32[32,2,128]{2,1,0:T(2,128)S(1)}, f32[32,2,128]{2,1,0:T(2,128)}, u32[]{:S(2)}) copy-start(f32[32,2,128]{2,1,0:T(2,128)} %param.14) | copy-start | bytes 98308
  28.6 27.0 %all-to-all-start.1 = ((f32[32,44,128]{2,1,0:T(8,128)}), f32[32,44,128]{2,1,0:T(8,128)S(1)}, u32[]{:S(2)}, u32[]{:S(2)}) async-start(f32[32,44,128]{2,1,0:T(8,128)} %all_to_all.17), calls=%async_computation.1 | async-start | bytes 1572864 | tf_op jit(solution)/shard_map/all_to_all | solution.py:276
  55.6 6.5 %copy-start.5 = (f32[21,21]{1,0:T(8,128)S(1)}, f32[21,21]{1,0:T(8,128)}, u32[]{:S(2)}) copy-start(f32[21,21]{1,0:T(8,128)} %param.15) | copy-start | bytes 5296
  56.7 18.8 %collective-permute-start.1 = (f32[1344,128]{1,0:T(8,128)S(1)}, f32[1344,128]{1,0:T(8,128)S(1)}, u32[]{:S(2)}, u32[]{:S(2)}) collective-permute-start(f32[1344,128]{1,0:T(8,128)S(1)} %shard_map.85), channel_id=1, source_target_pairs={{1,0},{2,1},{3,2},{4,3},{5,4},{6,5},{7,6},{8,7},{9,8},{10,9},{11,1... | collective-permute-start | bytes 2064392 | tf_op jit(solution)/shard_map/ppermute | solution.py:281
  62.2 13.4 %collective-permute-start = (f32[1344,128]{1,0:T(8,128)S(1)}, f32[1344,128]{1,0:T(8,128)S(1)}, u32[]{:S(2)}, u32[]{:S(2)}) collective-permute-start(f32[1344,128]{1,0:T(8,128)S(1)} %shard_map.85), channel_id=1, source_target_pairs={{0,1},{1,2},{2,3},{3,4},{4,5},{5,6},{6,7},{7,8},{8,9},{9,10},{10,1... | collective-permute-start | bytes 2064392 | tf_op jit(solution)/shard_map/ppermute | solution.py:281
  66.1 6.0 %collective-permute-start.3 = (f32[192,128]{1,0:T(8,128)S(1)}, f32[192,128]{1,0:T(8,128)S(1)}, u32[]{:S(2)}, u32[]{:S(2)}) collective-permute-start(f32[192,128]{1,0:T(8,128)S(1)} %get-tuple-element.14.lines_ref), channel_id=1, source_target_pairs={{1,0},{2,1},{3,2},{4,3},{5,4},{6,5},{7,6},{8,7},{9,8},{10,9},{11,1... | collective-permute-start | bytes 294920 | tf_op jit(solution)/shard_map/ppermute | solution.py:281
  69.9 5.7 %collective-permute-start.2 = (f32[192,128]{1,0:T(8,128)S(1)}, f32[192,128]{1,0:T(8,128)S(1)}, u32[]{:S(2)}, u32[]{:S(2)}) collective-permute-start(f32[192,128]{1,0:T(8,128)S(1)} %get-tuple-element.14.lines_ref), channel_id=1, source_target_pairs={{0,1},{1,2},{2,3},{3,4},{4,5},{5,6},{6,7},{7,8},{8,9},{9,10},{10,1... | collective-permute-start | bytes 294920 | tf_op jit(solution)/shard_map/ppermute | solution.py:281

commit v2 on v1

--- a/solution.py
+++ b/solution.py
@@ -14,15 +14,16 @@
 I32 = jnp.int32
 
 
-def call(body, outs, *args, flops=0):
+def call(body, outs, *args, flops=0, space=pltpu.VMEM, scratch=()):
     touched = sum(a.size * a.dtype.itemsize for a in args) + sum(
         4 * functools.reduce(lambda x, y: x * y, o.shape) for o in outs
     )
     return pl.pallas_call(
         body,
         out_shape=outs,
-        in_specs=[pl.BlockSpec(memory_space=pltpu.VMEM)] * len(args),
+        in_specs=[pl.BlockSpec(memory_space=space)] * len(args),
         out_specs=[pl.BlockSpec(memory_space=pltpu.VMEM)] * len(outs),
+        scratch_shapes=list(scratch),
         compiler_params=pltpu.CompilerParams(vmem_limit_bytes=24 * 2**20),
         cost_estimate=pl.CostEstimate(flops=flops, bytes_accessed=touched, transcendentals=0),
     )(*args)
@@ -44,27 +45,45 @@
 STENCIL_ROWS = 10
 
 
-def stencil_pack(nid_ref, idx_ref, weight_ref, count_ref, out_ref):
+def stencil_pack(nid_hbm, idx_hbm, weight_hbm, count_hbm, out_ref, nid_ref, idx_ref, weight_ref, count_ref, sems):
+    pairs = [(nid_hbm, nid_ref), (count_hbm, count_ref), (idx_hbm, idx_ref), (weight_hbm, weight_ref)]
+    copies = [pltpu.make_async_copy(a, b, sems.at[i]) for i, (a, b) in enumerate(pairs)]
+    for copy in copies:
+        copy.start()
+    for copy in copies:
+        copy.wait()
     rows = STENCIL_ROWS
     stations = idx_ref.shape[0] // 2
     peers = out_ref.shape[0] // rows
-    nid = nid_ref[:, :stations]
+    nid = nid_ref[...]
     target = nid // stations
     place = nid % stations
     owners = (iota((peers, stations), 0) == target).astype(F32)
     before = (iota((stations, stations), 0) < iota((stations, stations), 1)).astype(F32)
     earlier = jnp.dot(owners, before, preferred_element_type=F32)
     rank = jnp.sum(owners * earlier, axis=0, keepdims=True)
+    same = iota((stations, stations), 0) == iota((stations, stations), 1)
+    spread = (iota((stations, LANES), 1) % stations == iota((stations, LANES), 0)).astype(F32)
+    wide = jnp.dot(
+        jnp.broadcast_to(nid.astype(F32), (peers, stations)),
+        spread,
+        preferred_element_type=F32,
+        precision=HIGHEST,
+    )
     lane = iota((peers, LANES), 1)
     places = jnp.full((peers, LANES), -1.0, F32)
     cell = iota((stations, LANES), 1)
+    counts = [
+        jnp.sum(jnp.where(same, count_ref[azim : azim + 1, :], 0), axis=1, keepdims=True)
+        for azim in range(2)
+    ]
     for slot in range(SLOTS):
         pick = jnp.where(rank == float(slot), owners, 0.0)
         found = jnp.sum(pick * (place + 1).astype(F32), axis=1, keepdims=True) - 1.0
         places = jnp.where(lane == slot, found, places)
         for azim in range(2):
             idx = idx_ref[pl.ds(azim, stations, stride=2), :]
-            live = cell < count_ref[:, azim : azim + 1]
+            live = cell < counts[azim]
             idx = jnp.where(live, idx, -1).astype(F32)
             weight = weight_ref[pl.ds(azim, stations, stride=2), :]
             at = rows_of(slot, azim)
@@ -74,9 +93,7 @@
             out_ref[pl.ds(4 + at, peers, stride=rows), :] = jnp.dot(
                 pick, weight, preferred_element_type=F32, precision=HIGHEST
             )
-    out_ref[pl.ds(8, peers, stride=rows), :] = jnp.broadcast_to(
-        nid_ref[...].astype(F32), (peers, LANES)
-    )
+    out_ref[pl.ds(8, peers, stride=rows), :] = wide
     out_ref[pl.ds(9, peers, stride=rows), :] = places
 
 
@@ -131,7 +148,25 @@
                 out_ref[at : at + 4, :] = out
 
 
-def stencil_place(got_ref, speed_ref, diffuse_ref, low_ref, up_ref, wl_ref, wu_ref, lines_ref):
+def stencil_place(
+    got_ref, speed_ref, diffuse_ref, mixing_ref, low_ref, up_ref, wl_ref, wu_ref, lines_ref, mix_ref
+):
+    nv = mixing_ref.shape[0]
+    high, low = split(0.25 * mixing_ref[...])
+    by_row = (iota((mix_ref.shape[0], nv), 0) // 8 == iota((mix_ref.shape[0], nv), 1)).astype(F32)
+    by_column = (iota((nv, 8 * nv), 0) == iota((nv, 8 * nv), 1) // 8).astype(F32)
+    both = [
+        jnp.dot(
+            jnp.dot(by_row, part, preferred_element_type=F32),
+            by_column,
+            preferred_element_type=F32,
+        )
+        for part in (high, low)
+    ]
+    same = iota(both[0].shape, 0) % 8 == iota(both[0].shape, 1) % 8
+    both = [jnp.where(same, part, 0.0) for part in both]
+    rest = jnp.zeros((mix_ref.shape[0], mix_ref.shape[1] - 24 * nv), F32)
+    mix_ref[...] = jnp.concatenate([both[0], both[0], both[1], rest], axis=1).astype(BF16)
     rows = STENCIL_ROWS
     peers = got_ref.shape[0] // rows
     stations = low_ref.shape[0] // 2
@@ -272,8 +307,10 @@
     def flat(a):
         return a.reshape(2 * stations, LANES)
 
-    def exchange(a):
-        return lax.all_to_all(a, "stream", split_axis=0, concat_axis=0, tiled=True)
+    def exchange(a, rows, tile):
+        parts = a.reshape(peers, rows // tile, tile, LANES)
+        parts = lax.all_to_all(parts, "stream", split_axis=0, concat_axis=0, tiled=True)
+        return parts.reshape(peers * rows, LANES)
 
     def neighbours(a):
         up = [(i, (i + 1) % count) for i in range(count)]
@@ -283,42 +320,52 @@
     (packed,) = call(
         stencil_pack,
         [shape((peers * STENCIL_ROWS, LANES), F32)],
-        jnp.tile(new_index, LANES // stations)[None],
+        new_index[None],
         flat(stencil_index),
         flat(stencil_weight),
-        cell_count,
-    )
-    got = exchange(packed)
+        cell_count.T,
+        space=pltpu.HBM,
+        scratch=[
+            pltpu.VMEM((1, stations), I32),
+            pltpu.VMEM((2 * stations, LANES), I32),
+            pltpu.VMEM((2 * stations, LANES), F32),
+            pltpu.VMEM((2, stations), I32),
+            pltpu.SemaphoreType.DMA((4,)),
+        ],
+    )
+    got = exchange(packed, STENCIL_ROWS, 2)
 
     x = state_in.transpose(0, 2, 3, 1).reshape(nv * 2 * cells, total)
     (packed,) = call(state_pack, [shape((peers * STATE_ROWS, LANES), F32)], got, x)
-    got_state = exchange(packed)
+    got_state = exchange(packed, STATE_ROWS, 4)
 
     plane = shape((2 * stations, LANES), F32)
     index_plane = shape((2 * stations, LANES), I32)
-    low, up, wl, wu, lines = call(
+    low, up, wl, wu, lines, mix = call(
         stencil_place,
-        [index_plane, index_plane, plane, plane, shape((6 * stations, LANES), F32)],
+        [
+            index_plane,
+            index_plane,
+            plane,
+            plane,
+            shape((6 * stations, LANES), F32),
+            shape((8 * nv + 8, 24 * nv + 8), BF16),
+        ],
         got,
         flat(normal_speed),
         flat(azim_diffusion),
+        mixing,
     )
     lines_left, lines_right = neighbours(lines)
+    got_state, lines_left, lines_right = lax.optimization_barrier(
+        (got_state, lines_left, lines_right)
+    )
 
     (moved,) = call(
         refit, [shape((nv * 2 * stations, LANES), F32)], got_state, low, up, wl, wu
     )
     left, right = neighbours(moved)
 
-    mix = 0.25 * mixing
-    high = lax.reduce_precision(mix, 8, 7)
-    eye = jnp.eye(8, dtype=F32)
-
-    def spread(a):
-        return (a[:, None, :, None] * eye[None, :, None, :]).reshape(nv * 8, nv * 8)
-
-    wide = jnp.concatenate([spread(high), spread(high), spread(mix - high)], axis=1)
-    wide = jnp.pad(wide, ((0, 8), (0, 8))).astype(BF16)
     field = (nv, 2 * stations, LANES)
     (out,) = call(
         sections,
@@ -329,7 +376,7 @@
         lines,
         lines_left,
         lines_right,
-        wide,
+        mix,
     )
     return out.reshape(nv, stations, 2, LANES)
 

time: 78.6 us -> 73.4 us (0.934)
  waiting for transfers between devices: 39.6 us -> 34.6 us
  local copies, waits for them, and re-layouts: 7.61 us -> 3.54 us
  starting transfers between devices: 24 us -> 27.5 us
  Pallas kernels: 5.32 us -> 7.11 us
  other arithmetic: 1.47 us -> 0 us
    all_to_all x2, waiting for transfers between devices: 34 us -> 17.2 us  [exchange(): lax.all_to_all(parts, 'stream', split_axis=0, concat_axis=0, tiled=True)]
    ppermute x4, waiting for transfers between devices: 5.57 us -> 17.4 us  [neighbours(): return (lax.ppermute(a, 'azim', up), lax.ppermute(a, 'azim', down))]
    ppermute x4, starting transfers between devices: 9.19 us -> 12.8 us  [neighbours(): return (lax.ppermute(a, 'azim', up), lax.ppermute(a, 'azim', down))]
    another operation x3 -> x0, local copies, waits for them, and re-layouts: 2.73 us -> none
    pallas_call x5, Pallas kernels: 5.32 us -> 7.11 us  [call(): pl.pallas_call(body, out_shape=outs, in_specs=[pl.BlockSpec(memory_space=...]
    all_to_all x4 -> x0, local copies, waits for them, and re-layouts: 1.76 us -> none  [exchange(): return lax.all_to_all(a, 'stream', split_axis=0, concat_axis=0, tiled=True)]
    another operation x1 -> x0, other arithmetic: 1.33 us -> none
    reshape x1, local copies, waits for them, and re-layouts: 0.24 us -> 1.34 us  [shards(): x = state_in.transpose(0, 2, 3, 1).reshape(nv * 2 * cells, total)]
  transfers between devices with their start and end apart: 6 -> 6, of which waited for: 4 -> 6; matrix products, arithmetic and copies ran while one was open for 5% -> 2% of each run, Pallas kernels for 0% -> 1%
where the time goes in v2:
time: 73.4 us; the launch traced here: 72.8 us
  waiting for transfers between devices  34.6 us (47%)
  starting transfers between devices  27.5 us (37%)
  Pallas kernels  7.11 us (10%)
  local copies, waits for them, and re-layouts  3.54 us (5%)
    ppermute x4, waiting for transfers between devices, neighbours(): return (lax.ppermute(a, 'azim', up), lax.ppermute(a, 'azim', down))  17.4 us
    all_to_all x2, waiting for transfers between devices, exchange(): lax.all_to_all(parts, 'stream', split_axis=0, concat_axis=0, tiled=True)  17.2 us
    all_to_all x2, starting transfers between devices, exchange(): lax.all_to_all(parts, 'stream', split_axis=0, concat_axis=0, tiled=True)  14.7 us
    ppermute x4, starting transfers between devices, neighbours(): return (lax.ppermute(a, 'azim', up), lax.ppermute(a, 'azim', down))  12.8 us
    pallas_call x5, Pallas kernels, call(): pl.pallas_call(body, out_shape=outs, in_specs=[pl.BlockSpec(memory_space=...  7.11 us
    unnamed x14, local copies, waits for them, and re-layouts  2.21 us
  transfers between devices with their start and end apart: 6, of which 6 were waited for; matrix products, arithmetic and copies ran while one was open for 2% of the time, Pallas kernels for 1%

profile of v2, /device:TPU:8, one launch (start us, length us, event | category | flops | bytes accessed | tf_op | source)
XLA Modules:
  0.0 72.8 jit_solution(13997076768547850000)
XLA Ops:
  0.0 0.7 copy-done.5
  0.7 0.8 %copy-done = s32[32,2,128]{2,1,0:T(2,128)S(1)} copy-done((s32[32,2,128]{2,1,0:T(2,128)S(1)}, s32[32,2,128]{2,1,0:T(2,128)}, u32[]{:S(2)}) %copy-start) | copy-done | bytes 32792
  1.4 0.8 %copy-done.1 = f32[32,2,128]{2,1,0:T(2,128)S(1)} copy-done((f32[32,2,128]{2,1,0:T(2,128)S(1)}, f32[32,2,128]{2,1,0:T(2,128)}, u32[]{:S(2)}) %copy-start.1) | copy-done | bytes 32792
  2.2 1.1 %shard_map.82 = f32[320,128]{1,0:T(8,128)} custom-call(s32[1,32]{1,0:T(1,128)S(1)} %bitcast.26, s32[64,128]{1,0:T(8,128)S(1)} %bitcast.21, f32[64,128]{1,0:T(8,128)S(1)} %bitcast.22, s32[2,32]{1,0:T(2,128)S(1)} %bitcast.25), custom_call_target="tpu_custom_call" | custom-call | bytes 229760 | tf_op jit(solution)/shard_map/pallas_call | solution.py:21
  3.3 10.2 %all-to-all-start = ((f32[32,5,2,128]{3,2,1,0:T(2,128)}), f32[32,5,2,128]{3,2,1,0:T(2,128)S(1)}, u32[]{:S(2)}, u32[]{:S(2)}) async-start(f32[32,5,2,128]{3,2,1,0:T(2,128)} %bitcast.4), calls=%async_computation | async-start | bytes 327680 | tf_op jit(solution)/shard_map/all_to_all | solution.py:312
  13.5 1.3 %reshape.43.x_ref = f32[168,1024]{1,0:T(8,128)S(1)} reshape(f32[21,2,4,1024]{3,2,1,0:T(4,128)} %bitcast.27) | data formatting | bytes 1376256 | tf_op jit(solution)/shard_map/reshape | solution.py:338
  14.9 9.0 %all-to-all-done = f32[32,5,2,128]{3,2,1,0:T(2,128)S(1)} async-done(((f32[32,5,2,128]{3,2,1,0:T(2,128)}), f32[32,5,2,128]{3,2,1,0:T(2,128)S(1)}, u32[]{:S(2)}, u32[]{:S(2)}) %all-to-all-start) | async-done | bytes 163872 | tf_op jit(solution)/shard_map/all_to_all | solution.py:312
  23.9 1.9 %shard_map.83 = f32[1408,128]{1,0:T(8,128)} custom-call(f32[320,128]{1,0:T(8,128)S(1)} %bitcast.17, f32[168,1024]{1,0:T(8,128)S(1)} %reshape.43.x_ref), custom_call_target="tpu_custom_call" | custom-call | bytes 1572864 | tf_op jit(solution)/shard_map/pallas_call | solution.py:21
  25.8 4.5 %all-to-all-start.1 = ((f32[32,11,4,128]{3,2,1,0:T(4,128)}), f32[32,11,4,128]{3,2,1,0:T(4,128)S(1)}, u32[]{:S(2)}, u32[]{:S(2)}) async-start(f32[32,11,4,128]{3,2,1,0:T(4,128)} %bitcast.7), calls=%async_computation.1 | async-start | bytes 1441792 | tf_op jit(solution)/shard_map/all_to_all | solution.py:312
  30.3 0.0 copy-done.2
  30.3 0.0 copy-done.3
  30.3 0.0 copy-done.4
  30.4 0.4 shard_map.84
  30.8 7.2 %collective-permute-start.1 = (f32[192,128]{1,0:T(8,128)S(1)}, f32[192,128]{1,0:T(8,128)S(1)}, u32[]{:S(2)}, u32[]{:S(2)}) collective-permute-start(f32[192,128]{1,0:T(8,128)S(1)} %get-tuple-element.14.lines_ref), channel_id=1, source_target_pairs={{1,0},{2,1},{3,2},{4,3},{5,4},{6,5},{7,6},{8,7},{9,8},{10,9},{11,1... | collective-permute-start | bytes 294920 | tf_op jit(solution)/shard_map/ppermute | solution.py:318
  38.0 0.0 collective-permute-start
  38.0 2.2 %collective-permute-done.1.lines_right_ref = f32[192,128]{1,0:T(8,128)S(1)} collective-permute-done((f32[192,128]{1,0:T(8,128)S(1)}, f32[192,128]{1,0:T(8,128)S(1)}, u32[]{:S(2)}, u32[]{:S(2)}) %collective-permute-start.1) | collective-permute-done | bytes 98336 | tf_op jit(solution)/shard_map/ppermute | solution.py:318
  40.2 3.0 %collective-permute-done.lines_left_ref = f32[192,128]{1,0:T(8,128)S(1)} collective-permute-done((f32[192,128]{1,0:T(8,128)S(1)}, f32[192,128]{1,0:T(8,128)S(1)}, u32[]{:S(2)}, u32[]{:S(2)}) %collective-permute-start) | collective-permute-done | bytes 98336 | tf_op jit(solution)/shard_map/ppermute | solution.py:318
  43.2 8.2 %all-to-all-done.1 = f32[32,11,4,128]{3,2,1,0:T(4,128)S(1)} async-done(((f32[32,11,4,128]{3,2,1,0:T(4,128)}), f32[32,11,4,128]{3,2,1,0:T(4,128)S(1)}, u32[]{:S(2)}, u32[]{:S(2)}) %all-to-all-start.1) | async-done | bytes 720928 | tf_op jit(solution)/shard_map/all_to_all | solution.py:312
  51.4 1.1 %shard_map.85 = f32[1344,128]{1,0:T(8,128)S(1)} custom-call(f32[1408,128]{1,0:T(8,128)S(1)} %bitcast.15, s32[64,128]{1,0:T(8,128)S(1)} %get-tuple-element.16.low_ref, s32[64,128]{1,0:T(8,128)S(1)} %get-tuple-element.17.up_ref, f32[64,128]{1,0:T(8,128)S(1)} %get-tuple-element.18.wl_ref, f32[64,128]{1,0:T(8,128)S(1)} %get-tuple-element.19.wu_ref), custom_call_target="tpu_custom_call" | custom-call | bytes 1540096 | tf_op jit(solution)/shard_map/pallas_call | solution.py:21
  52.5 5.6 %collective-permute-start.3 = (f32[1344,128]{1,0:T(8,128)S(1)}, f32[1344,128]{1,0:T(8,128)S(1)}, u32[]{:S(2)}, u32[]{:S(2)}) collective-permute-start(f32[1344,128]{1,0:T(8,128)S(1)} %shard_map.85), channel_id=1, source_target_pairs={{1,0},{2,1},{3,2},{4,3},{5,4},{6,5},{7,6},{8,7},{9,8},{10,9},{11,1... | collective-permute-start | bytes 2064392 | tf_op jit(solution)/shard_map/ppermute | solution.py:318
  58.1 0.0 collective-permute-start.2
  58.1 8.5 %collective-permute-done.3 = f32[1344,128]{1,0:T(8,128)S(1)} collective-permute-done((f32[1344,128]{1,0:T(8,128)S(1)}, f32[1344,128]{1,0:T(8,128)S(1)}, u32[]{:S(2)}, u32[]{:S(2)}) %collective-permute-start.3) | collective-permute-done | bytes 688160 | tf_op jit(solution)/shard_map/ppermute | solution.py:318
  66.6 3.7 %collective-permute-done.2 = f32[1344,128]{1,0:T(8,128)S(1)} collective-permute-done((f32[1344,128]{1,0:T(8,128)S(1)}, f32[1344,128]{1,0:T(8,128)S(1)}, u32[]{:S(2)}, u32[]{:S(2)}) %collective-permute-start.2) | collective-permute-done | bytes 688160 | tf_op jit(solution)/shard_map/ppermute | solution.py:318
  70.3 2.6 %shard_map.86 = f32[21,64,128]{2,1,0:T(8,128)} custom-call(f32[21,64,128]{2,1,0:T(8,128)S(1)} %bitcast.16, f32[21,64,128]{2,1,0:T(8,128)S(1)} %bitcast.20, f32[21,64,128]{2,1,0:T(8,128)S(1)} %bitcast.19, f32[192,128]{1,0:T(8,128)S(1)} %get-tuple-element.14.lines_ref, f32[192,128]{1,0:T(8,128)S(1)} %collective-permute-done.lines_left_ref, ...), custom_call_target="tpu_custom_call" | custom-call | bytes 3227648 | tf_op jit(solution)/shard_map/pallas_call | solution.py:21
  (8 shorter events, 0.0 us)
Async XLA Ops:
  0.0 0.7 copy-start.5
  0.0 0.7 copy-start.6
  0.7 0.8 %copy-start = (s32[32,2,128]{2,1,0:T(2,128)S(1)}, s32[32,2,128]{2,1,0:T(2,128)}, u32[]{:S(2)}) copy-start(s32[32,2,128]{2,1,0:T(2,128)} %param.10) | copy-start | bytes 98308
  1.4 0.8 %copy-start.1 = (f32[32,2,128]{2,1,0:T(2,128)S(1)}, f32[32,2,128]{2,1,0:T(2,128)}, u32[]{:S(2)}) copy-start(f32[32,2,128]{2,1,0:T(2,128)} %param.11) | copy-start | bytes 98308
  3.3 20.5 %all-to-all-start = ((f32[32,5,2,128]{3,2,1,0:T(2,128)}), f32[32,5,2,128]{3,2,1,0:T(2,128)S(1)}, u32[]{:S(2)}, u32[]{:S(2)}) async-start(f32[32,5,2,128]{3,2,1,0:T(2,128)} %bitcast.4), calls=%async_computation | async-start | bytes 327680 | tf_op jit(solution)/shard_map/all_to_all | solution.py:312
  25.8 4.5 %copy-start.2 = (f32[32,2,128]{2,1,0:T(2,128)S(1)}, f32[32,2,128]{2,1,0:T(2,128)}, u32[]{:S(2)}) copy-start(f32[32,2,128]{2,1,0:T(2,128)} %param.13) | copy-start | bytes 98308
  25.8 4.5 %copy-start.3 = (f32[32,2,128]{2,1,0:T(2,128)S(1)}, f32[32,2,128]{2,1,0:T(2,128)}, u32[]{:S(2)}) copy-start(f32[32,2,128]{2,1,0:T(2,128)} %param.14) | copy-start | bytes 98308
  25.8 4.5 %copy-start.4 = (f32[21,21]{1,0:T(8,128)S(1)}, f32[21,21]{1,0:T(8,128)}, u32[]{:S(2)}) copy-start(f32[21,21]{1,0:T(8,128)} %mixing_ref.1) | copy-start | bytes 5296
  25.8 25.6 %all-to-all-start.1 = ((f32[32,11,4,128]{3,2,1,0:T(4,128)}), f32[32,11,4,128]{3,2,1,0:T(4,128)S(1)}, u32[]{:S(2)}, u32[]{:S(2)}) async-start(f32[32,11,4,128]{3,2,1,0:T(4,128)} %bitcast.7), calls=%async_computation.1 | async-start | bytes 1441792 | tf_op jit(solution)/shard_map/all_to_all | solution.py:312
  30.8 9.4 %collective-permute-start.1 = (f32[192,128]{1,0:T(8,128)S(1)}, f32[192,128]{1,0:T(8,128)S(1)}, u32[]{:S(2)}, u32[]{:S(2)}) collective-permute-start(f32[192,128]{1,0:T(8,128)S(1)} %get-tuple-element.14.lines_ref), channel_id=1, source_target_pairs={{1,0},{2,1},{3,2},{4,3},{5,4},{6,5},{7,6},{8,7},{9,8},{10,9},{11,1... | collective-permute-start | bytes 294920 | tf_op jit(solution)/shard_map/ppermute | solution.py:318
  38.0 5.3 %collective-permute-start = (f32[192,128]{1,0:T(8,128)S(1)}, f32[192,128]{1,0:T(8,128)S(1)}, u32[]{:S(2)}, u32[]{:S(2)}) collective-permute-start(f32[192,128]{1,0:T(8,128)S(1)} %get-tuple-element.14.lines_ref), channel_id=1, source_target_pairs={{0,1},{1,2},{2,3},{3,4},{4,5},{5,6},{6,7},{7,8},{8,9},{9,10},{10,1... | collective-permute-start | bytes 294920 | tf_op jit(solution)/shard_map/ppermute | solution.py:318
  52.5 14.1 %collective-permute-start.3 = (f32[1344,128]{1,0:T(8,128)S(1)}, f32[1344,128]{1,0:T(8,128)S(1)}, u32[]{:S(2)}, u32[]{:S(2)}) collective-permute-start(f32[1344,128]{1,0:T(8,128)S(1)} %shard_map.85), channel_id=1, source_target_pairs={{1,0},{2,1},{3,2},{4,3},{5,4},{6,5},{7,6},{8,7},{9,8},{10,9},{11,1... | collective-permute-start | bytes 2064392 | tf_op jit(solution)/shard_map/ppermute | solution.py:318
  58.1 12.2 %collective-permute-start.2 = (f32[1344,128]{1,0:T(8,128)S(1)}, f32[1344,128]{1,0:T(8,128)S(1)}, u32[]{:S(2)}, u32[]{:S(2)}) collective-permute-start(f32[1344,128]{1,0:T(8,128)S(1)} %shard_map.85), channel_id=1, source_target_pairs={{0,1},{1,2},{2,3},{3,4},{4,5},{5,6},{6,7},{7,8},{8,9},{9,10},{10,1... | collective-permute-start | bytes 2064392 | tf_op jit(solution)/shard_map/ppermute | solution.py:318

commit v3 on v2

--- a/solution.py
+++ b/solution.py
@@ -14,18 +14,18 @@
 I32 = jnp.int32
 
 
-def call(body, outs, *args, flops=0, space=pltpu.VMEM, scratch=()):
+def call(body, outs, *args, space=pltpu.VMEM, out_space=pltpu.VMEM, scratch=(), room=24):
     touched = sum(a.size * a.dtype.itemsize for a in args) + sum(
-        4 * functools.reduce(lambda x, y: x * y, o.shape) for o in outs
+        o.dtype.itemsize * functools.reduce(lambda x, y: x * y, o.shape) for o in outs
     )
     return pl.pallas_call(
         body,
         out_shape=outs,
         in_specs=[pl.BlockSpec(memory_space=space)] * len(args),
-        out_specs=[pl.BlockSpec(memory_space=pltpu.VMEM)] * len(outs),
+        out_specs=[pl.BlockSpec(memory_space=out_space)] * len(outs),
         scratch_shapes=list(scratch),
-        compiler_params=pltpu.CompilerParams(vmem_limit_bytes=24 * 2**20),
-        cost_estimate=pl.CostEstimate(flops=flops, bytes_accessed=touched, transcendentals=0),
+        compiler_params=pltpu.CompilerParams(vmem_limit_bytes=room * 2**20),
+        cost_estimate=pl.CostEstimate(flops=0, bytes_accessed=touched, transcendentals=0),
     )(*args)
 
 
@@ -97,10 +97,10 @@
     out_ref[pl.ds(9, peers, stride=rows), :] = places
 
 
-STATE_ROWS = 44
-
-
-def state_pack(got_ref, x_ref, out_ref):
+STATE_ROWS = 42
+
+
+def state_pack(got_ref, x_ref, out_hbm, out_ref, sems):
     rows, stencil_rows = STATE_ROWS, STENCIL_ROWS
     peers = out_ref.shape[0] // rows
     total = x_ref.shape[1]
@@ -117,6 +117,8 @@
     both = jnp.concatenate([high, low], axis=0).astype(BF16)
     lines = x_ref.shape[0]
     width = 2 * LANES
+    own_cell = iota((8, LANES), 0) % 4 == iota((8, LANES), 1) // 32
+    copies = []
     for chunk in range(total // width):
         pick = jnp.where(iota((width, total), 0) + chunk * width == nid, 1.0, 0.0).astype(BF16)
         moved = lax.dot_general(
@@ -143,9 +145,19 @@
             rest = y[160:168]
             turned = [rest] + [pltpu.roll(rest, 32 * d, 1) for d in range(1, 4)]
             for q in range(4):
-                out = jnp.where(quarter == 0, turned[(-q) % 4][:4], turned[(1 - q) % 4][4:])
+                out = turned[(-q) % 4]
+                for i in range(1, 4):
+                    out = jnp.where(quarter == i, turned[(i - q) % 4], out)
+                out = jnp.where(own_cell, out, 0.0)
                 at = (first + q) * rows + 40
-                out_ref[at : at + 4, :] = out
+                out_ref[at : at + 1, :] = jnp.sum(out[:4], axis=0, keepdims=True)
+                out_ref[at + 1 : at + 2, :] = jnp.sum(out[4:], axis=0, keepdims=True)
+        done = pl.ds(chunk * 8 * rows, 8 * rows)
+        copy = pltpu.make_async_copy(out_ref.at[done, :], out_hbm.at[done, :], sems.at[chunk])
+        copy.start()
+        copies.append(copy)
+    for copy in copies:
+        copy.wait()
 
 
 def stencil_place(
@@ -231,61 +243,112 @@
             x = lines(8 * group + 4 * half)
             for i in range(4):
                 fit(x[i * stations : (i + 1) * stations], half, 8 * group + 2 * i + half)
-    x = lines(40)
+    lane = iota((stations, LANES), 1)
+    last = [got_ref[pl.ds(40 + half, stations, stride=rows), :] for half in range(2)]
+    cells = []
+    for c in range(4):
+        a, b = [last[half] if c == half else pltpu.roll(last[half], (32 * (half - c)) % LANES, 1) for half in range(2)]
+        cells.append(jnp.where(lane < 32, a, b))
+    x = jnp.concatenate(cells, axis=0).T
     for half in range(2):
         fit(x[half * stations : (half + 1) * stations], half, 40 + half)
 
 
-def sections(m_ref, left_ref, right_ref, lines_ref, lines_left_ref, lines_right_ref, mix_ref, out_ref):
-    nv = m_ref.shape[0]
+def mixed(mix, fields):
+    nv = fields[0].shape[0]
+    x = jnp.concatenate([f.reshape(nv * 8, LANES) for f in fields], axis=1)
+    high, low = split(x)
+    pad = jnp.zeros((mix.shape[1] - 24 * nv, x.shape[1]), F32)
+    stacked = jnp.concatenate([high, low, high, pad], axis=0).astype(BF16)
+    y = jnp.dot(mix, stacked, preferred_element_type=F32)[: nv * 8]
+    return [y[:, i * LANES : (i + 1) * LANES].reshape(nv, 8, LANES) for i in range(len(fields))]
+
+
+def line_of(ref, azim, block):
+    return ref[:, pl.ds(azim * (ref.shape[1] // 2) + 8 * block, 8), :]
+
+
+def coefficients(ref, azim, block):
+    stations = ref.shape[0] // 6
+    return [
+        ref[pl.ds((2 * kind + azim) * stations + 8 * block, 8), :][None] for kind in range(3)
+    ]
+
+
+def slope(field):
+    below = jnp.where(iota(field.shape, 2) == 0, 0.0, pltpu.roll(field, 1, 2))
+    return field - below
+
+
+def inner(m_ref, lines_ref, mix_ref, base_ref, term_ref):
+    mix = mix_ref[...]
     stations = m_ref.shape[1] // 2
-    cell = iota((nv, 8, LANES), 2)
+    for block in range(stations // 8):
+        field = [line_of(m_ref, azim, block) for azim in range(2)]
+        term = mixed(mix, field)
+        base = []
+        for azim in range(2):
+            speed, diffuse, active = coefficients(lines_ref, azim, block)
+            lateral = field[1 - azim] - 2.0 * field[azim]
+            rate = diffuse * lateral - speed * slope(field[azim]) - term[azim]
+            base.append(field[azim] + active * rate)
+        term = mixed(mix, base)
+        for azim in range(2):
+            here = pl.ds(azim * stations + 8 * block, 8)
+            base_ref[:, here, :] = base[azim]
+            term_ref[:, here, :] = term[azim]
+
+
+def sections(
+    m_ref,
+    base_ref,
+    term_ref,
+    left_ref,
+    right_ref,
+    lines_ref,
+    lines_left_ref,
+    lines_right_ref,
+    mix_ref,
+    out_hbm,
+    out_ref,
+    sems,
+):
     mix = mix_ref[...]
-
-    def mixed(fields):
-        x = jnp.concatenate([f.reshape(nv * 8, LANES) for f in fields], axis=1)
-        high, low = split(x)
-        pad = jnp.zeros((8, x.shape[1]), F32)
-        stacked = jnp.concatenate([high, low, high, pad], axis=0).astype(BF16)
-        y = jnp.dot(mix, stacked, preferred_element_type=F32)[: nv * 8]
-        return [
-            y[:, i * LANES : (i + 1) * LANES].reshape(nv, 8, LANES) for i in range(len(fields))
-        ]
-
-    def rate(below, center, above, term, speed, diffuse):
-        lateral = (above + below) - 2.0 * center
-        shifted = jnp.where(cell == 0, 0.0, pltpu.roll(center, 1, 2))
-        return diffuse * lateral - speed * (center - shifted) - term
-
-    def coefficients(ref, azim, block):
-        def one(kind):
-            return ref[pl.ds((2 * kind + azim) * stations + 8 * block, 8), :][None]
-
-        return one(0), one(1), one(2)
-
+    stations = m_ref.shape[1] // 2
+    copies = []
     for block in range(stations // 8):
-        def line(ref, azim):
-            return ref[:, pl.ds(azim * stations + 8 * block, 8), :]
-
-        field = [line(r, a) for r in (left_ref, m_ref, right_ref) for a in range(2)]
-        co = [
+        field = [line_of(m_ref, azim, block) for azim in range(2)]
+        near = [line_of(left_ref, 1, block), line_of(right_ref, 0, block)]
+        far = [line_of(left_ref, 0, block), line_of(right_ref, 1, block)]
+        outer = [
             coefficients(lines_left_ref, 1, block),
-            coefficients(lines_ref, 0, block),
-            coefficients(lines_ref, 1, block),
             coefficients(lines_right_ref, 0, block),
         ]
-        term = mixed(field[1:5])
-        first = []
-        for i in range(4):
-            speed, diffuse, active = co[i]
-            r = rate(field[i], field[i + 1], field[i + 2], term[i], speed, diffuse)
-            first.append(field[i + 1] + active * r)
-        term = mixed(first[1:3])
+        own = [coefficients(lines_ref, azim, block) for azim in range(2)]
+        near_term = mixed(mix, near)
+        first = [
+            line_of(base_ref, azim, block) + (own[azim][2] * own[azim][1]) * near[azim]
+            for azim in range(2)
+        ]
         for azim in range(2):
-            speed, diffuse, active = co[1 + azim]
-            r = rate(first[azim], first[azim + 1], first[azim + 2], term[azim], speed, diffuse)
-            out = 0.5 * ((field[2 + azim] + first[1 + azim]) + active * r)
+            speed, diffuse, active = outer[azim]
+            lateral = (far[azim] + field[azim]) - 2.0 * near[azim]
+            rate = diffuse * lateral - speed * slope(near[azim]) - near_term[azim]
+            outside = near[azim] + active * rate
+            speed, diffuse, active = own[azim]
+            lateral = (outside + first[1 - azim]) - 2.0 * first[azim]
+            term = line_of(term_ref, azim, block) + (active * diffuse) * near_term[azim]
+            rate = diffuse * lateral - speed * slope(first[azim]) - term
+            out = 0.5 * ((field[azim] + first[azim]) + active * rate)
             out_ref[:, pl.ds(azim + 16 * block, 8, stride=2), :] = out
+        done = pl.ds(16 * block, 16)
+        copy = pltpu.make_async_copy(
+            out_ref.at[:, done, :], out_hbm.at[:, done, :], sems.at[block]
+        )
+        copy.start()
+        copies.append(copy)
+    for copy in copies:
+        copy.wait()
 
 
 def shards(
@@ -332,12 +395,20 @@
             pltpu.VMEM((2, stations), I32),
             pltpu.SemaphoreType.DMA((4,)),
         ],
+        room=60,
     )
     got = exchange(packed, STENCIL_ROWS, 2)
 
     x = state_in.transpose(0, 2, 3, 1).reshape(nv * 2 * cells, total)
-    (packed,) = call(state_pack, [shape((peers * STATE_ROWS, LANES), F32)], got, x)
-    got_state = exchange(packed, STATE_ROWS, 4)
+    (packed,) = call(
+        state_pack,
+        [shape((peers * STATE_ROWS, LANES), F32)],
+        got,
+        x,
+        out_space=pltpu.HBM,
+        scratch=[pltpu.VMEM((peers * STATE_ROWS, LANES), F32), pltpu.SemaphoreType.DMA((4,))],
+    )
+    got_state = exchange(packed, STATE_ROWS, 2)
 
     plane = shape((2 * stations, LANES), F32)
     index_plane = shape((2 * stations, LANES), I32)
@@ -367,16 +438,22 @@
     left, right = neighbours(moved)
 
     field = (nv, 2 * stations, LANES)
+    moved = moved.reshape(field)
+    base, term = call(inner, [shape(field, F32)] * 2, moved, lines, mix)
     (out,) = call(
         sections,
         [shape(field, F32)],
-        moved.reshape(field),
+        moved,
+        base,
+        term,
         left.reshape(field),
         right.reshape(field),
         lines,
         lines_left,
         lines_right,
         mix,
+        out_space=pltpu.HBM,
+        scratch=[pltpu.VMEM(field, F32), pltpu.SemaphoreType.DMA((4,))],
     )
     return out.reshape(nv, stations, 2, LANES)
 

time: 73.4 us -> 70.3 us (0.958)
  local copies, waits for them, and re-layouts: 3.54 us -> 1.36 us
  waiting for transfers between devices: 34.6 us -> 32.8 us
  Pallas kernels: 7.11 us -> 7.88 us
    unnamed x14 -> x6, local copies, waits for them, and re-layouts: 2.21 us -> 0.02 us
    ppermute x4, waiting for transfers between devices: 17.4 us -> 16.4 us  [neighbours(): return (lax.ppermute(a, 'azim', up), lax.ppermute(a, 'azim', down))]
    all_to_all x2, waiting for transfers between devices: 17.2 us -> 16.4 us  [exchange(): lax.all_to_all(parts, 'stream', split_axis=0, concat_axis=0, tiled=True)]
    pallas_call x5 -> x6, Pallas kernels: 7.11 us -> 7.88 us  [call(): pl.pallas_call(body, out_shape=outs, in_specs=[pl.BlockSpec(memory_space=...]
  transfers between devices with their start and end apart: 6 -> 6, of which waited for: 6 -> 6; matrix products, arithmetic and copies ran while one was open for 2% -> 2% of each run, Pallas kernels for 1% -> 2%
where the time goes in v3:
time: 70.3 us; the launch traced here: 69.8 us
  waiting for transfers between devices  32.8 us (47%)
  starting transfers between devices  27.7 us (39%)
  Pallas kernels  7.88 us (11%)
  local copies, waits for them, and re-layouts  1.36 us (2%)
    ppermute x4, waiting for transfers between devices, neighbours(): return (lax.ppermute(a, 'azim', up), lax.ppermute(a, 'azim', down))  16.4 us
    all_to_all x2, waiting for transfers between devices, exchange(): lax.all_to_all(parts, 'stream', split_axis=0, concat_axis=0, tiled=True)  16.4 us
    all_to_all x2, starting transfers between devices, exchange(): lax.all_to_all(parts, 'stream', split_axis=0, concat_axis=0, tiled=True)  14.7 us
    ppermute x4, starting transfers between devices, neighbours(): return (lax.ppermute(a, 'azim', up), lax.ppermute(a, 'azim', down))  13 us
    pallas_call x6, Pallas kernels, call(): pl.pallas_call(body, out_shape=outs, in_specs=[pl.BlockSpec(memory_space=...  7.88 us
  transfers between devices with their start and end apart: 6, of which 6 were waited for; matrix products, arithmetic and copies ran while one was open for 2% of the time, Pallas kernels for 2%

profile of v3, /device:TPU:8, one launch (start us, length us, event | category | flops | bytes accessed | tf_op | source)
XLA Modules:
  0.0 69.8 jit_solution(14512229227186241092)
XLA Ops:
  0.0 1.9 %shard_map.82 = f32[320,128]{1,0:T(8,128)} custom-call(s32[1,32]{1,0:T(1,128)} %bitcast.29, s32[64,128]{1,0:T(8,128)} %bitcast.26, f32[64,128]{1,0:T(8,128)} %bitcast.27, s32[2,32]{1,0:T(2,128)} %bitcast.28), custom_call_target="tpu_custom_call" | custom-call | bytes 229760 | tf_op jit(solution)/shard_map/pallas_call | solution.py:21
  1.9 10.2 %all-to-all-start = ((f32[32,5,2,128]{3,2,1,0:T(2,128)}), f32[32,5,2,128]{3,2,1,0:T(2,128)S(1)}, u32[]{:S(2)}, u32[]{:S(2)}) async-start(f32[32,5,2,128]{3,2,1,0:T(2,128)} %bitcast.25), calls=%async_computation | async-start | bytes 327680 | tf_op jit(solution)/shard_map/all_to_all | solution.py:375
  12.0 1.3 %reshape.43.x_ref = f32[168,1024]{1,0:T(8,128)S(1)} reshape(f32[21,2,4,1024]{3,2,1,0:T(4,128)} %bitcast.24) | data formatting | bytes 1376256 | tf_op jit(solution)/shard_map/reshape | solution.py:402
  13.4 9.0 %all-to-all-done = f32[32,5,2,128]{3,2,1,0:T(2,128)S(1)} async-done(((f32[32,5,2,128]{3,2,1,0:T(2,128)}), f32[32,5,2,128]{3,2,1,0:T(2,128)S(1)}, u32[]{:S(2)}, u32[]{:S(2)}) %all-to-all-start) | async-done | bytes 163872 | tf_op jit(solution)/shard_map/all_to_all | solution.py:375
  22.4 2.0 %shard_map.83 = f32[1344,128]{1,0:T(8,128)} custom-call(f32[320,128]{1,0:T(8,128)S(1)} %bitcast.18, f32[168,1024]{1,0:T(8,128)S(1)} %reshape.43.x_ref), custom_call_target="tpu_custom_call" | custom-call | bytes 1540096 | tf_op jit(solution)/shard_map/pallas_call | solution.py:21
  24.4 0.0 copy-start
  24.4 0.0 copy-start.1
  24.4 0.0 copy-start.2
  24.4 4.5 %all-to-all-start.1 = ((f32[32,21,2,128]{3,2,1,0:T(2,128)}), f32[32,21,2,128]{3,2,1,0:T(2,128)S(1)}, u32[]{:S(2)}, u32[]{:S(2)}) async-start(f32[32,21,2,128]{3,2,1,0:T(2,128)} %bitcast.7), calls=%async_computation.1 | async-start | bytes 1376256 | tf_op jit(solution)/shard_map/all_to_all | solution.py:375
  29.0 0.0 copy-done
  29.0 0.0 copy-done.1
  29.0 0.4 shard_map.84
  29.4 7.2 %collective-permute-start.1 = (f32[192,128]{1,0:T(8,128)S(1)}, f32[192,128]{1,0:T(8,128)S(1)}, u32[]{:S(2)}, u32[]{:S(2)}) collective-permute-start(f32[192,128]{1,0:T(8,128)S(1)} %get-tuple-element.16.lines_ref), channel_id=1, source_target_pairs={{1,0},{2,1},{3,2},{4,3},{5,4},{6,5},{7,6},{8,7},{9,8},{10,9},{11,1... | collective-permute-start | bytes 294920 | tf_op jit(solution)/shard_map/ppermute | solution.py:381
  36.6 0.0 collective-permute-start
  36.6 2.2 %collective-permute-done.1.lines_right_ref = f32[192,128]{1,0:T(8,128)S(1)} collective-permute-done((f32[192,128]{1,0:T(8,128)S(1)}, f32[192,128]{1,0:T(8,128)S(1)}, u32[]{:S(2)}, u32[]{:S(2)}) %collective-permute-start.1) | collective-permute-done | bytes 98336 | tf_op jit(solution)/shard_map/ppermute | solution.py:381
  38.8 3.0 %collective-permute-done.lines_left_ref = f32[192,128]{1,0:T(8,128)S(1)} collective-permute-done((f32[192,128]{1,0:T(8,128)S(1)}, f32[192,128]{1,0:T(8,128)S(1)}, u32[]{:S(2)}, u32[]{:S(2)}) %collective-permute-start) | collective-permute-done | bytes 98336 | tf_op jit(solution)/shard_map/ppermute | solution.py:381
  41.9 7.4 %all-to-all-done.1 = f32[32,21,2,128]{3,2,1,0:T(2,128)S(1)} async-done(((f32[32,21,2,128]{3,2,1,0:T(2,128)}), f32[32,21,2,128]{3,2,1,0:T(2,128)S(1)}, u32[]{:S(2)}, u32[]{:S(2)}) %all-to-all-start.1) | async-done | bytes 688160 | tf_op jit(solution)/shard_map/all_to_all | solution.py:375
  49.2 1.2 %shard_map.85 = f32[1344,128]{1,0:T(8,128)S(1)} custom-call(f32[1344,128]{1,0:T(8,128)S(1)} %bitcast.17, s32[64,128]{1,0:T(8,128)S(1)} %get-tuple-element.18.low_ref, s32[64,128]{1,0:T(8,128)S(1)} %get-tuple-element.19.up_ref, f32[64,128]{1,0:T(8,128)S(1)} %get-tuple-element.20.wl_ref, f32[64,128]{1,0:T(8,128)S(1)} %get-tuple-element.21.wu_ref), custom_call_target="tpu_custom_call" | custom-call | bytes 1507328 | tf_op jit(solution)/shard_map/pallas_call | solution.py:21
  50.4 5.8 %collective-permute-start.3 = (f32[1344,128]{1,0:T(8,128)S(1)}, f32[1344,128]{1,0:T(8,128)S(1)}, u32[]{:S(2)}, u32[]{:S(2)}) collective-permute-start(f32[1344,128]{1,0:T(8,128)S(1)} %shard_map.85), channel_id=1, source_target_pairs={{1,0},{2,1},{3,2},{4,3},{5,4},{6,5},{7,6},{8,7},{9,8},{10,9},{11,1... | collective-permute-start | bytes 2064392 | tf_op jit(solution)/shard_map/ppermute | solution.py:381
  56.2 0.0 collective-permute-start.2
  56.2 0.8 %shard_map.86 = (f32[21,64,128]{2,1,0:T(8,128)S(1)}, f32[21,64,128]{2,1,0:T(8,128)S(1)}) custom-call(f32[21,64,128]{2,1,0:T(8,128)S(1)} %bitcast.15, f32[192,128]{1,0:T(8,128)S(1)} %get-tuple-element.16.lines_ref, bf16[176,512]{1,0:T(8,128)(2,1)S(1)} %get-tuple-element.22.mix_ref), custom_call_target="tpu_custom_call" | custom-call | bytes 2342912 | tf_op jit(solution)/shard_map/pallas_call | solution.py:21
  57.0 7.7 %collective-permute-done.3 = f32[1344,128]{1,0:T(8,128)S(1)} collective-permute-done((f32[1344,128]{1,0:T(8,128)S(1)}, f32[1344,128]{1,0:T(8,128)S(1)}, u32[]{:S(2)}, u32[]{:S(2)}) %collective-permute-start.3) | collective-permute-done | bytes 688160 | tf_op jit(solution)/shard_map/ppermute | solution.py:381
  64.7 3.5 %collective-permute-done.2 = f32[1344,128]{1,0:T(8,128)S(1)} collective-permute-done((f32[1344,128]{1,0:T(8,128)S(1)}, f32[1344,128]{1,0:T(8,128)S(1)}, u32[]{:S(2)}, u32[]{:S(2)}) %collective-permute-start.2) | collective-permute-done | bytes 688160 | tf_op jit(solution)/shard_map/ppermute | solution.py:381
  68.2 1.7 %shard_map.87 = f32[21,64,128]{2,1,0:T(8,128)} custom-call(f32[21,64,128]{2,1,0:T(8,128)S(1)} %bitcast.16, f32[21,64,128]{2,1,0:T(8,128)S(1)} %get-tuple-element.23.base_ref, f32[21,64,128]{2,1,0:T(8,128)S(1)} %get-tuple-element.24.term_ref, f32[21,64,128]{2,1,0:T(8,128)S(1)} %bitcast.21, f32[21,64,128]{2,1,0:T(8,128)S(1)} %bitcast.20, ...), custom_call_target="tpu_custom_call" | custom-call | bytes 4603904 | tf_op jit(solution)/shard_map/pallas_call | solution.py:21
  (1 shorter events, 0.0 us)
Async XLA Ops:
  1.9 20.5 %all-to-all-start = ((f32[32,5,2,128]{3,2,1,0:T(2,128)}), f32[32,5,2,128]{3,2,1,0:T(2,128)S(1)}, u32[]{:S(2)}, u32[]{:S(2)}) async-start(f32[32,5,2,128]{3,2,1,0:T(2,128)} %bitcast.25), calls=%async_computation | async-start | bytes 327680 | tf_op jit(solution)/shard_map/all_to_all | solution.py:375
  24.4 4.6 %copy-start = (f32[32,2,128]{2,1,0:T(2,128)S(1)}, f32[32,2,128]{2,1,0:T(2,128)}, u32[]{:S(2)}) copy-start(f32[32,2,128]{2,1,0:T(2,128)} %param.13) | copy-start | bytes 98308
  24.4 4.6 %copy-start.1 = (f32[32,2,128]{2,1,0:T(2,128)S(1)}, f32[32,2,128]{2,1,0:T(2,128)}, u32[]{:S(2)}) copy-start(f32[32,2,128]{2,1,0:T(2,128)} %param.14) | copy-start | bytes 98308
  24.4 4.6 %copy-start.2 = (f32[21,21]{1,0:T(8,128)S(1)}, f32[21,21]{1,0:T(8,128)}, u32[]{:S(2)}) copy-start(f32[21,21]{1,0:T(8,128)} %mixing_ref.1) | copy-start | bytes 5296
  24.4 24.8 %all-to-all-start.1 = ((f32[32,21,2,128]{3,2,1,0:T(2,128)}), f32[32,21,2,128]{3,2,1,0:T(2,128)S(1)}, u32[]{:S(2)}, u32[]{:S(2)}) async-start(f32[32,21,2,128]{3,2,1,0:T(2,128)} %bitcast.7), calls=%async_computation.1 | async-start | bytes 1376256 | tf_op jit(solution)/shard_map/all_to_all | solution.py:375
  29.4 9.4 %collective-permute-start.1 = (f32[192,128]{1,0:T(8,128)S(1)}, f32[192,128]{1,0:T(8,128)S(1)}, u32[]{:S(2)}, u32[]{:S(2)}) collective-permute-start(f32[192,128]{1,0:T(8,128)S(1)} %get-tuple-element.16.lines_ref), channel_id=1, source_target_pairs={{1,0},{2,1},{3,2},{4,3},{5,4},{6,5},{7,6},{8,7},{9,8},{10,9},{11,1... | collective-permute-start | bytes 294920 | tf_op jit(solution)/shard_map/ppermute | solution.py:381
  36.6 5.3 %collective-permute-start = (f32[192,128]{1,0:T(8,128)S(1)}, f32[192,128]{1,0:T(8,128)S(1)}, u32[]{:S(2)}, u32[]{:S(2)}) collective-permute-start(f32[192,128]{1,0:T(8,128)S(1)} %get-tuple-element.16.lines_ref), channel_id=1, source_target_pairs={{0,1},{1,2},{2,3},{3,4},{4,5},{5,6},{6,7},{7,8},{8,9},{9,10},{10,1... | collective-permute-start | bytes 294920 | tf_op jit(solution)/shard_map/ppermute | solution.py:381
  50.4 14.3 %collective-permute-start.3 = (f32[1344,128]{1,0:T(8,128)S(1)}, f32[1344,128]{1,0:T(8,128)S(1)}, u32[]{:S(2)}, u32[]{:S(2)}) collective-permute-start(f32[1344,128]{1,0:T(8,128)S(1)} %shard_map.85), channel_id=1, source_target_pairs={{1,0},{2,1},{3,2},{4,3},{5,4},{6,5},{7,6},{8,7},{9,8},{10,9},{11,1... | collective-permute-start | bytes 2064392 | tf_op jit(solution)/shard_map/ppermute | solution.py:381
  56.2 12.0 %collective-permute-start.2 = (f32[1344,128]{1,0:T(8,128)S(1)}, f32[1344,128]{1,0:T(8,128)S(1)}, u32[]{:S(2)}, u32[]{:S(2)}) collective-permute-start(f32[1344,128]{1,0:T(8,128)S(1)} %shard_map.85), channel_id=1, source_target_pairs={{0,1},{1,2},{2,3},{3,4},{4,5},{5,6},{6,7},{7,8},{8,9},{9,10},{10,1... | collective-permute-start | bytes 2064392 | tf_op jit(solution)/shard_map/ppermute | solution.py:381

commit v4 on v3

--- a/solution.py
+++ b/solution.py
@@ -303,8 +303,8 @@
     m_ref,
     base_ref,
     term_ref,
+    right_ref,
     left_ref,
-    right_ref,
     lines_ref,
     lines_left_ref,
     lines_right_ref,
@@ -446,8 +446,8 @@
         moved,
         base,
         term,
+        right.reshape(field),
         left.reshape(field),
-        right.reshape(field),
         lines,
         lines_left,
         lines_right,

time: 70.3 us -> 68 us (0.967)
  the two profiles are of different devices: /device:TPU:8 before, /device:TPU:193 now
where the time goes in v4:
time: 68 us; the launch traced here: 67.6 us
  waiting for transfers between devices  30.6 us (45%)
  starting transfers between devices  27.6 us (41%)
  Pallas kernels  7.9 us (12%)
  local copies, waits for them, and re-layouts  1.36 us (2%)
    all_to_all x2, waiting for transfers between devices, exchange(): lax.all_to_all(parts, 'stream', split_axis=0, concat_axis=0, tiled=True)  17.3 us
    all_to_all x2, starting transfers between devices, exchange(): lax.all_to_all(parts, 'stream', split_axis=0, concat_axis=0, tiled=True)  14.5 us
    ppermute x4, waiting for transfers between devices, neighbours(): return (lax.ppermute(a, 'azim', up), lax.ppermute(a, 'azim', down))  13.3 us
    ppermute x4, starting transfers between devices, neighbours(): return (lax.ppermute(a, 'azim', up), lax.ppermute(a, 'azim', down))  13.1 us
    pallas_call x6, Pallas kernels, call(): pl.pallas_call(body, out_shape=outs, in_specs=[pl.BlockSpec(memory_space=...  7.9 us
  transfers between devices with their start and end apart: 6, of which 5 were waited for; matrix products, arithmetic and copies ran while one was open for 2% of the time, Pallas kernels for 2%

profile of v4, /device:TPU:193, one launch (start us, length us, event | category | flops | bytes accessed | tf_op | source)
XLA Modules:
  0.0 67.6 jit_solution(12377161248096300044)
XLA Ops:
  0.0 1.9 %shard_map.82 = f32[320,128]{1,0:T(8,128)} custom-call(s32[1,32]{1,0:T(1,128)} %bitcast.29, s32[64,128]{1,0:T(8,128)} %bitcast.26, f32[64,128]{1,0:T(8,128)} %bitcast.27, s32[2,32]{1,0:T(2,128)} %bitcast.28), custom_call_target="tpu_custom_call" | custom-call | bytes 229760 | tf_op jit(solution)/shard_map/pallas_call | solution.py:21
  1.9 9.7 %all-to-all-start = ((f32[32,5,2,128]{3,2,1,0:T(2,128)}), f32[32,5,2,128]{3,2,1,0:T(2,128)S(1)}, u32[]{:S(2)}, u32[]{:S(2)}) async-start(f32[32,5,2,128]{3,2,1,0:T(2,128)} %bitcast.25), calls=%async_computation | async-start | bytes 327680 | tf_op jit(solution)/shard_map/all_to_all | solution.py:375
  11.6 1.3 %reshape.43.x_ref = f32[168,1024]{1,0:T(8,128)S(1)} reshape(f32[21,2,4,1024]{3,2,1,0:T(4,128)} %bitcast.24) | data formatting | bytes 1376256 | tf_op jit(solution)/shard_map/reshape | solution.py:402
  12.9 8.0 %all-to-all-done = f32[32,5,2,128]{3,2,1,0:T(2,128)S(1)} async-done(((f32[32,5,2,128]{3,2,1,0:T(2,128)}), f32[32,5,2,128]{3,2,1,0:T(2,128)S(1)}, u32[]{:S(2)}, u32[]{:S(2)}) %all-to-all-start) | async-done | bytes 163872 | tf_op jit(solution)/shard_map/all_to_all | solution.py:375
  20.9 2.0 %shard_map.83 = f32[1344,128]{1,0:T(8,128)} custom-call(f32[320,128]{1,0:T(8,128)S(1)} %bitcast.18, f32[168,1024]{1,0:T(8,128)S(1)} %reshape.43.x_ref), custom_call_target="tpu_custom_call" | custom-call | bytes 1540096 | tf_op jit(solution)/shard_map/pallas_call | solution.py:21
  22.9 0.0 copy-start
  22.9 0.0 copy-start.1
  22.9 0.0 copy-start.2
  22.9 4.8 %all-to-all-start.1 = ((f32[32,21,2,128]{3,2,1,0:T(2,128)}), f32[32,21,2,128]{3,2,1,0:T(2,128)S(1)}, u32[]{:S(2)}, u32[]{:S(2)}) async-start(f32[32,21,2,128]{3,2,1,0:T(2,128)} %bitcast.7), calls=%async_computation.1 | async-start | bytes 1376256 | tf_op jit(solution)/shard_map/all_to_all | solution.py:375
  27.7 0.0 copy-done
  27.7 0.0 copy-done.1
  27.8 0.4 shard_map.84
  28.2 1.7 %collective-permute-start.1 = (f32[192,128]{1,0:T(8,128)S(1)}, f32[192,128]{1,0:T(8,128)S(1)}, u32[]{:S(2)}, u32[]{:S(2)}) collective-permute-start(f32[192,128]{1,0:T(8,128)S(1)} %get-tuple-element.16.lines_ref), channel_id=1, source_target_pairs={{1,0},{2,1},{3,2},{4,3},{5,4},{6,5},{7,6},{8,7},{9,8},{10,9},{11,1... | collective-permute-start | bytes 294920 | tf_op jit(solution)/shard_map/ppermute | solution.py:381
  29.9 3.2 %collective-permute-start = (f32[192,128]{1,0:T(8,128)S(1)}, f32[192,128]{1,0:T(8,128)S(1)}, u32[]{:S(2)}, u32[]{:S(2)}) collective-permute-start(f32[192,128]{1,0:T(8,128)S(1)} %get-tuple-element.16.lines_ref), channel_id=1, source_target_pairs={{0,1},{1,2},{2,3},{3,4},{4,5},{5,6},{6,7},{7,8},{8,9},{9,10},{10,1... | collective-permute-start | bytes 294920 | tf_op jit(solution)/shard_map/ppermute | solution.py:381
  33.1 2.6 %collective-permute-done.1.lines_right_ref = f32[192,128]{1,0:T(8,128)S(1)} collective-permute-done((f32[192,128]{1,0:T(8,128)S(1)}, f32[192,128]{1,0:T(8,128)S(1)}, u32[]{:S(2)}, u32[]{:S(2)}) %collective-permute-start.1) | collective-permute-done | bytes 98336 | tf_op jit(solution)/shard_map/ppermute | solution.py:381
  35.7 0.0 collective-permute-done.lines_left_ref
  35.7 9.3 %all-to-all-done.1 = f32[32,21,2,128]{3,2,1,0:T(2,128)S(1)} async-done(((f32[32,21,2,128]{3,2,1,0:T(2,128)}), f32[32,21,2,128]{3,2,1,0:T(2,128)S(1)}, u32[]{:S(2)}, u32[]{:S(2)}) %all-to-all-start.1) | async-done | bytes 688160 | tf_op jit(solution)/shard_map/all_to_all | solution.py:375
  45.0 1.2 %shard_map.85 = f32[1344,128]{1,0:T(8,128)S(1)} custom-call(f32[1344,128]{1,0:T(8,128)S(1)} %bitcast.17, s32[64,128]{1,0:T(8,128)S(1)} %get-tuple-element.18.low_ref, s32[64,128]{1,0:T(8,128)S(1)} %get-tuple-element.19.up_ref, f32[64,128]{1,0:T(8,128)S(1)} %get-tuple-element.20.wl_ref, f32[64,128]{1,0:T(8,128)S(1)} %get-tuple-element.21.wu_ref), custom_call_target="tpu_custom_call" | custom-call | bytes 1507328 | tf_op jit(solution)/shard_map/pallas_call | solution.py:21
  46.1 8.2 %collective-permute-start.3 = (f32[1344,128]{1,0:T(8,128)S(1)}, f32[1344,128]{1,0:T(8,128)S(1)}, u32[]{:S(2)}, u32[]{:S(2)}) collective-permute-start(f32[1344,128]{1,0:T(8,128)S(1)} %shard_map.85), channel_id=1, source_target_pairs={{0,1},{1,2},{2,3},{3,4},{4,5},{5,6},{6,7},{7,8},{8,9},{9,10},{10,1... | collective-permute-start | bytes 2064392 | tf_op jit(solution)/shard_map/ppermute | solution.py:381
  54.3 0.0 collective-permute-start.2
  54.4 0.8 %shard_map.86 = (f32[21,64,128]{2,1,0:T(8,128)S(1)}, f32[21,64,128]{2,1,0:T(8,128)S(1)}) custom-call(f32[21,64,128]{2,1,0:T(8,128)S(1)} %bitcast.15, f32[192,128]{1,0:T(8,128)S(1)} %get-tuple-element.16.lines_ref, bf16[176,512]{1,0:T(8,128)(2,1)S(1)} %get-tuple-element.22.mix_ref), custom_call_target="tpu_custom_call" | custom-call | bytes 2342912 | tf_op jit(solution)/shard_map/pallas_call | solution.py:21
  55.1 7.1 %collective-permute-done.3 = f32[1344,128]{1,0:T(8,128)S(1)} collective-permute-done((f32[1344,128]{1,0:T(8,128)S(1)}, f32[1344,128]{1,0:T(8,128)S(1)}, u32[]{:S(2)}, u32[]{:S(2)}) %collective-permute-start.3) | collective-permute-done | bytes 688160 | tf_op jit(solution)/shard_map/ppermute | solution.py:381
  62.2 3.7 %collective-permute-done.2 = f32[1344,128]{1,0:T(8,128)S(1)} collective-permute-done((f32[1344,128]{1,0:T(8,128)S(1)}, f32[1344,128]{1,0:T(8,128)S(1)}, u32[]{:S(2)}, u32[]{:S(2)}) %collective-permute-start.2) | collective-permute-done | bytes 688160 | tf_op jit(solution)/shard_map/ppermute | solution.py:381
  65.9 1.7 %shard_map.87 = f32[21,64,128]{2,1,0:T(8,128)} custom-call(f32[21,64,128]{2,1,0:T(8,128)S(1)} %bitcast.16, f32[21,64,128]{2,1,0:T(8,128)S(1)} %get-tuple-element.23.base_ref, f32[21,64,128]{2,1,0:T(8,128)S(1)} %get-tuple-element.24.term_ref, f32[21,64,128]{2,1,0:T(8,128)S(1)} %bitcast.21, f32[21,64,128]{2,1,0:T(8,128)S(1)} %bitcast.20, ...), custom_call_target="tpu_custom_call" | custom-call | bytes 4603904 | tf_op jit(solution)/shard_map/pallas_call | solution.py:21
  (1 shorter events, 0.0 us)
Async XLA Ops:
  1.9 19.1 %all-to-all-start = ((f32[32,5,2,128]{3,2,1,0:T(2,128)}), f32[32,5,2,128]{3,2,1,0:T(2,128)S(1)}, u32[]{:S(2)}, u32[]{:S(2)}) async-start(f32[32,5,2,128]{3,2,1,0:T(2,128)} %bitcast.25), calls=%async_computation | async-start | bytes 327680 | tf_op jit(solution)/shard_map/all_to_all | solution.py:375
  22.9 4.8 %copy-start = (f32[32,2,128]{2,1,0:T(2,128)S(1)}, f32[32,2,128]{2,1,0:T(2,128)}, u32[]{:S(2)}) copy-start(f32[32,2,128]{2,1,0:T(2,128)} %param.13) | copy-start | bytes 98308
  22.9 4.8 %copy-start.1 = (f32[32,2,128]{2,1,0:T(2,128)S(1)}, f32[32,2,128]{2,1,0:T(2,128)}, u32[]{:S(2)}) copy-start(f32[32,2,128]{2,1,0:T(2,128)} %param.14) | copy-start | bytes 98308
  22.9 4.8 %copy-start.2 = (f32[21,21]{1,0:T(8,128)S(1)}, f32[21,21]{1,0:T(8,128)}, u32[]{:S(2)}) copy-start(f32[21,21]{1,0:T(8,128)} %mixing_ref.1) | copy-start | bytes 5296
  22.9 22.0 %all-to-all-start.1 = ((f32[32,21,2,128]{3,2,1,0:T(2,128)}), f32[32,21,2,128]{3,2,1,0:T(2,128)S(1)}, u32[]{:S(2)}, u32[]{:S(2)}) async-start(f32[32,21,2,128]{3,2,1,0:T(2,128)} %bitcast.7), calls=%async_computation.1 | async-start | bytes 1376256 | tf_op jit(solution)/shard_map/all_to_all | solution.py:375
  28.2 7.5 %collective-permute-start.1 = (f32[192,128]{1,0:T(8,128)S(1)}, f32[192,128]{1,0:T(8,128)S(1)}, u32[]{:S(2)}, u32[]{:S(2)}) collective-permute-start(f32[192,128]{1,0:T(8,128)S(1)} %get-tuple-element.16.lines_ref), channel_id=1, source_target_pairs={{1,0},{2,1},{3,2},{4,3},{5,4},{6,5},{7,6},{8,7},{9,8},{10,9},{11,1... | collective-permute-start | bytes 294920 | tf_op jit(solution)/shard_map/ppermute | solution.py:381
  29.9 5.8 %collective-permute-start = (f32[192,128]{1,0:T(8,128)S(1)}, f32[192,128]{1,0:T(8,128)S(1)}, u32[]{:S(2)}, u32[]{:S(2)}) collective-permute-start(f32[192,128]{1,0:T(8,128)S(1)} %get-tuple-element.16.lines_ref), channel_id=1, source_target_pairs={{0,1},{1,2},{2,3},{3,4},{4,5},{5,6},{6,7},{7,8},{8,9},{9,10},{10,1... | collective-permute-start | bytes 294920 | tf_op jit(solution)/shard_map/ppermute | solution.py:381
  46.1 16.1 %collective-permute-start.3 = (f32[1344,128]{1,0:T(8,128)S(1)}, f32[1344,128]{1,0:T(8,128)S(1)}, u32[]{:S(2)}, u32[]{:S(2)}) collective-permute-start(f32[1344,128]{1,0:T(8,128)S(1)} %shard_map.85), channel_id=1, source_target_pairs={{0,1},{1,2},{2,3},{3,4},{4,5},{5,6},{6,7},{7,8},{8,9},{9,10},{10,1... | collective-permute-start | bytes 2064392 | tf_op jit(solution)/shard_map/ppermute | solution.py:381
  54.3 11.6 %collective-permute-start.2 = (f32[1344,128]{1,0:T(8,128)S(1)}, f32[1344,128]{1,0:T(8,128)S(1)}, u32[]{:S(2)}, u32[]{:S(2)}) collective-permute-start(f32[1344,128]{1,0:T(8,128)S(1)} %shard_map.85), channel_id=1, source_target_pairs={{1,0},{2,1},{3,2},{4,3},{5,4},{6,5},{7,6},{8,7},{9,8},{10,9},{11,1... | collective-permute-start | bytes 2064392 | tf_op jit(solution)/shard_map/ppermute | solution.py:381

commit v5 on v4

--- a/solution.py
+++ b/solution.py
@@ -8,6 +8,7 @@
 
 LANES = 128
 SLOTS = 2
+MARK = 1e30
 HIGHEST = lax.Precision.HIGHEST
 F32 = jnp.float32
 BF16 = jnp.bfloat16
@@ -97,10 +98,43 @@
     out_ref[pl.ds(9, peers, stride=rows), :] = places
 
 
+def stencil_place(got_ref, low_ref, up_ref, wl_ref, wu_ref):
+    rows = STENCIL_ROWS
+    peers = got_ref.shape[0] // rows
+    stations = low_ref.shape[0] // 2
+    spots = got_ref[pl.ds(9, peers, stride=rows), :].T
+    place = iota((stations, peers), 0).astype(F32)
+    picks = [jnp.where(spots[slot : slot + 1, :] == place, 1.0, 0.0) for slot in range(SLOTS)]
+    for azim in range(2):
+        idx = jnp.zeros((stations, LANES), F32)
+        weight = jnp.zeros((stations, LANES), F32)
+        for slot in range(SLOTS):
+            at = rows_of(slot, azim)
+            idx += jnp.dot(
+                picks[slot],
+                got_ref[pl.ds(at, peers, stride=rows), :],
+                preferred_element_type=F32,
+            )
+            weight += jnp.dot(
+                picks[slot],
+                got_ref[pl.ds(4 + at, peers, stride=rows), :],
+                preferred_element_type=F32,
+                precision=HIGHEST,
+            )
+        live = idx >= 0.0
+        low = jnp.where(live, idx, 0.0).astype(I32)
+        up = low + 1
+        here = pl.ds(azim * stations, stations)
+        low_ref[here, :] = (low % 4) * 32 + low // 4
+        up_ref[here, :] = (up % 4) * 32 + up // 4
+        wl_ref[here, :] = jnp.where(live, 1.0 - weight, 0.0)
+        wu_ref[here, :] = jnp.where(live, weight, 0.0)
+
+
 STATE_ROWS = 42
 
 
-def state_pack(got_ref, x_ref, out_hbm, out_ref, sems):
+def state_pack(got_ref, x_ref, out_ref, low_ref, up_ref, wl_ref, wu_ref):
     rows, stencil_rows = STATE_ROWS, STENCIL_ROWS
     peers = out_ref.shape[0] // rows
     total = x_ref.shape[1]
@@ -118,7 +152,6 @@
     lines = x_ref.shape[0]
     width = 2 * LANES
     own_cell = iota((8, LANES), 0) % 4 == iota((8, LANES), 1) // 32
-    copies = []
     for chunk in range(total // width):
         pick = jnp.where(iota((width, total), 0) + chunk * width == nid, 1.0, 0.0).astype(BF16)
         moved = lax.dot_general(
@@ -152,17 +185,15 @@
                 at = (first + q) * rows + 40
                 out_ref[at : at + 1, :] = jnp.sum(out[:4], axis=0, keepdims=True)
                 out_ref[at + 1 : at + 2, :] = jnp.sum(out[4:], axis=0, keepdims=True)
-        done = pl.ds(chunk * 8 * rows, 8 * rows)
-        copy = pltpu.make_async_copy(out_ref.at[done, :], out_hbm.at[done, :], sems.at[chunk])
-        copy.start()
-        copies.append(copy)
-    for copy in copies:
-        copy.wait()
-
-
-def stencil_place(
-    got_ref, speed_ref, diffuse_ref, mixing_ref, low_ref, up_ref, wl_ref, wu_ref, lines_ref, mix_ref
-):
+    stencil_place(got_ref, low_ref, up_ref, wl_ref, wu_ref)
+
+
+def line_setup(speed_ref, diffuse_ref, mixing_ref, lines_ref, mix_ref):
+    stations = speed_ref.shape[0] // 2
+    for azim in range(2):
+        here = pl.ds(azim, stations, stride=2)
+        lines_ref[pl.ds(azim * stations, stations), :] = speed_ref[here, :]
+        lines_ref[pl.ds((2 + azim) * stations, stations), :] = diffuse_ref[here, :]
     nv = mixing_ref.shape[0]
     high, low = split(0.25 * mixing_ref[...])
     by_row = (iota((mix_ref.shape[0], nv), 0) // 8 == iota((mix_ref.shape[0], nv), 1)).astype(F32)
@@ -179,43 +210,6 @@
     both = [jnp.where(same, part, 0.0) for part in both]
     rest = jnp.zeros((mix_ref.shape[0], mix_ref.shape[1] - 24 * nv), F32)
     mix_ref[...] = jnp.concatenate([both[0], both[0], both[1], rest], axis=1).astype(BF16)
-    rows = STENCIL_ROWS
-    peers = got_ref.shape[0] // rows
-    stations = low_ref.shape[0] // 2
-    spots = got_ref[pl.ds(9, peers, stride=rows), :].T
-    place = iota((stations, peers), 0).astype(F32)
-    picks = [jnp.where(spots[slot : slot + 1, :] == place, 1.0, 0.0) for slot in range(SLOTS)]
-    for azim in range(2):
-        idx = jnp.zeros((stations, LANES), F32)
-        weight = jnp.zeros((stations, LANES), F32)
-        for slot in range(SLOTS):
-            at = rows_of(slot, azim)
-            idx += jnp.dot(
-                picks[slot],
-                got_ref[pl.ds(at, peers, stride=rows), :],
-                preferred_element_type=F32,
-            )
-            weight += jnp.dot(
-                picks[slot],
-                got_ref[pl.ds(4 + at, peers, stride=rows), :],
-                preferred_element_type=F32,
-                precision=HIGHEST,
-            )
-        live = idx >= 0.0
-        low = jnp.where(live, idx, 0.0).astype(I32)
-        up = low + 1
-        here = pl.ds(azim * stations, stations)
-        low_ref[here, :] = (low % 4) * 32 + low // 4
-        up_ref[here, :] = (up % 4) * 32 + up // 4
-        wl_ref[here, :] = jnp.where(live, 1.0 - weight, 0.0)
-        wu_ref[here, :] = jnp.where(live, weight, 0.0)
-        lines_ref[pl.ds(azim * stations, stations), :] = speed_ref[
-            pl.ds(azim, stations, stride=2), :
-        ]
-        lines_ref[pl.ds((2 + azim) * stations, stations), :] = diffuse_ref[
-            pl.ds(azim, stations, stride=2), :
-        ]
-        lines_ref[pl.ds((4 + azim) * stations, stations), :] = jnp.where(live, 1.0, 0.0)
 
 
 def refit(got_ref, low_ref, up_ref, wl_ref, wu_ref, out_ref):
@@ -234,9 +228,10 @@
         here = pl.ds(azim * stations, stations)
         lower = jnp.take_along_axis(x, low_ref[here, :], axis=1)
         upper = jnp.take_along_axis(x, up_ref[here, :], axis=1)
-        out_ref[pl.ds(line * stations, stations), :] = (
-            wl_ref[here, :] * lower + wu_ref[here, :] * upper
-        )
+        fitted = wl_ref[here, :] * lower + wu_ref[here, :] * upper
+        if line < 2:
+            fitted = jnp.where(wl_ref[here, :] + wu_ref[here, :] > 0.0, fitted, MARK)
+        out_ref[pl.ds(line * stations, stations), :] = fitted
 
     for group in range(5):
         for half in range(2):
@@ -268,10 +263,17 @@
     return ref[:, pl.ds(azim * (ref.shape[1] // 2) + 8 * block, 8), :]
 
 
+def marked_line(ref, azim, block):
+    field = line_of(ref, azim, block)
+    live = field[:1] < 0.5 * MARK
+    first = jnp.where(live, field[:1], 0.0)
+    return jnp.concatenate([first, field[1:]], axis=0), jnp.where(live, 1.0, 0.0)
+
+
 def coefficients(ref, azim, block):
-    stations = ref.shape[0] // 6
+    stations = ref.shape[0] // 4
     return [
-        ref[pl.ds((2 * kind + azim) * stations + 8 * block, 8), :][None] for kind in range(3)
+        ref[pl.ds((2 * kind + azim) * stations + 8 * block, 8), :][None] for kind in range(2)
     ]
 
 
@@ -284,11 +286,12 @@
     mix = mix_ref[...]
     stations = m_ref.shape[1] // 2
     for block in range(stations // 8):
-        field = [line_of(m_ref, azim, block) for azim in range(2)]
+        field, live = zip(*[marked_line(m_ref, azim, block) for azim in range(2)])
         term = mixed(mix, field)
         base = []
         for azim in range(2):
-            speed, diffuse, active = coefficients(lines_ref, azim, block)
+            speed, diffuse = coefficients(lines_ref, azim, block)
+            active = live[azim]
             lateral = field[1 - azim] - 2.0 * field[azim]
             rate = diffuse * lateral - speed * slope(field[azim]) - term[azim]
             base.append(field[azim] + active * rate)
@@ -317,9 +320,11 @@
     stations = m_ref.shape[1] // 2
     copies = []
     for block in range(stations // 8):
-        field = [line_of(m_ref, azim, block) for azim in range(2)]
-        near = [line_of(left_ref, 1, block), line_of(right_ref, 0, block)]
-        far = [line_of(left_ref, 0, block), line_of(right_ref, 1, block)]
+        field, live = zip(*[marked_line(m_ref, azim, block) for azim in range(2)])
+        near, near_live = zip(
+            marked_line(left_ref, 1, block), marked_line(right_ref, 0, block)
+        )
+        far = [marked_line(left_ref, 0, block)[0], marked_line(right_ref, 1, block)[0]]
         outer = [
             coefficients(lines_left_ref, 1, block),
             coefficients(lines_right_ref, 0, block),
@@ -327,15 +332,16 @@
         own = [coefficients(lines_ref, azim, block) for azim in range(2)]
         near_term = mixed(mix, near)
         first = [
-            line_of(base_ref, azim, block) + (own[azim][2] * own[azim][1]) * near[azim]
+            line_of(base_ref, azim, block) + (live[azim] * own[azim][1]) * near[azim]
             for azim in range(2)
         ]
         for azim in range(2):
-            speed, diffuse, active = outer[azim]
+            speed, diffuse = outer[azim]
             lateral = (far[azim] + field[azim]) - 2.0 * near[azim]
             rate = diffuse * lateral - speed * slope(near[azim]) - near_term[azim]
-            outside = near[azim] + active * rate
-            speed, diffuse, active = own[azim]
+            outside = near[azim] + near_live[azim] * rate
+            speed, diffuse = own[azim]
+            active = live[azim]
             lateral = (outside + first[1 - azim]) - 2.0 * first[azim]
             term = line_of(term_ref, azim, block) + (active * diffuse) * near_term[azim]
             rate = diffuse * lateral - speed * slope(first[azim]) - term
@@ -399,38 +405,28 @@
     )
     got = exchange(packed, STENCIL_ROWS, 2)
 
-    x = state_in.transpose(0, 2, 3, 1).reshape(nv * 2 * cells, total)
-    (packed,) = call(
-        state_pack,
-        [shape((peers * STATE_ROWS, LANES), F32)],
-        got,
-        x,
-        out_space=pltpu.HBM,
-        scratch=[pltpu.VMEM((peers * STATE_ROWS, LANES), F32), pltpu.SemaphoreType.DMA((4,))],
-    )
-    got_state = exchange(packed, STATE_ROWS, 2)
-
-    plane = shape((2 * stations, LANES), F32)
-    index_plane = shape((2 * stations, LANES), I32)
-    low, up, wl, wu, lines, mix = call(
-        stencil_place,
-        [
-            index_plane,
-            index_plane,
-            plane,
-            plane,
-            shape((6 * stations, LANES), F32),
-            shape((8 * nv + 8, 24 * nv + 8), BF16),
-        ],
-        got,
+    lines, mix = call(
+        line_setup,
+        [shape((4 * stations, LANES), F32), shape((8 * nv + 8, 24 * nv + 8), BF16)],
         flat(normal_speed),
         flat(azim_diffusion),
         mixing,
     )
     lines_left, lines_right = neighbours(lines)
-    got_state, lines_left, lines_right = lax.optimization_barrier(
-        (got_state, lines_left, lines_right)
-    )
+
+    x = state_in.transpose(0, 2, 3, 1).reshape(nv * 2 * cells, total)
+    plane = shape((2 * stations, LANES), F32)
+    index_plane = shape((2 * stations, LANES), I32)
+    packed, low, up, wl, wu = call(
+        state_pack,
+        [shape((peers * STATE_ROWS, LANES), F32), index_plane, index_plane, plane, plane],
+        got,
+        x,
+    )
+    packed, lines_left, lines_right, mix = lax.optimization_barrier(
+        (packed, lines_left, lines_right, mix)
+    )
+    got_state = exchange(packed, STATE_ROWS, 2)
 
     (moved,) = call(
         refit, [shape((nv * 2 * stations, LANES), F32)], got_state, low, up, wl, wu

time: 68 us -> 67.4 us (level)
  the two profiles are of different devices: /device:TPU:193 before, /device:TPU:8 now
where the time goes in v5:
time: 67.4 us; the launch traced here: 67 us
  blocking collectives  27.1 us (40%)
  starting transfers between devices  21.2 us (31%)
  waiting for transfers between devices  10.1 us (15%)
  Pallas kernels  7.14 us (11%)
  local copies, waits for them, and re-layouts  1.35 us (2%)
    all_to_all x1, blocking collectives, exchange(): lax.all_to_all(parts, 'stream', split_axis=0, concat_axis=0, tiled=True)  27.1 us
    ppermute x4, starting transfers between devices, neighbours(): return (lax.ppermute(a, 'azim', up), lax.ppermute(a, 'azim', down))  10.9 us
    all_to_all x1, starting transfers between devices, exchange(): lax.all_to_all(parts, 'stream', split_axis=0, concat_axis=0, tiled=True)  10.3 us
    ppermute x4, waiting for transfers between devices, neighbours(): return (lax.ppermute(a, 'azim', up), lax.ppermute(a, 'azim', down))  9.42 us
    pallas_call x6, Pallas kernels, call(): pl.pallas_call(body, out_shape=outs, in_specs=[pl.BlockSpec(memory_space=...  7.14 us
  transfers between devices with their start and end apart: 5, of which 3 were waited for; matrix products, arithmetic and copies ran while one was open for 2% of the time, Pallas kernels for 4%

profile of v5, /device:TPU:8, one launch (start us, length us, event | category | flops | bytes accessed | tf_op | source)
XLA Modules:
  0.0 67.0 jit_solution(2183136922571957245)
XLA Ops:
  0.0 1.9 %shard_map.82 = f32[320,128]{1,0:T(8,128)} custom-call(s32[1,32]{1,0:T(1,128)} %bitcast.29, s32[64,128]{1,0:T(8,128)} %bitcast.26, f32[64,128]{1,0:T(8,128)} %bitcast.27, s32[2,32]{1,0:T(2,128)} %bitcast.28), custom_call_target="tpu_custom_call" | custom-call | bytes 229760 | tf_op jit(solution)/shard_map/pallas_call | solution.py:22
  1.9 0.0 copy-start
  1.9 0.0 copy-start.1
  1.9 0.0 copy-start.2
  1.9 10.3 %all-to-all-start = ((f32[32,5,2,128]{3,2,1,0:T(2,128)}), f32[32,5,2,128]{3,2,1,0:T(2,128)S(1)}, u32[]{:S(2)}, u32[]{:S(2)}) async-start(f32[32,5,2,128]{3,2,1,0:T(2,128)} %bitcast.25), calls=%async_computation | async-start | bytes 327680 | tf_op jit(solution)/shard_map/all_to_all | solution.py:381
  12.2 0.0 copy-done
  12.2 0.0 copy-done.1
  12.2 0.0 copy-done.2
  12.2 0.4 shard_map.84
  12.6 7.9 %collective-permute-start.1 = (f32[128,128]{1,0:T(8,128)S(1)}, f32[128,128]{1,0:T(8,128)S(1)}, u32[]{:S(2)}, u32[]{:S(2)}) collective-permute-start(f32[128,128]{1,0:T(8,128)S(1)} %get-tuple-element.19.lines_ref), channel_id=1, source_target_pairs={{1,0},{2,1},{3,2},{4,3},{5,4},{6,5},{7,6},{8,7},{9,8},{10,9},{11,1... | collective-permute-start | bytes 196616 | tf_op jit(solution)/shard_map/ppermute | solution.py:387
  20.6 0.0 collective-permute-start
  20.6 1.3 %reshape.43.x_ref = f32[168,1024]{1,0:T(8,128)S(1)} reshape(f32[21,2,4,1024]{3,2,1,0:T(4,128)} %bitcast.24) | data formatting | bytes 1376256 | tf_op jit(solution)/shard_map/reshape | solution.py:417
  21.9 0.7 %all-to-all-done = f32[32,5,2,128]{3,2,1,0:T(2,128)S(1)} async-done(((f32[32,5,2,128]{3,2,1,0:T(2,128)}), f32[32,5,2,128]{3,2,1,0:T(2,128)S(1)}, u32[]{:S(2)}, u32[]{:S(2)}) %all-to-all-start) | async-done | bytes 163872 | tf_op jit(solution)/shard_map/all_to_all | solution.py:381
  22.6 1.3 %shard_map.83 = (f32[1344,128]{1,0:T(8,128)S(1)}, s32[64,128]{1,0:T(8,128)S(1)}, s32[64,128]{1,0:T(8,128)S(1)}, f32[64,128]{1,0:T(8,128)S(1)}, f32[64,128]{1,0:T(8,128)S(1)}) custom-call(f32[320,128]{1,0:T(8,128)S(1)} %bitcast.21, f32[168,1024]{1,0:T(8,128)S(1)} %reshape.43.x_ref), custom_call_target="tpu_custom_call" | custom-call | bytes 1671168 | tf_op jit(solution)/shard_map/pallas_call | solution.py:22
  23.8 0.0 collective-permute-done.1.lines_right_ref
  23.9 1.6 %collective-permute-done.lines_left_ref = f32[128,128]{1,0:T(8,128)S(1)} collective-permute-done((f32[128,128]{1,0:T(8,128)S(1)}, f32[128,128]{1,0:T(8,128)S(1)}, u32[]{:S(2)}, u32[]{:S(2)}) %collective-permute-start) | collective-permute-done | bytes 65568 | tf_op jit(solution)/shard_map/ppermute | solution.py:387
  25.5 27.1 %all_to_all.10 = f32[32,21,2,128]{3,2,1,0:T(2,128)S(1)} all-to-all(f32[32,21,2,128]{3,2,1,0:T(2,128)S(1)} %bitcast.20), channel_id=1, replica_groups=mesh['stream'=32,'azim'=16] {'stream'}, dimensions={0} | all-to-all | bytes 1376256 | tf_op jit(solution)/shard_map/all_to_all | solution.py:381
  52.6 1.2 %shard_map.85 = f32[1344,128]{1,0:T(8,128)S(1)} custom-call(f32[1344,128]{1,0:T(8,128)S(1)} %bitcast.17, s32[64,128]{1,0:T(8,128)S(1)} %get-tuple-element.22.low_ref, s32[64,128]{1,0:T(8,128)S(1)} %get-tuple-element.23.up_ref, f32[64,128]{1,0:T(8,128)S(1)} %get-tuple-element.24.wl_ref, f32[64,128]{1,0:T(8,128)S(1)} %get-tuple-element.25.wu_ref), custom_call_target="tpu_custom_call" | custom-call | bytes 1507328 | tf_op jit(solution)/shard_map/pallas_call | solution.py:22
  53.8 0.0 collective-permute-start.3
  53.8 2.9 %collective-permute-start.2 = (f32[1344,128]{1,0:T(8,128)S(1)}, f32[1344,128]{1,0:T(8,128)S(1)}, u32[]{:S(2)}, u32[]{:S(2)}) collective-permute-start(f32[1344,128]{1,0:T(8,128)S(1)} %shard_map.85), channel_id=1, source_target_pairs={{1,0},{2,1},{3,2},{4,3},{5,4},{6,5},{7,6},{8,7},{9,8},{10,9},{11,1... | collective-permute-start | bytes 2064392 | tf_op jit(solution)/shard_map/ppermute | solution.py:387
  56.8 0.8 %shard_map.86 = (f32[21,64,128]{2,1,0:T(8,128)S(1)}, f32[21,64,128]{2,1,0:T(8,128)S(1)}) custom-call(f32[21,64,128]{2,1,0:T(8,128)S(1)} %bitcast.15, f32[128,128]{1,0:T(8,128)S(1)} %get-tuple-element.19.lines_ref, bf16[176,512]{1,0:T(8,128)(2,1)S(1)} %get-tuple-element.26.mix_ref), custom_call_target="tpu_custom_call" | custom-call | bytes 2310144 | tf_op jit(solution)/shard_map/pallas_call | solution.py:22
  57.6 7.8 %collective-permute-done.3 = f32[1344,128]{1,0:T(8,128)S(1)} collective-permute-done((f32[1344,128]{1,0:T(8,128)S(1)}, f32[1344,128]{1,0:T(8,128)S(1)}, u32[]{:S(2)}, u32[]{:S(2)}) %collective-permute-start.3) | collective-permute-done | bytes 688160 | tf_op jit(solution)/shard_map/ppermute | solution.py:387
  65.4 0.0 collective-permute-done.2
  65.4 1.7 %shard_map.87 = f32[21,64,128]{2,1,0:T(8,128)} custom-call(f32[21,64,128]{2,1,0:T(8,128)S(1)} %bitcast.16, f32[21,64,128]{2,1,0:T(8,128)S(1)} %get-tuple-element.27.base_ref, f32[21,64,128]{2,1,0:T(8,128)S(1)} %get-tuple-element.28.term_ref, f32[21,64,128]{2,1,0:T(8,128)S(1)} %bitcast.19, f32[21,64,128]{2,1,0:T(8,128)S(1)} %bitcast.18, ...), custom_call_target="tpu_custom_call" | custom-call | bytes 4505600 | tf_op jit(solution)/shard_map/pallas_call | solution.py:22
Async XLA Ops:
  1.9 10.4 %copy-start = (f32[32,2,128]{2,1,0:T(2,128)S(1)}, f32[32,2,128]{2,1,0:T(2,128)}, u32[]{:S(2)}) copy-start(f32[32,2,128]{2,1,0:T(2,128)} %param.13) | copy-start | bytes 98308
  1.9 10.4 %copy-start.1 = (f32[32,2,128]{2,1,0:T(2,128)S(1)}, f32[32,2,128]{2,1,0:T(2,128)}, u32[]{:S(2)}) copy-start(f32[32,2,128]{2,1,0:T(2,128)} %param.14) | copy-start | bytes 98308
  1.9 10.4 %copy-start.2 = (f32[21,21]{1,0:T(8,128)S(1)}, f32[21,21]{1,0:T(8,128)}, u32[]{:S(2)}) copy-start(f32[21,21]{1,0:T(8,128)} %mixing_ref.1) | copy-start | bytes 5296
  1.9 20.7 %all-to-all-start = ((f32[32,5,2,128]{3,2,1,0:T(2,128)}), f32[32,5,2,128]{3,2,1,0:T(2,128)S(1)}, u32[]{:S(2)}, u32[]{:S(2)}) async-start(f32[32,5,2,128]{3,2,1,0:T(2,128)} %bitcast.25), calls=%async_computation | async-start | bytes 327680 | tf_op jit(solution)/shard_map/all_to_all | solution.py:381
  12.6 11.2 %collective-permute-start.1 = (f32[128,128]{1,0:T(8,128)S(1)}, f32[128,128]{1,0:T(8,128)S(1)}, u32[]{:S(2)}, u32[]{:S(2)}) collective-permute-start(f32[128,128]{1,0:T(8,128)S(1)} %get-tuple-element.19.lines_ref), channel_id=1, source_target_pairs={{1,0},{2,1},{3,2},{4,3},{5,4},{6,5},{7,6},{8,7},{9,8},{10,9},{11,1... | collective-permute-start | bytes 196616 | tf_op jit(solution)/shard_map/ppermute | solution.py:387
  20.6 4.9 %collective-permute-start = (f32[128,128]{1,0:T(8,128)S(1)}, f32[128,128]{1,0:T(8,128)S(1)}, u32[]{:S(2)}, u32[]{:S(2)}) collective-permute-start(f32[128,128]{1,0:T(8,128)S(1)} %get-tuple-element.19.lines_ref), channel_id=1, source_target_pairs={{0,1},{1,2},{2,3},{3,4},{4,5},{5,6},{6,7},{7,8},{8,9},{9,10},{10,1... | collective-permute-start | bytes 196616 | tf_op jit(solution)/shard_map/ppermute | solution.py:387
  53.8 11.6 %collective-permute-start.3 = (f32[1344,128]{1,0:T(8,128)S(1)}, f32[1344,128]{1,0:T(8,128)S(1)}, u32[]{:S(2)}, u32[]{:S(2)}) collective-permute-start(f32[1344,128]{1,0:T(8,128)S(1)} %shard_map.85), channel_id=1, source_target_pairs={{0,1},{1,2},{2,3},{3,4},{4,5},{5,6},{6,7},{7,8},{8,9},{9,10},{10,1... | collective-permute-start | bytes 2064392 | tf_op jit(solution)/shard_map/ppermute | solution.py:387
  53.8 11.6 %collective-permute-start.2 = (f32[1344,128]{1,0:T(8,128)S(1)}, f32[1344,128]{1,0:T(8,128)S(1)}, u32[]{:S(2)}, u32[]{:S(2)}) collective-permute-start(f32[1344,128]{1,0:T(8,128)S(1)} %shard_map.85), channel_id=1, source_target_pairs={{1,0},{2,1},{3,2},{4,3},{5,4},{6,5},{7,6},{8,7},{9,8},{10,9},{11,1... | collective-permute-start | bytes 2064392 | tf_op jit(solution)/shard_map/ppermute | solution.py:387

commit v6 on v5

--- a/solution.py
+++ b/solution.py
@@ -147,13 +147,23 @@
             row = jnp.where(quarter == i, new_rows[4 * tile + i : 4 * tile + i + 1], row)
         tiles.append(row)
     nid = jnp.concatenate(tiles, axis=1)
+    stations = total // peers
+    owner = jnp.broadcast_to((nid // stations).astype(F32), (16, total)).astype(BF16)
+    place = jnp.where(iota((stations, total), 0) == nid % stations, 1.0, 0.0).astype(BF16)
+    none = jnp.zeros((16, total), BF16)
     high, low = split(x_ref[...])
     both = jnp.concatenate([high, low], axis=0).astype(BF16)
     lines = x_ref.shape[0]
     width = 2 * LANES
     own_cell = iota((8, LANES), 0) % 4 == iota((8, LANES), 1) // 32
     for chunk in range(total // width):
-        pick = jnp.where(iota((width, total), 0) + chunk * width == nid, 1.0, 0.0).astype(BF16)
+        rows_here = []
+        for peer in range(chunk * 8, chunk * 8 + 8):
+            mine = owner == jnp.bfloat16(peer)
+            rows_here += [
+                jnp.where(mine, place[at : at + 16], none) for at in range(0, stations, 16)
+            ]
+        pick = jnp.concatenate(rows_here, axis=0)
         moved = lax.dot_general(
             both, pick, (((1,), (1,)), ((), ())), preferred_element_type=F32
         )
@@ -224,13 +234,18 @@
         ]
         return jnp.concatenate(cells, axis=0).T
 
+    def read(ref):
+        return [ref[pl.ds(azim * stations, stations), :] for azim in range(2)]
+
+    low, up, wl, wu = read(low_ref), read(up_ref), read(wl_ref), read(wu_ref)
+
+    def take(x, index):
+        return jnp.take_along_axis(x, index, axis=1, mode="promise_in_bounds")
+
     def fit(x, azim, line):
-        here = pl.ds(azim * stations, stations)
-        lower = jnp.take_along_axis(x, low_ref[here, :], axis=1)
-        upper = jnp.take_along_axis(x, up_ref[here, :], axis=1)
-        fitted = wl_ref[here, :] * lower + wu_ref[here, :] * upper
+        fitted = wl[azim] * take(x, low[azim]) + wu[azim] * take(x, up[azim])
         if line < 2:
-            fitted = jnp.where(wl_ref[here, :] + wu_ref[here, :] > 0.0, fitted, MARK)
+            fitted = jnp.where(wl[azim] + wu[azim] > 0.0, fitted, MARK)
         out_ref[pl.ds(line * stations, stations), :] = fitted
 
     for group in range(5):
@@ -277,12 +292,18 @@
     ]
 
 
-def slope(field):
-    below = jnp.where(iota(field.shape, 2) == 0, 0.0, pltpu.roll(field, 1, 2))
-    return field - below
-
-
-def inner(m_ref, lines_ref, mix_ref, base_ref, term_ref):
+def factors(ref, azim, block, active):
+    speed, diffuse = coefficients(ref, azim, block)
+    side, below = active * diffuse, active * speed
+    own = 1.0 - (2.0 * side + below)
+    return own, side, jnp.where(iota(below.shape, 2) == 0, 0.0, below)
+
+
+def shifted(field):
+    return pltpu.roll(field, 1, 2)
+
+
+def inner(m_ref, lines_ref, mix_ref, base_ref, rest_ref):
     mix = mix_ref[...]
     stations = m_ref.shape[1] // 2
     for block in range(stations // 8):
@@ -290,22 +311,22 @@
         term = mixed(mix, field)
         base = []
         for azim in range(2):
-            speed, diffuse = coefficients(lines_ref, azim, block)
-            active = live[azim]
-            lateral = field[1 - azim] - 2.0 * field[azim]
-            rate = diffuse * lateral - speed * slope(field[azim]) - term[azim]
-            base.append(field[azim] + active * rate)
+            own, side, below = factors(lines_ref, azim, block, live[azim])
+            base.append(
+                (own * field[azim] + side * field[1 - azim])
+                + (below * shifted(field[azim]) - live[azim] * term[azim])
+            )
         term = mixed(mix, base)
         for azim in range(2):
             here = pl.ds(azim * stations + 8 * block, 8)
             base_ref[:, here, :] = base[azim]
-            term_ref[:, here, :] = term[azim]
+            rest_ref[:, here, :] = 0.5 * (field[azim] - live[azim] * term[azim])
 
 
 def sections(
     m_ref,
     base_ref,
-    term_ref,
+    rest_ref,
     right_ref,
     left_ref,
     lines_ref,
@@ -326,26 +347,25 @@
         )
         far = [marked_line(left_ref, 0, block)[0], marked_line(right_ref, 1, block)[0]]
         outer = [
-            coefficients(lines_left_ref, 1, block),
-            coefficients(lines_right_ref, 0, block),
+            factors(lines_left_ref, 1, block, near_live[0]),
+            factors(lines_right_ref, 0, block, near_live[1]),
         ]
-        own = [coefficients(lines_ref, azim, block) for azim in range(2)]
+        inside = [factors(lines_ref, azim, block, live[azim]) for azim in range(2)]
         near_term = mixed(mix, near)
         first = [
-            line_of(base_ref, azim, block) + (live[azim] * own[azim][1]) * near[azim]
-            for azim in range(2)
+            line_of(base_ref, azim, block) + inside[azim][1] * near[azim] for azim in range(2)
         ]
         for azim in range(2):
-            speed, diffuse = outer[azim]
-            lateral = (far[azim] + field[azim]) - 2.0 * near[azim]
-            rate = diffuse * lateral - speed * slope(near[azim]) - near_term[azim]
-            outside = near[azim] + near_live[azim] * rate
-            speed, diffuse = own[azim]
-            active = live[azim]
-            lateral = (outside + first[1 - azim]) - 2.0 * first[azim]
-            term = line_of(term_ref, azim, block) + (active * diffuse) * near_term[azim]
-            rate = diffuse * lateral - speed * slope(first[azim]) - term
-            out = 0.5 * ((field[azim] + first[azim]) + active * rate)
+            own, side, below = outer[azim]
+            beyond = (own * near[azim] + side * (far[azim] + field[azim])) + (
+                below * shifted(near[azim]) - near_live[azim] * near_term[azim]
+            )
+            own, side, below = [0.5 * factor for factor in inside[azim]]
+            out = (
+                (line_of(rest_ref, azim, block) + own * first[azim])
+                + side * ((beyond + first[1 - azim]) - near_term[azim])
+                + below * shifted(first[azim])
+            )
             out_ref[:, pl.ds(azim + 16 * block, 8, stride=2), :] = out
         done = pl.ds(16 * block, 16)
         copy = pltpu.make_async_copy(
@@ -435,13 +455,13 @@
 
     field = (nv, 2 * stations, LANES)
     moved = moved.reshape(field)
-    base, term = call(inner, [shape(field, F32)] * 2, moved, lines, mix)
+    base, rest = call(inner, [shape(field, F32)] * 2, moved, lines, mix)
     (out,) = call(
         sections,
         [shape(field, F32)],
         moved,
         base,
-        term,
+        rest,
         right.reshape(field),
         left.reshape(field),
         lines,

time: 67.4 us -> 67.2 us (level)
  transfers between devices with their start and end apart: 5 -> 5, of which waited for: 3 -> 3; matrix products, arithmetic and copies ran while one was open for 2% -> 2% of each run, Pallas kernels for 4% -> 3%
where the time goes in v6:
time: 67.2 us; the launch traced here: 66.8 us
  blocking collectives  27.1 us (40%)
  starting transfers between devices  21.2 us (32%)
  waiting for transfers between devices  10.3 us (15%)
  Pallas kernels  6.75 us (10%)
  local copies, waits for them, and re-layouts  1.35 us (2%)
    all_to_all x1, blocking collectives, exchange(): lax.all_to_all(parts, 'stream', split_axis=0, concat_axis=0, tiled=True)  27.1 us
    ppermute x4, starting transfers between devices, neighbours(): return (lax.ppermute(a, 'azim', up), lax.ppermute(a, 'azim', down))  10.9 us
    all_to_all x1, starting transfers between devices, exchange(): lax.all_to_all(parts, 'stream', split_axis=0, concat_axis=0, tiled=True)  10.3 us
    ppermute x4, waiting for transfers between devices, neighbours(): return (lax.ppermute(a, 'azim', up), lax.ppermute(a, 'azim', down))  9.61 us
    pallas_call x6, Pallas kernels, call(): pl.pallas_call(body, out_shape=outs, in_specs=[pl.BlockSpec(memory_space=...  6.75 us
  transfers between devices with their start and end apart: 5, of which 3 were waited for; matrix products, arithmetic and copies ran while one was open for 2% of the time, Pallas kernels for 3%

profile of v6, /device:TPU:8, one launch (start us, length us, event | category | flops | bytes accessed | tf_op | source)
XLA Modules:
  0.0 66.8 jit_solution(2589383246791517471)
XLA Ops:
  0.0 1.9 %shard_map.82 = f32[320,128]{1,0:T(8,128)} custom-call(s32[1,32]{1,0:T(1,128)} %bitcast.29, s32[64,128]{1,0:T(8,128)} %bitcast.26, f32[64,128]{1,0:T(8,128)} %bitcast.27, s32[2,32]{1,0:T(2,128)} %bitcast.28), custom_call_target="tpu_custom_call" | custom-call | bytes 229760 | tf_op jit(solution)/shard_map/pallas_call | solution.py:22
  1.9 0.0 copy-start
  1.9 0.0 copy-start.1
  1.9 0.0 copy-start.2
  1.9 10.3 %all-to-all-start = ((f32[32,5,2,128]{3,2,1,0:T(2,128)}), f32[32,5,2,128]{3,2,1,0:T(2,128)S(1)}, u32[]{:S(2)}, u32[]{:S(2)}) async-start(f32[32,5,2,128]{3,2,1,0:T(2,128)} %bitcast.25), calls=%async_computation | async-start | bytes 327680 | tf_op jit(solution)/shard_map/all_to_all | solution.py:401
  12.2 0.0 copy-done
  12.2 0.0 copy-done.1
  12.2 0.0 copy-done.2
  12.2 0.4 shard_map.84
  12.6 7.9 %collective-permute-start.1 = (f32[128,128]{1,0:T(8,128)S(1)}, f32[128,128]{1,0:T(8,128)S(1)}, u32[]{:S(2)}, u32[]{:S(2)}) collective-permute-start(f32[128,128]{1,0:T(8,128)S(1)} %get-tuple-element.19.lines_ref), channel_id=1, source_target_pairs={{1,0},{2,1},{3,2},{4,3},{5,4},{6,5},{7,6},{8,7},{9,8},{10,9},{11,1... | collective-permute-start | bytes 196616 | tf_op jit(solution)/shard_map/ppermute | solution.py:407
  20.6 0.0 collective-permute-start
  20.6 1.3 %reshape.43.x_ref = f32[168,1024]{1,0:T(8,128)S(1)} reshape(f32[21,2,4,1024]{3,2,1,0:T(4,128)} %bitcast.24) | data formatting | bytes 1376256 | tf_op jit(solution)/shard_map/reshape | solution.py:437
  21.9 0.7 %all-to-all-done = f32[32,5,2,128]{3,2,1,0:T(2,128)S(1)} async-done(((f32[32,5,2,128]{3,2,1,0:T(2,128)}), f32[32,5,2,128]{3,2,1,0:T(2,128)S(1)}, u32[]{:S(2)}, u32[]{:S(2)}) %all-to-all-start) | async-done | bytes 163872 | tf_op jit(solution)/shard_map/all_to_all | solution.py:401
  22.6 1.1 %shard_map.83 = (f32[1344,128]{1,0:T(8,128)S(1)}, s32[64,128]{1,0:T(8,128)S(1)}, s32[64,128]{1,0:T(8,128)S(1)}, f32[64,128]{1,0:T(8,128)S(1)}, f32[64,128]{1,0:T(8,128)S(1)}) custom-call(f32[320,128]{1,0:T(8,128)S(1)} %bitcast.21, f32[168,1024]{1,0:T(8,128)S(1)} %reshape.43.x_ref), custom_call_target="tpu_custom_call" | custom-call | bytes 1671168 | tf_op jit(solution)/shard_map/pallas_call | solution.py:22
  23.7 0.0 collective-permute-done.1.lines_right_ref
  23.7 1.8 %collective-permute-done.lines_left_ref = f32[128,128]{1,0:T(8,128)S(1)} collective-permute-done((f32[128,128]{1,0:T(8,128)S(1)}, f32[128,128]{1,0:T(8,128)S(1)}, u32[]{:S(2)}, u32[]{:S(2)}) %collective-permute-start) | collective-permute-done | bytes 65568 | tf_op jit(solution)/shard_map/ppermute | solution.py:407
  25.5 27.1 %all_to_all.10 = f32[32,21,2,128]{3,2,1,0:T(2,128)S(1)} all-to-all(f32[32,21,2,128]{3,2,1,0:T(2,128)S(1)} %bitcast.20), channel_id=1, replica_groups=mesh['stream'=32,'azim'=16] {'stream'}, dimensions={0} | all-to-all | bytes 1376256 | tf_op jit(solution)/shard_map/all_to_all | solution.py:401
  52.6 1.2 %shard_map.85 = f32[1344,128]{1,0:T(8,128)S(1)} custom-call(f32[1344,128]{1,0:T(8,128)S(1)} %bitcast.17, s32[64,128]{1,0:T(8,128)S(1)} %get-tuple-element.22.low_ref, s32[64,128]{1,0:T(8,128)S(1)} %get-tuple-element.23.up_ref, f32[64,128]{1,0:T(8,128)S(1)} %get-tuple-element.24.wl_ref, f32[64,128]{1,0:T(8,128)S(1)} %get-tuple-element.25.wu_ref), custom_call_target="tpu_custom_call" | custom-call | bytes 1507328 | tf_op jit(solution)/shard_map/pallas_call | solution.py:22
  53.8 0.0 collective-permute-start.3
  53.8 2.9 %collective-permute-start.2 = (f32[1344,128]{1,0:T(8,128)S(1)}, f32[1344,128]{1,0:T(8,128)S(1)}, u32[]{:S(2)}, u32[]{:S(2)}) collective-permute-start(f32[1344,128]{1,0:T(8,128)S(1)} %shard_map.85), channel_id=1, source_target_pairs={{1,0},{2,1},{3,2},{4,3},{5,4},{6,5},{7,6},{8,7},{9,8},{10,9},{11,1... | collective-permute-start | bytes 2064392 | tf_op jit(solution)/shard_map/ppermute | solution.py:407
  56.8 0.8 %shard_map.86 = (f32[21,64,128]{2,1,0:T(8,128)S(1)}, f32[21,64,128]{2,1,0:T(8,128)S(1)}) custom-call(f32[21,64,128]{2,1,0:T(8,128)S(1)} %bitcast.15, f32[128,128]{1,0:T(8,128)S(1)} %get-tuple-element.19.lines_ref, bf16[176,512]{1,0:T(8,128)(2,1)S(1)} %get-tuple-element.26.mix_ref), custom_call_target="tpu_custom_call" | custom-call | bytes 2310144 | tf_op jit(solution)/shard_map/pallas_call | solution.py:22
  57.5 7.8 %collective-permute-done.3 = f32[1344,128]{1,0:T(8,128)S(1)} collective-permute-done((f32[1344,128]{1,0:T(8,128)S(1)}, f32[1344,128]{1,0:T(8,128)S(1)}, u32[]{:S(2)}, u32[]{:S(2)}) %collective-permute-start.3) | collective-permute-done | bytes 688160 | tf_op jit(solution)/shard_map/ppermute | solution.py:407
  65.4 0.0 collective-permute-done.2
  65.4 1.5 %shard_map.87 = f32[21,64,128]{2,1,0:T(8,128)} custom-call(f32[21,64,128]{2,1,0:T(8,128)S(1)} %bitcast.16, f32[21,64,128]{2,1,0:T(8,128)S(1)} %get-tuple-element.27.base_ref, f32[21,64,128]{2,1,0:T(8,128)S(1)} %get-tuple-element.28.rest_ref, f32[21,64,128]{2,1,0:T(8,128)S(1)} %bitcast.19, f32[21,64,128]{2,1,0:T(8,128)S(1)} %bitcast.18, ...), custom_call_target="tpu_custom_call" | custom-call | bytes 4505600 | tf_op jit(solution)/shard_map/pallas_call | solution.py:22
Async XLA Ops:
  1.9 10.4 %copy-start = (f32[32,2,128]{2,1,0:T(2,128)S(1)}, f32[32,2,128]{2,1,0:T(2,128)}, u32[]{:S(2)}) copy-start(f32[32,2,128]{2,1,0:T(2,128)} %param.13) | copy-start | bytes 98308
  1.9 10.4 %copy-start.1 = (f32[32,2,128]{2,1,0:T(2,128)S(1)}, f32[32,2,128]{2,1,0:T(2,128)}, u32[]{:S(2)}) copy-start(f32[32,2,128]{2,1,0:T(2,128)} %param.14) | copy-start | bytes 98308
  1.9 10.4 %copy-start.2 = (f32[21,21]{1,0:T(8,128)S(1)}, f32[21,21]{1,0:T(8,128)}, u32[]{:S(2)}) copy-start(f32[21,21]{1,0:T(8,128)} %mixing_ref.1) | copy-start | bytes 5296
  1.9 20.7 %all-to-all-start = ((f32[32,5,2,128]{3,2,1,0:T(2,128)}), f32[32,5,2,128]{3,2,1,0:T(2,128)S(1)}, u32[]{:S(2)}, u32[]{:S(2)}) async-start(f32[32,5,2,128]{3,2,1,0:T(2,128)} %bitcast.25), calls=%async_computation | async-start | bytes 327680 | tf_op jit(solution)/shard_map/all_to_all | solution.py:401
  12.6 11.1 %collective-permute-start.1 = (f32[128,128]{1,0:T(8,128)S(1)}, f32[128,128]{1,0:T(8,128)S(1)}, u32[]{:S(2)}, u32[]{:S(2)}) collective-permute-start(f32[128,128]{1,0:T(8,128)S(1)} %get-tuple-element.19.lines_ref), channel_id=1, source_target_pairs={{1,0},{2,1},{3,2},{4,3},{5,4},{6,5},{7,6},{8,7},{9,8},{10,9},{11,1... | collective-permute-start | bytes 196616 | tf_op jit(solution)/shard_map/ppermute | solution.py:407
  20.6 4.9 %collective-permute-start = (f32[128,128]{1,0:T(8,128)S(1)}, f32[128,128]{1,0:T(8,128)S(1)}, u32[]{:S(2)}, u32[]{:S(2)}) collective-permute-start(f32[128,128]{1,0:T(8,128)S(1)} %get-tuple-element.19.lines_ref), channel_id=1, source_target_pairs={{0,1},{1,2},{2,3},{3,4},{4,5},{5,6},{6,7},{7,8},{8,9},{9,10},{10,1... | collective-permute-start | bytes 196616 | tf_op jit(solution)/shard_map/ppermute | solution.py:407
  53.8 11.6 %collective-permute-start.3 = (f32[1344,128]{1,0:T(8,128)S(1)}, f32[1344,128]{1,0:T(8,128)S(1)}, u32[]{:S(2)}, u32[]{:S(2)}) collective-permute-start(f32[1344,128]{1,0:T(8,128)S(1)} %shard_map.85), channel_id=1, source_target_pairs={{0,1},{1,2},{2,3},{3,4},{4,5},{5,6},{6,7},{7,8},{8,9},{9,10},{10,1... | collective-permute-start | bytes 2064392 | tf_op jit(solution)/shard_map/ppermute | solution.py:407
  53.8 11.6 %collective-permute-start.2 = (f32[1344,128]{1,0:T(8,128)S(1)}, f32[1344,128]{1,0:T(8,128)S(1)}, u32[]{:S(2)}, u32[]{:S(2)}) collective-permute-start(f32[1344,128]{1,0:T(8,128)S(1)} %shard_map.85), channel_id=1, source_target_pairs={{1,0},{2,1},{3,2},{4,3},{5,4},{6,5},{7,6},{8,7},{9,8},{10,9},{11,1... | collective-permute-start | bytes 2064392 | tf_op jit(solution)/shard_map/ppermute | solution.py:407

commit v7 on v6

--- a/solution.py
+++ b/solution.py
@@ -222,9 +222,10 @@
     mix_ref[...] = jnp.concatenate([both[0], both[0], both[1], rest], axis=1).astype(BF16)
 
 
-def refit(got_ref, low_ref, up_ref, wl_ref, wu_ref, out_ref):
+def refit(got_ref, low_ref, up_ref, wl_ref, wu_ref, out_ref, line_ref):
     rows = STATE_ROWS
     stations = low_ref.shape[0] // 2
+    nv = out_ref.shape[0] // low_ref.shape[0]
 
     def lines(first_row):
         cells = [
@@ -234,34 +235,43 @@
         ]
         return jnp.concatenate(cells, axis=0).T
 
-    def read(ref):
-        return [ref[pl.ds(azim * stations, stations), :] for azim in range(2)]
-
-    low, up, wl, wu = read(low_ref), read(up_ref), read(wl_ref), read(wu_ref)
-
-    def take(x, index):
-        return jnp.take_along_axis(x, index, axis=1, mode="promise_in_bounds")
-
-    def fit(x, azim, line):
-        fitted = wl[azim] * take(x, low[azim]) + wu[azim] * take(x, up[azim])
-        if line < 2:
-            fitted = jnp.where(wl[azim] + wu[azim] > 0.0, fitted, MARK)
-        out_ref[pl.ds(line * stations, stations), :] = fitted
+    def keep(x, line):
+        line_ref[pl.ds(line * stations, stations), :] = x
 
     for group in range(5):
         for half in range(2):
             x = lines(8 * group + 4 * half)
             for i in range(4):
-                fit(x[i * stations : (i + 1) * stations], half, 8 * group + 2 * i + half)
+                keep(x[i * stations : (i + 1) * stations], 8 * group + 2 * i + half)
     lane = iota((stations, LANES), 1)
     last = [got_ref[pl.ds(40 + half, stations, stride=rows), :] for half in range(2)]
     cells = []
     for c in range(4):
-        a, b = [last[half] if c == half else pltpu.roll(last[half], (32 * (half - c)) % LANES, 1) for half in range(2)]
+        a, b = [
+            last[half] if c == half else pltpu.roll(last[half], (32 * (half - c)) % LANES, 1)
+            for half in range(2)
+        ]
         cells.append(jnp.where(lane < 32, a, b))
     x = jnp.concatenate(cells, axis=0).T
     for half in range(2):
-        fit(x[half * stations : (half + 1) * stations], half, 40 + half)
+        keep(x[half * stations : (half + 1) * stations], 40 + half)
+
+    def take(x, index):
+        return jnp.take_along_axis(x, index, axis=1, mode="promise_in_bounds")
+
+    for azim in range(2):
+        for block in range(stations // 8):
+            at = azim * stations + 8 * block
+            here = pl.ds(at, 8)
+            low, up, wl, wu = low_ref[here, :], up_ref[here, :], wl_ref[here, :], wu_ref[here, :]
+            parts = [line_ref[pl.ds(2 * stations * v + at, 8), :] for v in range(nv)]
+            lower = [wl * take(part, low) for part in parts]
+            upper = [wu * take(part, up) for part in parts]
+            for v in range(nv):
+                fitted = lower[v] + upper[v]
+                if v == 0:
+                    fitted = jnp.where(wl + wu > 0.0, fitted, MARK)
+                out_ref[pl.ds(2 * stations * v + at, 8), :] = fitted
 
 
 def mixed(mix, fields):
@@ -449,7 +459,14 @@
     got_state = exchange(packed, STATE_ROWS, 2)
 
     (moved,) = call(
-        refit, [shape((nv * 2 * stations, LANES), F32)], got_state, low, up, wl, wu
+        refit,
+        [shape((nv * 2 * stations, LANES), F32)],
+        got_state,
+        low,
+        up,
+        wl,
+        wu,
+        scratch=[pltpu.VMEM((nv * 2 * stations, LANES), F32)],
     )
     left, right = neighbours(moved)
 

time: 67.2 us -> 66.8 us (level)
  no operation moved by 1% of the time
where the time goes in v7:
time: 66.8 us; the launch traced here: 66.4 us
  blocking collectives  27.1 us (41%)
  starting transfers between devices  21.2 us (32%)
  waiting for transfers between devices  10.3 us (15%)
  Pallas kernels  6.32 us (9%)
  local copies, waits for them, and re-layouts  1.35 us (2%)
    all_to_all x1, blocking collectives, exchange(): lax.all_to_all(parts, 'stream', split_axis=0, concat_axis=0, tiled=True)  27.1 us
    ppermute x4, starting transfers between devices, neighbours(): return (lax.ppermute(a, 'azim', up), lax.ppermute(a, 'azim', down))  10.9 us
    all_to_all x1, starting transfers between devices, exchange(): lax.all_to_all(parts, 'stream', split_axis=0, concat_axis=0, tiled=True)  10.3 us
    ppermute x4, waiting for transfers between devices, neighbours(): return (lax.ppermute(a, 'azim', up), lax.ppermute(a, 'azim', down))  9.61 us
    pallas_call x6, Pallas kernels, call(): pl.pallas_call(body, out_shape=outs, in_specs=[pl.BlockSpec(memory_space=...  6.32 us
  transfers between devices with their start and end apart: 5, of which 3 were waited for; matrix products, arithmetic and copies ran while one was open for 2% of the time, Pallas kernels for 3%

profile of v7, /device:TPU:8, one launch (start us, length us, event | category | flops | bytes accessed | tf_op | source)
XLA Modules:
  0.0 66.4 jit_solution(17687594663479860973)
XLA Ops:
  0.0 1.9 %shard_map.82 = f32[320,128]{1,0:T(8,128)} custom-call(s32[1,32]{1,0:T(1,128)} %bitcast.29, s32[64,128]{1,0:T(8,128)} %bitcast.26, f32[64,128]{1,0:T(8,128)} %bitcast.27, s32[2,32]{1,0:T(2,128)} %bitcast.28), custom_call_target="tpu_custom_call" | custom-call | bytes 229760 | tf_op jit(solution)/shard_map/pallas_call | solution.py:22
  1.9 0.0 copy-start
  1.9 0.0 copy-start.1
  1.9 0.0 copy-start.2
  1.9 10.3 %all-to-all-start = ((f32[32,5,2,128]{3,2,1,0:T(2,128)}), f32[32,5,2,128]{3,2,1,0:T(2,128)S(1)}, u32[]{:S(2)}, u32[]{:S(2)}) async-start(f32[32,5,2,128]{3,2,1,0:T(2,128)} %bitcast.25), calls=%async_computation | async-start | bytes 327680 | tf_op jit(solution)/shard_map/all_to_all | solution.py:411
  12.2 0.0 copy-done
  12.2 0.0 copy-done.1
  12.2 0.0 copy-done.2
  12.2 0.4 shard_map.84
  12.6 7.9 %collective-permute-start.1 = (f32[128,128]{1,0:T(8,128)S(1)}, f32[128,128]{1,0:T(8,128)S(1)}, u32[]{:S(2)}, u32[]{:S(2)}) collective-permute-start(f32[128,128]{1,0:T(8,128)S(1)} %get-tuple-element.19.lines_ref), channel_id=1, source_target_pairs={{1,0},{2,1},{3,2},{4,3},{5,4},{6,5},{7,6},{8,7},{9,8},{10,9},{11,1... | collective-permute-start | bytes 196616 | tf_op jit(solution)/shard_map/ppermute | solution.py:417
  20.6 0.0 collective-permute-start
  20.6 1.3 %reshape.43.x_ref = f32[168,1024]{1,0:T(8,128)S(1)} reshape(f32[21,2,4,1024]{3,2,1,0:T(4,128)} %bitcast.24) | data formatting | bytes 1376256 | tf_op jit(solution)/shard_map/reshape | solution.py:447
  21.9 0.7 %all-to-all-done = f32[32,5,2,128]{3,2,1,0:T(2,128)S(1)} async-done(((f32[32,5,2,128]{3,2,1,0:T(2,128)}), f32[32,5,2,128]{3,2,1,0:T(2,128)S(1)}, u32[]{:S(2)}, u32[]{:S(2)}) %all-to-all-start) | async-done | bytes 163872 | tf_op jit(solution)/shard_map/all_to_all | solution.py:411
  22.6 1.1 %shard_map.83 = (f32[1344,128]{1,0:T(8,128)S(1)}, s32[64,128]{1,0:T(8,128)S(1)}, s32[64,128]{1,0:T(8,128)S(1)}, f32[64,128]{1,0:T(8,128)S(1)}, f32[64,128]{1,0:T(8,128)S(1)}) custom-call(f32[320,128]{1,0:T(8,128)S(1)} %bitcast.21, f32[168,1024]{1,0:T(8,128)S(1)} %reshape.43.x_ref), custom_call_target="tpu_custom_call" | custom-call | bytes 1671168 | tf_op jit(solution)/shard_map/pallas_call | solution.py:22
  23.7 0.0 collective-permute-done.1.lines_right_ref
  23.7 1.8 %collective-permute-done.lines_left_ref = f32[128,128]{1,0:T(8,128)S(1)} collective-permute-done((f32[128,128]{1,0:T(8,128)S(1)}, f32[128,128]{1,0:T(8,128)S(1)}, u32[]{:S(2)}, u32[]{:S(2)}) %collective-permute-start) | collective-permute-done | bytes 65568 | tf_op jit(solution)/shard_map/ppermute | solution.py:417
  25.5 27.1 %all_to_all.10 = f32[32,21,2,128]{3,2,1,0:T(2,128)S(1)} all-to-all(f32[32,21,2,128]{3,2,1,0:T(2,128)S(1)} %bitcast.20), channel_id=1, replica_groups=mesh['stream'=32,'azim'=16] {'stream'}, dimensions={0} | all-to-all | bytes 1376256 | tf_op jit(solution)/shard_map/all_to_all | solution.py:411
  52.6 0.8 %shard_map.85 = f32[1344,128]{1,0:T(8,128)S(1)} custom-call(f32[1344,128]{1,0:T(8,128)S(1)} %bitcast.17, s32[64,128]{1,0:T(8,128)S(1)} %get-tuple-element.22.low_ref, s32[64,128]{1,0:T(8,128)S(1)} %get-tuple-element.23.up_ref, f32[64,128]{1,0:T(8,128)S(1)} %get-tuple-element.24.wl_ref, f32[64,128]{1,0:T(8,128)S(1)} %get-tuple-element.25.wu_ref), custom_call_target="tpu_custom_call" | custom-call | bytes 1507328 | tf_op jit(solution)/shard_map/pallas_call | solution.py:22
  53.4 0.0 collective-permute-start.3
  53.4 2.9 %collective-permute-start.2 = (f32[1344,128]{1,0:T(8,128)S(1)}, f32[1344,128]{1,0:T(8,128)S(1)}, u32[]{:S(2)}, u32[]{:S(2)}) collective-permute-start(f32[1344,128]{1,0:T(8,128)S(1)} %shard_map.85), channel_id=1, source_target_pairs={{1,0},{2,1},{3,2},{4,3},{5,4},{6,5},{7,6},{8,7},{9,8},{10,9},{11,1... | collective-permute-start | bytes 2064392 | tf_op jit(solution)/shard_map/ppermute | solution.py:417
  56.3 0.8 %shard_map.86 = (f32[21,64,128]{2,1,0:T(8,128)S(1)}, f32[21,64,128]{2,1,0:T(8,128)S(1)}) custom-call(f32[21,64,128]{2,1,0:T(8,128)S(1)} %bitcast.15, f32[128,128]{1,0:T(8,128)S(1)} %get-tuple-element.19.lines_ref, bf16[176,512]{1,0:T(8,128)(2,1)S(1)} %get-tuple-element.26.mix_ref), custom_call_target="tpu_custom_call" | custom-call | bytes 2310144 | tf_op jit(solution)/shard_map/pallas_call | solution.py:22
  57.1 7.8 %collective-permute-done.3 = f32[1344,128]{1,0:T(8,128)S(1)} collective-permute-done((f32[1344,128]{1,0:T(8,128)S(1)}, f32[1344,128]{1,0:T(8,128)S(1)}, u32[]{:S(2)}, u32[]{:S(2)}) %collective-permute-start.3) | collective-permute-done | bytes 688160 | tf_op jit(solution)/shard_map/ppermute | solution.py:417
  64.9 0.0 collective-permute-done.2
  64.9 1.5 %shard_map.87 = f32[21,64,128]{2,1,0:T(8,128)} custom-call(f32[21,64,128]{2,1,0:T(8,128)S(1)} %bitcast.16, f32[21,64,128]{2,1,0:T(8,128)S(1)} %get-tuple-element.27.base_ref, f32[21,64,128]{2,1,0:T(8,128)S(1)} %get-tuple-element.28.rest_ref, f32[21,64,128]{2,1,0:T(8,128)S(1)} %bitcast.19, f32[21,64,128]{2,1,0:T(8,128)S(1)} %bitcast.18, ...), custom_call_target="tpu_custom_call" | custom-call | bytes 4505600 | tf_op jit(solution)/shard_map/pallas_call | solution.py:22
Async XLA Ops:
  1.9 10.4 %copy-start = (f32[32,2,128]{2,1,0:T(2,128)S(1)}, f32[32,2,128]{2,1,0:T(2,128)}, u32[]{:S(2)}) copy-start(f32[32,2,128]{2,1,0:T(2,128)} %param.13) | copy-start | bytes 98308
  1.9 10.4 %copy-start.1 = (f32[32,2,128]{2,1,0:T(2,128)S(1)}, f32[32,2,128]{2,1,0:T(2,128)}, u32[]{:S(2)}) copy-start(f32[32,2,128]{2,1,0:T(2,128)} %param.14) | copy-start | bytes 98308
  1.9 10.4 %copy-start.2 = (f32[21,21]{1,0:T(8,128)S(1)}, f32[21,21]{1,0:T(8,128)}, u32[]{:S(2)}) copy-start(f32[21,21]{1,0:T(8,128)} %mixing_ref.1) | copy-start | bytes 5296
  1.9 20.7 %all-to-all-start = ((f32[32,5,2,128]{3,2,1,0:T(2,128)}), f32[32,5,2,128]{3,2,1,0:T(2,128)S(1)}, u32[]{:S(2)}, u32[]{:S(2)}) async-start(f32[32,5,2,128]{3,2,1,0:T(2,128)} %bitcast.25), calls=%async_computation | async-start | bytes 327680 | tf_op jit(solution)/shard_map/all_to_all | solution.py:411
  12.6 11.1 %collective-permute-start.1 = (f32[128,128]{1,0:T(8,128)S(1)}, f32[128,128]{1,0:T(8,128)S(1)}, u32[]{:S(2)}, u32[]{:S(2)}) collective-permute-start(f32[128,128]{1,0:T(8,128)S(1)} %get-tuple-element.19.lines_ref), channel_id=1, source_target_pairs={{1,0},{2,1},{3,2},{4,3},{5,4},{6,5},{7,6},{8,7},{9,8},{10,9},{11,1... | collective-permute-start | bytes 196616 | tf_op jit(solution)/shard_map/ppermute | solution.py:417
  20.6 4.9 %collective-permute-start = (f32[128,128]{1,0:T(8,128)S(1)}, f32[128,128]{1,0:T(8,128)S(1)}, u32[]{:S(2)}, u32[]{:S(2)}) collective-permute-start(f32[128,128]{1,0:T(8,128)S(1)} %get-tuple-element.19.lines_ref), channel_id=1, source_target_pairs={{0,1},{1,2},{2,3},{3,4},{4,5},{5,6},{6,7},{7,8},{8,9},{9,10},{10,1... | collective-permute-start | bytes 196616 | tf_op jit(solution)/shard_map/ppermute | solution.py:417
  53.4 11.6 %collective-permute-start.3 = (f32[1344,128]{1,0:T(8,128)S(1)}, f32[1344,128]{1,0:T(8,128)S(1)}, u32[]{:S(2)}, u32[]{:S(2)}) collective-permute-start(f32[1344,128]{1,0:T(8,128)S(1)} %shard_map.85), channel_id=1, source_target_pairs={{0,1},{1,2},{2,3},{3,4},{4,5},{5,6},{6,7},{7,8},{8,9},{9,10},{10,1... | collective-permute-start | bytes 2064392 | tf_op jit(solution)/shard_map/ppermute | solution.py:417
  53.4 11.6 %collective-permute-start.2 = (f32[1344,128]{1,0:T(8,128)S(1)}, f32[1344,128]{1,0:T(8,128)S(1)}, u32[]{:S(2)}, u32[]{:S(2)}) collective-permute-start(f32[1344,128]{1,0:T(8,128)S(1)} %shard_map.85), channel_id=1, source_target_pairs={{1,0},{2,1},{3,2},{4,3},{5,4},{6,5},{7,6},{8,7},{9,8},{10,9},{11,1... | collective-permute-start | bytes 2064392 | tf_op jit(solution)/shard_map/ppermute | solution.py:417

commit v8 on v7

--- a/solution.py
+++ b/solution.py
@@ -43,7 +43,7 @@
     return slot * 2 + azim
 
 
-STENCIL_ROWS = 10
+STENCIL_ROWS = 9
 
 
 def stencil_pack(nid_hbm, idx_hbm, weight_hbm, count_hbm, out_ref, nid_ref, idx_ref, weight_ref, count_ref, sems):
@@ -64,7 +64,7 @@
     earlier = jnp.dot(owners, before, preferred_element_type=F32)
     rank = jnp.sum(owners * earlier, axis=0, keepdims=True)
     same = iota((stations, stations), 0) == iota((stations, stations), 1)
-    spread = (iota((stations, LANES), 1) % stations == iota((stations, LANES), 0)).astype(F32)
+    spread = (iota((stations, LANES), 1) == iota((stations, LANES), 0)).astype(F32)
     wide = jnp.dot(
         jnp.broadcast_to(nid.astype(F32), (peers, stations)),
         spread,
@@ -81,7 +81,7 @@
     for slot in range(SLOTS):
         pick = jnp.where(rank == float(slot), owners, 0.0)
         found = jnp.sum(pick * (place + 1).astype(F32), axis=1, keepdims=True) - 1.0
-        places = jnp.where(lane == slot, found, places)
+        places = jnp.where(lane == stations + slot, found, places)
         for azim in range(2):
             idx = idx_ref[pl.ds(azim, stations, stride=2), :]
             live = cell < counts[azim]
@@ -94,17 +94,16 @@
             out_ref[pl.ds(4 + at, peers, stride=rows), :] = jnp.dot(
                 pick, weight, preferred_element_type=F32, precision=HIGHEST
             )
-    out_ref[pl.ds(8, peers, stride=rows), :] = wide
-    out_ref[pl.ds(9, peers, stride=rows), :] = places
+    out_ref[pl.ds(8, peers, stride=rows), :] = jnp.where(lane < stations, wide, places)
 
 
 def stencil_place(got_ref, low_ref, up_ref, wl_ref, wu_ref):
     rows = STENCIL_ROWS
     peers = got_ref.shape[0] // rows
     stations = low_ref.shape[0] // 2
-    spots = got_ref[pl.ds(9, peers, stride=rows), :].T
+    spots = got_ref[pl.ds(8, peers, stride=rows), :].T
     place = iota((stations, peers), 0).astype(F32)
-    picks = [jnp.where(spots[slot : slot + 1, :] == place, 1.0, 0.0) for slot in range(SLOTS)]
+    picks = [jnp.where(spots[stations + slot : stations + slot + 1, :] == place, 1.0, 0.0) for slot in range(SLOTS)]
     for azim in range(2):
         idx = jnp.zeros((stations, LANES), F32)
         weight = jnp.zeros((stations, LANES), F32)
@@ -138,7 +137,10 @@
     rows, stencil_rows = STATE_ROWS, STENCIL_ROWS
     peers = out_ref.shape[0] // rows
     total = x_ref.shape[1]
-    new_rows = got_ref[pl.ds(8, peers, stride=stencil_rows), :].astype(I32)
+    new_rows = got_ref[pl.ds(8, peers, stride=stencil_rows), :]
+    new_rows = jnp.where(iota((peers, LANES), 1) < 32, new_rows, 0.0)
+    new_rows = new_rows + pltpu.roll(new_rows, 64, 1)
+    new_rows = (new_rows + pltpu.roll(new_rows, 32, 1)).astype(I32)
     quarter = iota((1, LANES), 1) // 32
     tiles = []
     for tile in range(total // LANES):
@@ -433,7 +435,7 @@
         ],
         room=60,
     )
-    got = exchange(packed, STENCIL_ROWS, 2)
+    got = exchange(packed, STENCIL_ROWS, 1)
 
     lines, mix = call(
         line_setup,

time: 66.8 us -> 66.8 us (level)
  transfers between devices with their start and end apart: 5 -> 5, of which waited for: 3 -> 3; matrix products, arithmetic and copies ran while one was open for 2% -> 2% of each run, Pallas kernels for 3% -> 4%
where the time goes in v8:
time: 66.8 us; the launch traced here: 66.4 us
  blocking collectives  27.1 us (41%)
  starting transfers between devices  21.2 us (32%)
  waiting for transfers between devices  10.1 us (15%)
  Pallas kernels  6.46 us (10%)
  local copies, waits for them, and re-layouts  1.35 us (2%)
    all_to_all x1, blocking collectives, exchange(): lax.all_to_all(parts, 'stream', split_axis=0, concat_axis=0, tiled=True)  27.1 us
    ppermute x4, starting transfers between devices, neighbours(): return (lax.ppermute(a, 'azim', up), lax.ppermute(a, 'azim', down))  10.9 us
    all_to_all x1, starting transfers between devices, exchange(): lax.all_to_all(parts, 'stream', split_axis=0, concat_axis=0, tiled=True)  10.3 us
    ppermute x4, waiting for transfers between devices, neighbours(): return (lax.ppermute(a, 'azim', up), lax.ppermute(a, 'azim', down))  9.79 us
    pallas_call x6, Pallas kernels, call(): pl.pallas_call(body, out_shape=outs, in_specs=[pl.BlockSpec(memory_space=...  6.46 us
  transfers between devices with their start and end apart: 5, of which 3 were waited for; matrix products, arithmetic and copies ran while one was open for 2% of the time, Pallas kernels for 4%

profile of v8, /device:TPU:8, one launch (start us, length us, event | category | flops | bytes accessed | tf_op | source)
XLA Modules:
  0.0 66.4 jit_solution(8732110122749035757)
XLA Ops:
  0.0 1.8 %shard_map.82 = f32[288,128]{1,0:T(8,128)} custom-call(s32[1,32]{1,0:T(1,128)} %bitcast.29, s32[64,128]{1,0:T(8,128)} %bitcast.26, f32[64,128]{1,0:T(8,128)} %bitcast.27, s32[2,32]{1,0:T(2,128)} %bitcast.28), custom_call_target="tpu_custom_call" | custom-call | bytes 213376 | tf_op jit(solution)/shard_map/pallas_call | solution.py:22
  1.9 0.0 copy-start
  1.9 0.0 copy-start.1
  1.9 0.0 copy-start.2
  1.9 10.3 %all-to-all-start = ((f32[32,9,1,128]{3,2,1,0:T(1,128)}), f32[32,9,1,128]{3,2,1,0:T(1,128)S(1)}, u32[]{:S(2)}, u32[]{:S(2)}) async-start(f32[32,9,1,128]{3,2,1,0:T(1,128)} %bitcast.25), calls=%async_computation | async-start | bytes 294912 | tf_op jit(solution)/shard_map/all_to_all | solution.py:413
  12.2 0.0 copy-done
  12.2 0.0 copy-done.1
  12.2 0.0 copy-done.2
  12.2 0.4 shard_map.84
  12.6 7.9 %collective-permute-start.1 = (f32[128,128]{1,0:T(8,128)S(1)}, f32[128,128]{1,0:T(8,128)S(1)}, u32[]{:S(2)}, u32[]{:S(2)}) collective-permute-start(f32[128,128]{1,0:T(8,128)S(1)} %get-tuple-element.19.lines_ref), channel_id=1, source_target_pairs={{1,0},{2,1},{3,2},{4,3},{5,4},{6,5},{7,6},{8,7},{9,8},{10,9},{11,1... | collective-permute-start | bytes 196616 | tf_op jit(solution)/shard_map/ppermute | solution.py:419
  20.6 0.0 collective-permute-start
  20.6 1.3 %reshape.43.x_ref = f32[168,1024]{1,0:T(8,128)S(1)} reshape(f32[21,2,4,1024]{3,2,1,0:T(4,128)} %bitcast.24) | data formatting | bytes 1376256 | tf_op jit(solution)/shard_map/reshape | solution.py:449
  21.9 0.3 all-to-all-done
  22.2 1.2 %shard_map.83 = (f32[1344,128]{1,0:T(8,128)S(1)}, s32[64,128]{1,0:T(8,128)S(1)}, s32[64,128]{1,0:T(8,128)S(1)}, f32[64,128]{1,0:T(8,128)S(1)}, f32[64,128]{1,0:T(8,128)S(1)}) custom-call(f32[288,128]{1,0:T(8,128)S(1)} %bitcast.21, f32[168,1024]{1,0:T(8,128)S(1)} %reshape.43.x_ref), custom_call_target="tpu_custom_call" | custom-call | bytes 1654784 | tf_op jit(solution)/shard_map/pallas_call | solution.py:22
  23.5 0.0 collective-permute-done.1.lines_right_ref
  23.5 1.9 %collective-permute-done.lines_left_ref = f32[128,128]{1,0:T(8,128)S(1)} collective-permute-done((f32[128,128]{1,0:T(8,128)S(1)}, f32[128,128]{1,0:T(8,128)S(1)}, u32[]{:S(2)}, u32[]{:S(2)}) %collective-permute-start) | collective-permute-done | bytes 65568 | tf_op jit(solution)/shard_map/ppermute | solution.py:419
  25.5 27.1 %all_to_all.10 = f32[32,21,2,128]{3,2,1,0:T(2,128)S(1)} all-to-all(f32[32,21,2,128]{3,2,1,0:T(2,128)S(1)} %bitcast.20), channel_id=1, replica_groups=mesh['stream'=32,'azim'=16] {'stream'}, dimensions={0} | all-to-all | bytes 1376256 | tf_op jit(solution)/shard_map/all_to_all | solution.py:413
  52.6 0.8 %shard_map.85 = f32[1344,128]{1,0:T(8,128)S(1)} custom-call(f32[1344,128]{1,0:T(8,128)S(1)} %bitcast.17, s32[64,128]{1,0:T(8,128)S(1)} %get-tuple-element.22.low_ref, s32[64,128]{1,0:T(8,128)S(1)} %get-tuple-element.23.up_ref, f32[64,128]{1,0:T(8,128)S(1)} %get-tuple-element.24.wl_ref, f32[64,128]{1,0:T(8,128)S(1)} %get-tuple-element.25.wu_ref), custom_call_target="tpu_custom_call" | custom-call | bytes 1507328 | tf_op jit(solution)/shard_map/pallas_call | solution.py:22
  53.3 0.0 collective-permute-start.3
  53.4 2.9 %collective-permute-start.2 = (f32[1344,128]{1,0:T(8,128)S(1)}, f32[1344,128]{1,0:T(8,128)S(1)}, u32[]{:S(2)}, u32[]{:S(2)}) collective-permute-start(f32[1344,128]{1,0:T(8,128)S(1)} %shard_map.85), channel_id=1, source_target_pairs={{1,0},{2,1},{3,2},{4,3},{5,4},{6,5},{7,6},{8,7},{9,8},{10,9},{11,1... | collective-permute-start | bytes 2064392 | tf_op jit(solution)/shard_map/ppermute | solution.py:419
  56.3 0.8 %shard_map.86 = (f32[21,64,128]{2,1,0:T(8,128)S(1)}, f32[21,64,128]{2,1,0:T(8,128)S(1)}) custom-call(f32[21,64,128]{2,1,0:T(8,128)S(1)} %bitcast.15, f32[128,128]{1,0:T(8,128)S(1)} %get-tuple-element.19.lines_ref, bf16[176,512]{1,0:T(8,128)(2,1)S(1)} %get-tuple-element.26.mix_ref), custom_call_target="tpu_custom_call" | custom-call | bytes 2310144 | tf_op jit(solution)/shard_map/pallas_call | solution.py:22
  57.1 7.8 %collective-permute-done.3 = f32[1344,128]{1,0:T(8,128)S(1)} collective-permute-done((f32[1344,128]{1,0:T(8,128)S(1)}, f32[1344,128]{1,0:T(8,128)S(1)}, u32[]{:S(2)}, u32[]{:S(2)}) %collective-permute-start.3) | collective-permute-done | bytes 688160 | tf_op jit(solution)/shard_map/ppermute | solution.py:419
  64.9 0.0 collective-permute-done.2
  64.9 1.5 %shard_map.87 = f32[21,64,128]{2,1,0:T(8,128)} custom-call(f32[21,64,128]{2,1,0:T(8,128)S(1)} %bitcast.16, f32[21,64,128]{2,1,0:T(8,128)S(1)} %get-tuple-element.27.base_ref, f32[21,64,128]{2,1,0:T(8,128)S(1)} %get-tuple-element.28.rest_ref, f32[21,64,128]{2,1,0:T(8,128)S(1)} %bitcast.19, f32[21,64,128]{2,1,0:T(8,128)S(1)} %bitcast.18, ...), custom_call_target="tpu_custom_call" | custom-call | bytes 4505600 | tf_op jit(solution)/shard_map/pallas_call | solution.py:22
Async XLA Ops:
  1.9 10.4 %copy-start = (f32[32,2,128]{2,1,0:T(2,128)S(1)}, f32[32,2,128]{2,1,0:T(2,128)}, u32[]{:S(2)}) copy-start(f32[32,2,128]{2,1,0:T(2,128)} %param.13) | copy-start | bytes 98308
  1.9 10.4 %copy-start.1 = (f32[32,2,128]{2,1,0:T(2,128)S(1)}, f32[32,2,128]{2,1,0:T(2,128)}, u32[]{:S(2)}) copy-start(f32[32,2,128]{2,1,0:T(2,128)} %param.14) | copy-start | bytes 98308
  1.9 10.4 %copy-start.2 = (f32[21,21]{1,0:T(8,128)S(1)}, f32[21,21]{1,0:T(8,128)}, u32[]{:S(2)}) copy-start(f32[21,21]{1,0:T(8,128)} %mixing_ref.1) | copy-start | bytes 5296
  1.9 20.3 %all-to-all-start = ((f32[32,9,1,128]{3,2,1,0:T(1,128)}), f32[32,9,1,128]{3,2,1,0:T(1,128)S(1)}, u32[]{:S(2)}, u32[]{:S(2)}) async-start(f32[32,9,1,128]{3,2,1,0:T(1,128)} %bitcast.25), calls=%async_computation | async-start | bytes 294912 | tf_op jit(solution)/shard_map/all_to_all | solution.py:413
  12.6 10.9 %collective-permute-start.1 = (f32[128,128]{1,0:T(8,128)S(1)}, f32[128,128]{1,0:T(8,128)S(1)}, u32[]{:S(2)}, u32[]{:S(2)}) collective-permute-start(f32[128,128]{1,0:T(8,128)S(1)} %get-tuple-element.19.lines_ref), channel_id=1, source_target_pairs={{1,0},{2,1},{3,2},{4,3},{5,4},{6,5},{7,6},{8,7},{9,8},{10,9},{11,1... | collective-permute-start | bytes 196616 | tf_op jit(solution)/shard_map/ppermute | solution.py:419
  20.6 4.9 %collective-permute-start = (f32[128,128]{1,0:T(8,128)S(1)}, f32[128,128]{1,0:T(8,128)S(1)}, u32[]{:S(2)}, u32[]{:S(2)}) collective-permute-start(f32[128,128]{1,0:T(8,128)S(1)} %get-tuple-element.19.lines_ref), channel_id=1, source_target_pairs={{0,1},{1,2},{2,3},{3,4},{4,5},{5,6},{6,7},{7,8},{8,9},{9,10},{10,1... | collective-permute-start | bytes 196616 | tf_op jit(solution)/shard_map/ppermute | solution.py:419
  53.3 11.6 %collective-permute-start.3 = (f32[1344,128]{1,0:T(8,128)S(1)}, f32[1344,128]{1,0:T(8,128)S(1)}, u32[]{:S(2)}, u32[]{:S(2)}) collective-permute-start(f32[1344,128]{1,0:T(8,128)S(1)} %shard_map.85), channel_id=1, source_target_pairs={{0,1},{1,2},{2,3},{3,4},{4,5},{5,6},{6,7},{7,8},{8,9},{9,10},{10,1... | collective-permute-start | bytes 2064392 | tf_op jit(solution)/shard_map/ppermute | solution.py:419
  53.4 11.6 %collective-permute-start.2 = (f32[1344,128]{1,0:T(8,128)S(1)}, f32[1344,128]{1,0:T(8,128)S(1)}, u32[]{:S(2)}, u32[]{:S(2)}) collective-permute-start(f32[1344,128]{1,0:T(8,128)S(1)} %shard_map.85), channel_id=1, source_target_pairs={{1,0},{2,1},{3,2},{4,3},{5,4},{6,5},{7,6},{8,7},{9,8},{10,9},{11,1... | collective-permute-start | bytes 2064392 | tf_op jit(solution)/shard_map/ppermute | solution.py:419

commit v9 on v8

--- a/solution.py
+++ b/solution.py
@@ -137,16 +137,14 @@
     rows, stencil_rows = STATE_ROWS, STENCIL_ROWS
     peers = out_ref.shape[0] // rows
     total = x_ref.shape[1]
-    new_rows = got_ref[pl.ds(8, peers, stride=stencil_rows), :]
-    new_rows = jnp.where(iota((peers, LANES), 1) < 32, new_rows, 0.0)
-    new_rows = new_rows + pltpu.roll(new_rows, 64, 1)
-    new_rows = (new_rows + pltpu.roll(new_rows, 32, 1)).astype(I32)
+    new_rows = got_ref[pl.ds(8, peers, stride=stencil_rows), :].astype(I32)
     quarter = iota((1, LANES), 1) // 32
+    turned = [new_rows] + [pltpu.roll(new_rows, 32 * i, 1) for i in range(1, 4)]
     tiles = []
     for tile in range(total // LANES):
-        row = new_rows[4 * tile : 4 * tile + 1]
+        row = turned[0][4 * tile : 4 * tile + 1]
         for i in range(1, 4):
-            row = jnp.where(quarter == i, new_rows[4 * tile + i : 4 * tile + i + 1], row)
+            row = jnp.where(quarter == i, turned[i][4 * tile + i : 4 * tile + i + 1], row)
         tiles.append(row)
     nid = jnp.concatenate(tiles, axis=1)
     stations = total // peers
@@ -200,12 +198,14 @@
     stencil_place(got_ref, low_ref, up_ref, wl_ref, wu_ref)
 
 
-def line_setup(speed_ref, diffuse_ref, mixing_ref, lines_ref, mix_ref):
+def line_setup(speed_ref, diffuse_ref, mixing_ref, lines_ref, first_ref, second_ref, mix_ref):
     stations = speed_ref.shape[0] // 2
     for azim in range(2):
         here = pl.ds(azim, stations, stride=2)
-        lines_ref[pl.ds(azim * stations, stations), :] = speed_ref[here, :]
-        lines_ref[pl.ds((2 + azim) * stations, stations), :] = diffuse_ref[here, :]
+        for ref in (lines_ref, first_ref) if azim == 0 else (lines_ref, second_ref):
+            at = azim * 2 * stations if ref is lines_ref else 0
+            ref[pl.ds(at, stations), :] = speed_ref[here, :]
+            ref[pl.ds(at + stations, stations), :] = diffuse_ref[here, :]
     nv = mixing_ref.shape[0]
     high, low = split(0.25 * mixing_ref[...])
     by_row = (iota((mix_ref.shape[0], nv), 0) // 8 == iota((mix_ref.shape[0], nv), 1)).astype(F32)
@@ -298,9 +298,9 @@
 
 
 def coefficients(ref, azim, block):
-    stations = ref.shape[0] // 4
+    stations = ref.shape[0] // 4 if azim is not None else ref.shape[0] // 2
     return [
-        ref[pl.ds((2 * kind + azim) * stations + 8 * block, 8), :][None] for kind in range(2)
+        ref[pl.ds((2 * (azim or 0) + kind) * stations + 8 * block, 8), :][None] for kind in range(2)
     ]
 
 
@@ -336,6 +336,7 @@
 
 
 def sections(
+    lines_right_ref,
     m_ref,
     base_ref,
     rest_ref,
@@ -343,7 +344,6 @@
     left_ref,
     lines_ref,
     lines_left_ref,
-    lines_right_ref,
     mix_ref,
     out_hbm,
     out_ref,
@@ -359,8 +359,8 @@
         )
         far = [marked_line(left_ref, 0, block)[0], marked_line(right_ref, 1, block)[0]]
         outer = [
-            factors(lines_left_ref, 1, block, near_live[0]),
-            factors(lines_right_ref, 0, block, near_live[1]),
+            factors(lines_left_ref, None, block, near_live[0]),
+            factors(lines_right_ref, None, block, near_live[1]),
         ]
         inside = [factors(lines_ref, azim, block, live[azim]) for azim in range(2)]
         near_term = mixed(mix, near)
@@ -437,14 +437,16 @@
     )
     got = exchange(packed, STENCIL_ROWS, 1)
 
-    lines, mix = call(
+    one = shape((2 * stations, LANES), F32)
+    lines, line_first, line_second, mix = call(
         line_setup,
-        [shape((4 * stations, LANES), F32), shape((8 * nv + 8, 24 * nv + 8), BF16)],
+        [shape((4 * stations, LANES), F32), one, one, shape((8 * nv + 8, 24 * nv + 8), BF16)],
         flat(normal_speed),
         flat(azim_diffusion),
         mixing,
     )
-    lines_left, lines_right = neighbours(lines)
+    upward = [(i, (i + 1) % count) for i in range(count)]
+    lines_left = lax.ppermute(line_second, "azim", upward)
 
     x = state_in.transpose(0, 2, 3, 1).reshape(nv * 2 * cells, total)
     plane = shape((2 * stations, LANES), F32)
@@ -455,9 +457,7 @@
         got,
         x,
     )
-    packed, lines_left, lines_right, mix = lax.optimization_barrier(
-        (packed, lines_left, lines_right, mix)
-    )
+    packed, lines_left, mix = lax.optimization_barrier((packed, lines_left, mix))
     got_state = exchange(packed, STATE_ROWS, 2)
 
     (moved,) = call(
@@ -470,6 +470,8 @@
         wu,
         scratch=[pltpu.VMEM((nv * 2 * stations, LANES), F32)],
     )
+    moved, line_first = lax.optimization_barrier((moved, line_first))
+    lines_right = lax.ppermute(line_first, "azim", [(j, i) for i, j in upward])
     left, right = neighbours(moved)
 
     field = (nv, 2 * stations, LANES)
@@ -478,6 +480,7 @@
     (out,) = call(
         sections,
         [shape(field, F32)],
+        lines_right,
         moved,
         base,
         rest,
@@ -485,7 +488,6 @@
         left.reshape(field),
         lines,
         lines_left,
-        lines_right,
         mix,
         out_space=pltpu.HBM,
         scratch=[pltpu.VMEM(field, F32), pltpu.SemaphoreType.DMA((4,))],

time: 66.8 us -> 66.3 us (level)
  the two profiles are of different devices: /device:TPU:8 before, /device:TPU:201 now
where the time goes in v9:
time: 66.3 us; the launch traced here: 65.9 us
  blocking collectives  27.6 us (42%)
  starting transfers between devices  16.6 us (25%)
  waiting for transfers between devices  13.8 us (21%)
  Pallas kernels  6.39 us (10%)
  local copies, waits for them, and re-layouts  1.35 us (2%)
    all_to_all x1, blocking collectives, exchange(): lax.all_to_all(parts, 'stream', split_axis=0, concat_axis=0, tiled=True)  27.6 us
    ppermute x1, waiting for transfers between devices, shards(): lines_right = lax.ppermute(line_first, 'azim', [(j, i) for i, j in upward])  11 us
    all_to_all x1, starting transfers between devices, exchange(): lax.all_to_all(parts, 'stream', split_axis=0, concat_axis=0, tiled=True)  9.75 us
    pallas_call x6, Pallas kernels, call(): pl.pallas_call(body, out_shape=outs, in_specs=[pl.BlockSpec(memory_space=...  6.39 us
    ppermute x1, starting transfers between devices, shards(): lines_left = lax.ppermute(line_second, 'azim', upward)  4.44 us
    all_to_all x1, waiting for transfers between devices, exchange(): lax.all_to_all(parts, 'stream', split_axis=0, concat_axis=0, tiled=True)  2.8 us
    ppermute x2, starting transfers between devices, neighbours(): return (lax.ppermute(a, 'azim', up), lax.ppermute(a, 'azim', down))  2.28 us
    reshape x1, local copies, waits for them, and re-layouts, shards(): x = state_in.transpose(0, 2, 3, 1).reshape(nv * 2 * cells, total)  1.33 us
  transfers between devices with their start and end apart: 5, of which 2 were waited for; matrix products, arithmetic and copies ran while one was open for 2% of the time, Pallas kernels for 4%

profile of v9, /device:TPU:201, one launch (start us, length us, event | category | flops | bytes accessed | tf_op | source)
XLA Modules:
  0.0 65.9 jit_solution(7055626848793147926)
XLA Ops:
  0.0 1.8 %shard_map.82 = f32[288,128]{1,0:T(8,128)} custom-call(s32[1,32]{1,0:T(1,128)} %bitcast.29, s32[64,128]{1,0:T(8,128)} %bitcast.26, f32[64,128]{1,0:T(8,128)} %bitcast.27, s32[2,32]{1,0:T(2,128)} %bitcast.28), custom_call_target="tpu_custom_call" | custom-call | bytes 213376 | tf_op jit(solution)/shard_map/pallas_call | solution.py:22
  1.9 0.0 copy-start
  1.9 0.0 copy-start.1
  1.9 0.0 copy-start.2
  1.9 9.7 %all-to-all-start = ((f32[32,9,1,128]{3,2,1,0:T(1,128)}), f32[32,9,1,128]{3,2,1,0:T(1,128)S(1)}, u32[]{:S(2)}, u32[]{:S(2)}) async-start(f32[32,9,1,128]{3,2,1,0:T(1,128)} %bitcast.25), calls=%async_computation | async-start | bytes 294912 | tf_op jit(solution)/shard_map/all_to_all | solution.py:413
  11.6 0.0 copy-done
  11.7 0.0 copy-done.1
  11.7 0.0 copy-done.2
  11.7 0.4 shard_map.84
  12.1 4.4 %collective-permute-start = (f32[64,128]{1,0:T(8,128)S(1)}, f32[64,128]{1,0:T(8,128)S(1)}, u32[]{:S(2)}, u32[]{:S(2)}) collective-permute-start(f32[64,128]{1,0:T(8,128)S(1)} %get-tuple-element.22), channel_id=1, source_target_pairs={{0,1},{1,2},{2,3},{3,4},{4,5},{5,6},{6,7},{7,8},{8,9},{9,10},{10,1... | collective-permute-start | bytes 98312 | tf_op jit(solution)/shard_map/ppermute | solution.py:449
  16.5 1.3 %reshape.43.x_ref = f32[168,1024]{1,0:T(8,128)S(1)} reshape(f32[21,2,4,1024]{3,2,1,0:T(4,128)} %bitcast.24) | data formatting | bytes 1376256 | tf_op jit(solution)/shard_map/reshape | solution.py:451
  17.8 2.8 %all-to-all-done = f32[32,9,1,128]{3,2,1,0:T(1,128)S(1)} async-done(((f32[32,9,1,128]{3,2,1,0:T(1,128)}), f32[32,9,1,128]{3,2,1,0:T(1,128)S(1)}, u32[]{:S(2)}, u32[]{:S(2)}) %all-to-all-start) | async-done | bytes 147488 | tf_op jit(solution)/shard_map/all_to_all | solution.py:413
  20.6 1.2 %shard_map.83 = (f32[1344,128]{1,0:T(8,128)S(1)}, s32[64,128]{1,0:T(8,128)S(1)}, s32[64,128]{1,0:T(8,128)S(1)}, f32[64,128]{1,0:T(8,128)S(1)}, f32[64,128]{1,0:T(8,128)S(1)}) custom-call(f32[288,128]{1,0:T(8,128)S(1)} %bitcast.21, f32[168,1024]{1,0:T(8,128)S(1)} %reshape.43.x_ref), custom_call_target="tpu_custom_call" | custom-call | bytes 1654784 | tf_op jit(solution)/shard_map/pallas_call | solution.py:22
  21.8 0.0 collective-permute-done.lines_left_ref
  21.8 27.6 %all_to_all.10 = f32[32,21,2,128]{3,2,1,0:T(2,128)S(1)} all-to-all(f32[32,21,2,128]{3,2,1,0:T(2,128)S(1)} %bitcast.18), channel_id=1, replica_groups=mesh['stream'=32,'azim'=16] {'stream'}, dimensions={0} | all-to-all | bytes 1376256 | tf_op jit(solution)/shard_map/all_to_all | solution.py:413
  49.5 0.8 %shard_map.85 = f32[1344,128]{1,0:T(8,128)S(1)} custom-call(f32[1344,128]{1,0:T(8,128)S(1)} %bitcast.17, s32[64,128]{1,0:T(8,128)S(1)} %get-tuple-element.25.low_ref, s32[64,128]{1,0:T(8,128)S(1)} %get-tuple-element.26.up_ref, f32[64,128]{1,0:T(8,128)S(1)} %get-tuple-element.27.wl_ref, f32[64,128]{1,0:T(8,128)S(1)} %get-tuple-element.28.wu_ref), custom_call_target="tpu_custom_call" | custom-call | bytes 1507328 | tf_op jit(solution)/shard_map/pallas_call | solution.py:22
  50.2 2.3 %collective-permute-start.3 = (f32[1344,128]{1,0:T(8,128)S(1)}, f32[1344,128]{1,0:T(8,128)S(1)}, u32[]{:S(2)}, u32[]{:S(2)}) collective-permute-start(f32[1344,128]{1,0:T(8,128)S(1)} %shard_map.85), channel_id=1, source_target_pairs={{0,1},{1,2},{2,3},{3,4},{4,5},{5,6},{6,7},{7,8},{8,9},{9,10},{10,1... | collective-permute-start | bytes 2064392 | tf_op jit(solution)/shard_map/ppermute | solution.py:419
  52.5 0.0 collective-permute-start.2
  52.5 0.1 collective-permute-start.1
  52.6 0.8 %shard_map.86 = (f32[21,64,128]{2,1,0:T(8,128)S(1)}, f32[21,64,128]{2,1,0:T(8,128)S(1)}) custom-call(f32[21,64,128]{2,1,0:T(8,128)S(1)} %bitcast.15, f32[128,128]{1,0:T(8,128)S(1)} %get-tuple-element.32.lines_ref, bf16[176,512]{1,0:T(8,128)(2,1)S(1)} %get-tuple-element.33.mix_ref), custom_call_target="tpu_custom_call" | custom-call | bytes 2310144 | tf_op jit(solution)/shard_map/pallas_call | solution.py:22
  53.4 11.0 %collective-permute-done.1.lines_right_ref = f32[64,128]{1,0:T(8,128)S(1)} collective-permute-done((f32[64,128]{1,0:T(8,128)S(1)}, f32[64,128]{1,0:T(8,128)S(1)}, u32[]{:S(2)}, u32[]{:S(2)}) %collective-permute-start.1) | collective-permute-done | bytes 32800 | tf_op jit(solution)/shard_map/ppermute | solution.py:474
  64.4 0.0 collective-permute-done.3
  64.4 0.0 collective-permute-done.2
  64.4 1.5 %shard_map.87 = f32[21,64,128]{2,1,0:T(8,128)} custom-call(f32[64,128]{1,0:T(8,128)S(1)} %collective-permute-done.1.lines_right_ref, f32[21,64,128]{2,1,0:T(8,128)S(1)} %bitcast.16, f32[21,64,128]{2,1,0:T(8,128)S(1)} %get-tuple-element.34.base_ref, f32[21,64,128]{2,1,0:T(8,128)S(1)} %get-tuple-element.35.rest_ref, f32[21,64,128]{2,1,0:T(8,128)S(1)} %bitcast.20, ...), custom_call_target="tpu_custom_call" | custom-call | bytes 4440064 | tf_op jit(solution)/shard_map/pallas_call | solution.py:22
Async XLA Ops:
  1.9 9.8 %copy-start = (f32[32,2,128]{2,1,0:T(2,128)S(1)}, f32[32,2,128]{2,1,0:T(2,128)}, u32[]{:S(2)}) copy-start(f32[32,2,128]{2,1,0:T(2,128)} %param.13) | copy-start | bytes 98308
  1.9 9.8 %copy-start.1 = (f32[32,2,128]{2,1,0:T(2,128)S(1)}, f32[32,2,128]{2,1,0:T(2,128)}, u32[]{:S(2)}) copy-start(f32[32,2,128]{2,1,0:T(2,128)} %param.14) | copy-start | bytes 98308
  1.9 9.8 %copy-start.2 = (f32[21,21]{1,0:T(8,128)S(1)}, f32[21,21]{1,0:T(8,128)}, u32[]{:S(2)}) copy-start(f32[21,21]{1,0:T(8,128)} %mixing_ref.1) | copy-start | bytes 5296
  1.9 18.7 %all-to-all-start = ((f32[32,9,1,128]{3,2,1,0:T(1,128)}), f32[32,9,1,128]{3,2,1,0:T(1,128)S(1)}, u32[]{:S(2)}, u32[]{:S(2)}) async-start(f32[32,9,1,128]{3,2,1,0:T(1,128)} %bitcast.25), calls=%async_computation | async-start | bytes 294912 | tf_op jit(solution)/shard_map/all_to_all | solution.py:413
  12.1 9.8 %collective-permute-start = (f32[64,128]{1,0:T(8,128)S(1)}, f32[64,128]{1,0:T(8,128)S(1)}, u32[]{:S(2)}, u32[]{:S(2)}) collective-permute-start(f32[64,128]{1,0:T(8,128)S(1)} %get-tuple-element.22), channel_id=1, source_target_pairs={{0,1},{1,2},{2,3},{3,4},{4,5},{5,6},{6,7},{7,8},{8,9},{9,10},{10,1... | collective-permute-start | bytes 98312 | tf_op jit(solution)/shard_map/ppermute | solution.py:449
  50.2 14.2 %collective-permute-start.3 = (f32[1344,128]{1,0:T(8,128)S(1)}, f32[1344,128]{1,0:T(8,128)S(1)}, u32[]{:S(2)}, u32[]{:S(2)}) collective-permute-start(f32[1344,128]{1,0:T(8,128)S(1)} %shard_map.85), channel_id=1, source_target_pairs={{0,1},{1,2},{2,3},{3,4},{4,5},{5,6},{6,7},{7,8},{8,9},{9,10},{10,1... | collective-permute-start | bytes 2064392 | tf_op jit(solution)/shard_map/ppermute | solution.py:419
  52.5 11.9 %collective-permute-start.2 = (f32[1344,128]{1,0:T(8,128)S(1)}, f32[1344,128]{1,0:T(8,128)S(1)}, u32[]{:S(2)}, u32[]{:S(2)}) collective-permute-start(f32[1344,128]{1,0:T(8,128)S(1)} %shard_map.85), channel_id=1, source_target_pairs={{1,0},{2,1},{3,2},{4,3},{5,4},{6,5},{7,6},{8,7},{9,8},{10,9},{11,1... | collective-permute-start | bytes 2064392 | tf_op jit(solution)/shard_map/ppermute | solution.py:419
  52.5 11.9 %collective-permute-start.1 = (f32[64,128]{1,0:T(8,128)S(1)}, f32[64,128]{1,0:T(8,128)S(1)}, u32[]{:S(2)}, u32[]{:S(2)}) collective-permute-start(f32[64,128]{1,0:T(8,128)S(1)} %get-tuple-element.30), channel_id=1, source_target_pairs={{1,0},{2,1},{3,2},{4,3},{5,4},{6,5},{7,6},{8,7},{9,8},{10,9},{11,1... | collective-permute-start | bytes 98312 | tf_op jit(solution)/shard_map/ppermute | solution.py:474
